TPU v7x, 32 devices: a whole 2x2x4 slice. The times are simulated.
32 devices in a mesh: branch: 4 (over z), mp: 2 (over x), dp: 4 (over y, core).
Axes of the slice: x: 2, y: 2, z: 4, core: 2. Of those that a mesh axis runs over, the one named last changes fastest.
Arguments:
- context: bfloat16 [2048, 4096], P(('branch', 'dp'), 'mp'), may hold values from -6 to 6
- residual: bfloat16 [2048, 4096], P(('branch', 'dp')), may hold values from -12 to 12
- attn_weight: bfloat16 [4, 4096, 4096], P('branch', 'mp', 'dp'), may hold values from -0.1875 to 0.1875
- norm_gain: bfloat16 [4096], replicated, may hold values from 0.099609375 to 1.8984375
- gate_weight: bfloat16 [4, 4096, 5504], P('branch', None, ('mp', 'dp')), may hold values from -0.09375 to 0.09375
- up_weight: bfloat16 [4, 4096, 5504], P('branch', None, ('mp', 'dp')), may hold values from -0.09375 to 0.09375
- down_weight: bfloat16 [4, 5504, 4096], P('branch', ('mp', 'dp')), may hold values from -0.078125 to 0.078125
- cotangent: bfloat16 [2048, 4096], P(('branch', 'dp')), may hold values from -0.796875 to 0.796875
- expert_ids: int32 [2048, 2], P(('branch', 'dp')), may hold values from 0 to 3, as said below
- gate_fixed: int32 [2048, 2], P(('branch', 'dp')), may hold values from 1 to 32767, as said below
Outputs:
- grad_gate: bfloat16 [4, 4096, 5504], P('branch', None, ('mp', 'dp'))
- grad_up: bfloat16 [4, 4096, 5504], P('branch', None, ('mp', 'dp'))
- grad_down: bfloat16 [4, 5504, 4096], P('branch', ('mp', 'dp'))
Inputs may be any that keep to these rules, and one draw needn't show every extreme that they name: `expert_ids`: the two entries of a row differ; in every aligned block of 128 rows some expert is named by more than 80 choices. `gate_fixed`: the two entries of a row sum to 32768.
All inputs are finite; a program needn't handle non-finite values.
Results may differ from a plain program's by a relative error of at most 0.025.
Values may be sent and summed in bfloat16 or wider, within the bound.
No kernel may reach another device: no remote copies, remote signals or barrier semaphores. Data moves between devices by JAX's collectives and lax.ppermute only.
A program may use at most 128 MiB of HBM per device.

v0:
```python
import functools

import jax
import jax.numpy as jnp
from jax import lax
from jax.sharding import PartitionSpec as P


def slot_positions(id_block, capacity, experts):
    rows = id_block.shape[0]
    picks = jnp.concatenate([id_block[:, 0], id_block[:, 1]], axis=0)
    onehot = (picks[:, None] == jnp.arange(experts, dtype=jnp.int32)[None, :]).astype(jnp.int32)
    position = jnp.sum((jnp.cumsum(onehot, axis=0) - 1) * onehot, axis=1)
    position = jnp.where(position < capacity, position, -1)
    return jnp.stack([position[:rows], position[rows:]], axis=1)


def expert_pass(weight_set, totals, block_rows, first_row):
    w_gate, w_up, w_down = weight_set
    tokens_in, cotan_rows = block_rows
    pre_gate = jnp.dot(tokens_in, w_gate, preferred_element_type=jnp.float32)
    pre_up = jnp.dot(tokens_in, w_up, preferred_element_type=jnp.float32)
    sigmoid_gate = jax.nn.sigmoid(pre_gate)
    active = pre_gate * sigmoid_gate
    hidden = (active * pre_up).astype(jnp.bfloat16)
    back_grad = lax.dot_general(
        cotan_rows, w_down, (((1,), (1,)), ((), ())), preferred_element_type=jnp.float32
    )
    d_gate = (back_grad * pre_up * sigmoid_gate * (1.0 + pre_gate * (1.0 - sigmoid_gate))).astype(
        jnp.bfloat16
    )
    d_up = (back_grad * active).astype(jnp.bfloat16)
    contract = (((0,), (0,)), ((), ()))
    sum_gate = lax.dot_general(tokens_in, d_gate, contract, preferred_element_type=jnp.float32)
    sum_up = lax.dot_general(tokens_in, d_up, contract, preferred_element_type=jnp.float32)
    sum_down = lax.dot_general(hidden, cotan_rows, contract, preferred_element_type=jnp.float32)
    return (sum_gate, sum_up, sum_down)


def per_device(
    context,
    residual,
    attn_weight,
    norm_gain,
    gate_weight,
    up_weight,
    down_weight,
    cotangent,
    expert_ids,
    gate_fixed,
):
    branches = lax.axis_size("branch")
    summed = lax.psum(attn_weight[0].astype(jnp.float32).astype(jnp.bfloat16), "branch").astype(
        jnp.float32
    )
    merged = (summed / branches).astype(jnp.bfloat16)
    context_all = lax.all_gather(context, "dp", axis=0, tiled=True)
    local_part = jnp.dot(context_all, merged, preferred_element_type=jnp.float32).astype(
        jnp.bfloat16
    )
    partial_out = lax.all_to_all(local_part, "dp", split_axis=0, concat_axis=1, tiled=True)
    attention = lax.psum(partial_out.astype(jnp.float32).astype(jnp.bfloat16), "mp").astype(
        jnp.float32
    )
    mixed_in = residual.astype(jnp.float32) + attention
    inv_rms = lax.rsqrt(jnp.mean(mixed_in * mixed_in, axis=1, keepdims=True) + 1e-05)
    normed = (mixed_in * inv_rms * norm_gain.astype(jnp.float32)[None, :]).astype(jnp.bfloat16)
    model_width = residual.shape[1]
    group_tokens = residual.shape[0]
    experts = branches * gate_weight.shape[0]
    capacity = 5 * group_tokens // (2 * experts)
    slots = slot_positions(expert_ids, capacity, experts)
    slot_share = capacity // lax.axis_size("mp")
    offset = lax.axis_index("mp") * slot_share
    local_slot = slots - offset
    in_share = (slots >= 0) & (local_slot >= 0) & (local_slot < slot_share)
    slot_code = jnp.where(in_share, expert_ids * slot_share + local_slot, -1)
    target = jnp.arange(experts * slot_share, dtype=jnp.int32)
    matches = slot_code[None, :, :] == target[:, None, None]
    selector = jnp.any(matches, axis=2).astype(jnp.bfloat16)
    row_gate = jnp.sum(
        jnp.where(matches, gate_fixed[None, :, :].astype(jnp.float32) / 32768.0, 0.0), axis=(1, 2)
    )
    send_in = jnp.dot(selector, normed, preferred_element_type=jnp.float32).astype(jnp.bfloat16)
    send_in = send_in.reshape(experts, slot_share, model_width)
    cot_rows = jnp.dot(selector, cotangent, preferred_element_type=jnp.float32)
    send_cot = (
        (cot_rows * row_gate[:, None])
        .astype(jnp.bfloat16)
        .reshape(experts, slot_share, model_width)
    )
    hidden_width = gate_weight.shape[2]
    start_totals = (
        jnp.zeros((model_width, hidden_width), jnp.float32),
        jnp.zeros((model_width, hidden_width), jnp.float32),
        jnp.zeros((hidden_width, model_width), jnp.float32),
    )
    accumulate = functools.partial(expert_pass, (gate_weight[0], up_weight[0], down_weight[0]))
    routed_in, routed_cot = (
        lax.all_to_all(send_in, "branch", split_axis=0, concat_axis=1, tiled=True),
        lax.all_to_all(send_cot, "branch", split_axis=0, concat_axis=1, tiled=True),
    )
    totals = accumulate(
        start_totals,
        (
            lax.all_gather(routed_in[0], ("mp", "dp"), axis=0, tiled=True),
            lax.all_gather(routed_cot[0], ("mp", "dp"), axis=0, tiled=True),
        ),
        jnp.int32(0),
    )
    grad_gate = totals[0].astype(jnp.bfloat16)[None]
    grad_up = totals[1].astype(jnp.bfloat16)[None]
    grad_down = totals[2].astype(jnp.bfloat16)[None]
    return (grad_gate, grad_up, grad_down)


def solution(mesh):
    return jax.shard_map(
        per_device,
        mesh=mesh,
        in_specs=(
            P(("branch", "dp"), "mp"),
            P(("branch", "dp"), None),
            P("branch", "mp", "dp"),
            P(),
            P("branch", None, ("mp", "dp")),
            P("branch", None, ("mp", "dp")),
            P("branch", ("mp", "dp"), None),
            P(("branch", "dp"), None),
            P(("branch", "dp"), None),
            P(("branch", "dp"), None),
        ),
        out_specs=(
            P("branch", None, ("mp", "dp")),
            P("branch", None, ("mp", "dp")),
            P("branch", ("mp", "dp"), None),
        ),
        check_vma=False,
    )
```

profile of v0, /device:TPU:0, one launch (start us, length us, event | category | flops | bytes accessed | tf_op | source)
XLA Modules:
  0.0 444.8 jit_solution(6179528329244827212)
XLA Ops:
  8.1 0.7 all-gather.4.cloned.1.call-update
  8.8 0.0 all-reduce.3.cloned.1.call-start
  8.8 0.5 all-reduce.3.cloned.1.call-update
  9.4 1.2 reduce-window.6
  10.6 0.1 slice.24
  10.7 0.1 copy.18
  10.8 0.1 copy.19
  10.9 0.1 add_bitcast_fusion
  11.1 24.7 %all-gather.4.cloned.1.call-done = bf16[512,2048]{1,0:T(8,128)(2,1)} async-done(((bf16[128,2048]{1,0:T(8,128)(2,1)}), bf16[512,2048]{1,0:T(8,128)(2,1)}) %all-gather.4.cloned.1.call-update) | async-done | bytes 2097168 | tf_op jit(solution)/shard_map/all_gather | solution.py:57
  35.8 133.3 %all-reduce.3.cloned.1.call-done = bf16[2048,1024]{1,0:T(8,128)(2,1)} async-done(((bf16[2048,1024]{1,0:T(8,128)(2,1)}), bf16[2048,1024]{1,0:T(8,128)(2,1)}) %all-reduce.3.cloned.1.call-update) | async-done | bytes 4194320 | tf_op jit(solution)/shard_map/psum | solution.py:53
  169.1 6.1 %fusion.14 = bf16[1024,512]{0,1:T(8,128)(2,1)} fusion(bf16[512,2048]{1,0:T(8,128)(2,1)} %all-gather.4.cloned.1.call-done, bf16[2048,1024]{1,0:T(8,128)(2,1)} %all-reduce.3.cloned.1.call-done), kind=kOutput, calls=%fused_computation.27 | convolution fusion | flops 2154299392 | bytes 7340032 | tf_op jit(solution)/shard_map/dot_general | solution.py:58
  175.2 3.5 all-to-all-start
  178.8 0.1 select_reduce_fusion
  178.9 1.6 fusion.9
  180.5 12.7 %all-to-all-done = bf16[4,128,1024]{2,1,0:T(8,128)(2,1)S(1)} async-done(((bf16[4,128,1024]{2,1,0:T(8,128)(2,1)}), bf16[4,128,1024]{2,1,0:T(8,128)(2,1)S(1)}, u32[]{:S(2)}, u32[]{:S(2)}) %all-to-all-start) | async-done | bytes 1048608 | tf_op jit(solution)/shard_map/all_to_all | solution.py:61
  193.2 3.7 all-to-all-start.2
  196.9 0.0 all-reduce.5.cloned.1.call-start
  196.9 1.1 copy.21
  198.1 30.2 %all-to-all-done.2 = bf16[4,40,4096]{2,1,0:T(8,128)(2,1)S(1)} async-done(((bf16[4,40,4096]{2,1,0:T(8,128)(2,1)}), bf16[4,40,4096]{2,1,0:T(8,128)(2,1)S(1)}, u32[]{:S(2)}, u32[]{:S(2)}) %all-to-all-start.2) | async-done | bytes 1310752 | tf_op jit(solution)/shard_map/all_to_all | solution.py:101
  228.3 1.1 copy-done.2
  229.4 11.8 %all-reduce.5.cloned.1.call-done = bf16[128,4096]{1,0:T(8,128)(2,1)} async-done(((bf16[128,4096]{1,0:T(8,128)(2,1)}), bf16[128,4096]{1,0:T(8,128)(2,1)}) %all-reduce.5.cloned.1.call-update) | async-done | bytes 1048592 | tf_op jit(solution)/shard_map/psum | solution.py:62
  241.2 1.6 multiply_reduce_fusion
  242.9 1.8 convolution_convert_fusion.3
  244.7 35.9 %all_to_all.37 = bf16[4,40,4096]{2,1,0:T(8,128)(2,1)} all-to-all(bf16[4,40,4096]{2,1,0:T(8,128)(2,1)S(1)} %bitcast.63), channel_id=1, replica_groups=mesh['branch'=4,'mp'=2,'dp'=4] {'branch'}, dimensions={0} | all-to-all | bytes 2621440 | tf_op jit(solution)/shard_map/all_to_all | solution.py:100
  280.6 26.4 %all-gather.8.cloned.1.call-done = bf16[1280,4096]{1,0:T(8,128)(2,1)} async-done(((bf16[160,4096]{1,0:T(8,128)(2,1)}), bf16[1280,4096]{1,0:T(8,128)(2,1)}) %all-gather.8.cloned.1.call-update) | async-done | bytes 10485776 | tf_op jit(solution)/shard_map/all_gather | solution.py:107
  307.0 13.8 %fusion.7 = f32[1280,688]{0,1:T(8,128)} fusion(bf16[1280,4096]{1,0:T(8,128)(2,1)} %all-gather.8.cloned.1.call-done, bf16[1,688,4096]{2,1,0:T(8,128)(2,1)} %param.16), kind=kOutput, calls=%fused_computation.11 | convolution fusion | flops 7214202880 | bytes 19644416 | tf_op jit(solution)/shard_map/dot_general | solution.py:26
  320.8 51.3 %all-gather.6.cloned.1.call-done = bf16[1280,4096]{1,0:T(8,128)(2,1)} async-done(((bf16[160,4096]{1,0:T(8,128)(2,1)}), bf16[1280,4096]{1,0:T(8,128)(2,1)}) %all-gather.6.cloned.1.call-update) | async-done | bytes 10485776 | tf_op jit(solution)/shard_map/all_gather | solution.py:106
  372.0 13.9 %fusion.3 = f32[1280,688]{0,1:T(8,128)} fusion(bf16[1280,4096]{1,0:T(8,128)(2,1)} %all-gather.6.cloned.1.call-done, bf16[1,4096,688]{1,2,0:T(8,128)(2,1)} %param.14), kind=kOutput, calls=%fused_computation.7 | convolution fusion | flops 7214202880 | bytes 19644416 | tf_op jit(solution)/shard_map/dot_general | solution.py:21
  386.0 11.3 %fusion.5 = f32[1280,688]{0,1:T(8,128)} fusion(bf16[1280,4096]{1,0:T(8,128)(2,1)S(1)} %copy-done.7, bf16[1,4096,688]{1,2,0:T(8,128)(2,1)} %param.15), kind=kOutput, calls=%fused_computation.9 | convolution fusion | flops 7214202880 | bytes 19644416 | tf_op jit(solution)/shard_map/dot_general | solution.py:22
  397.3 12.6 %fusion = bf16[1,688,4096]{2,1,0:T(8,128)(2,1)} fusion(bf16[1280,4096]{1,0:T(8,128)(2,1)S(1)} %bitcast.69, f32[1280,688]{0,1:T(8,128)} %fusion.5, f32[1280,688]{0,1:T(8,128)} %fusion.3), kind=kOutput, calls=%fused_computation.4 | convolution fusion | flops 7222304768 | bytes 23166976 | tf_op jit(solution)/shard_map/dot_general | solution.py:36
  409.9 17.9 %fusion.1 = bf16[1,4096,688]{1,2,0:T(8,128)(2,1)} fusion(bf16[1280,4096]{1,0:T(8,128)(2,1)S(1)} %copy-done.7, f32[1280,688]{0,1:T(8,128)} %fusion.3, f32[1280,688]{0,1:T(8,128)} %fusion.7, f32[1280,688]{0,1:T(8,128)} %fusion.5), kind=kOutput, calls=%fused_computation.5 | convolution fusion | flops 7225827328 | bytes 26689536 | tf_op jit(solution)/shard_map/dot_general | solution.py:34
  427.8 9.9 %fusion.2 = bf16[1,4096,688]{1,2,0:T(8,128)(2,1)} fusion(bf16[1280,4096]{1,0:T(8,128)(2,1)S(1)} %copy-done.7, f32[1280,688]{0,1:T(8,128)S(1)} %copy-done.8, f32[1280,688]{0,1:T(8,128)S(1)} %copy-done.9), kind=kOutput, calls=%fused_computation.6 | convolution fusion | flops 7222304768 | bytes 23166976 | tf_op jit(solution)/shard_map/dot_general | solution.py:35
  (45 shorter events, 0.4 us)
Async XLA Ops:
  8.0 170.9 %copy-start = (bf16[128,4096]{1,0:T(8,128)(2,1)S(1)}, bf16[128,4096]{1,0:T(8,128)(2,1)}, u32[]{:S(2)}) copy-start(bf16[128,4096]{1,0:T(8,128)(2,1)} %param.17) | copy-start | bytes 3145732
  8.0 1.3 copy-start.5
  8.0 27.8 %all-gather.4.cloned.1.call-start = ((), (), s32[]{:S(2)}) async-start(), calls=%async_computation.4 | async-start | bytes 2621440 | tf_op jit(solution)/shard_map/all_gather | solution.py:57
  8.8 160.3 %all-reduce.3.cloned.1.call-start = ((), (), s32[]{:S(2)}) async-start(), calls=%async_computation.3 | async-start | bytes 8388608 | tf_op jit(solution)/shard_map/psum | solution.py:53
  11.1 167.7 %copy-start.6 = (s32[128,2]{0,1:T(2,128)S(1)}, s32[128,2]{0,1:T(2,128)}, u32[]{:S(2)}) copy-start(s32[128,2]{0,1:T(2,128)} %param.19) | copy-start | bytes 3076
  175.2 18.0 %all-to-all-start = ((bf16[4,128,1024]{2,1,0:T(8,128)(2,1)}), bf16[4,128,1024]{2,1,0:T(8,128)(2,1)S(1)}, u32[]{:S(2)}, u32[]{:S(2)}) async-start(bf16[4,128,1024]{2,1,0:T(8,128)(2,1)} %bitcast.9), calls=%async_computation | async-start | bytes 2097152 | tf_op jit(solution)/shard_map/all_to_all | solution.py:61
  193.2 36.2 %copy-start.4 = (bf16[4096]{0:T(1024)(128)(2,1)S(1)}, bf16[4096]{0:T(1024)(128)(2,1)}, u32[]{:S(2)}) copy-start(bf16[4096]{0:T(1024)(128)(2,1)} %param.13) | copy-start | bytes 24580
  193.2 48.1 %copy-start.3 = (bf16[128,4096]{1,0:T(8,128)(2,1)S(1)}, bf16[128,4096]{1,0:T(8,128)(2,1)}, u32[]{:S(2)}) copy-start(bf16[128,4096]{1,0:T(8,128)(2,1)} %param.11) | copy-start | bytes 3145732
  193.2 35.1 %all-to-all-start.2 = ((bf16[4,40,4096]{2,1,0:T(8,128)(2,1)}), bf16[4,40,4096]{2,1,0:T(8,128)(2,1)S(1)}, u32[]{:S(2)}, u32[]{:S(2)}) async-start(bf16[4,40,4096]{2,1,0:T(8,128)(2,1)} %bitcast.13), calls=%async_computation.2 | async-start | bytes 2621440 | tf_op jit(solution)/shard_map/all_to_all | solution.py:101
  196.9 44.4 %all-reduce.5.cloned.1.call-start = ((), (), s32[]{:S(2)}) async-start(), calls=%async_computation.5 | async-start | bytes 2097152 | tf_op jit(solution)/shard_map/psum | solution.py:62
  198.0 109.0 %all-gather.8.cloned.1.call-start = ((), (), s32[]{:S(2)}) async-start(), calls=%async_computation.7 | async-start | bytes 11796480 | tf_op jit(solution)/shard_map/all_gather | solution.py:107
  228.3 1.1 copy-start.2
  229.3 142.7 %all-gather.6.cloned.1.call-start = ((), (), s32[]{:S(2)}) async-start(), calls=%async_computation.6 | async-start | bytes 11796480 | tf_op jit(solution)/shard_map/all_gather | solution.py:106
  372.0 13.9 %copy-start.7 = (bf16[1280,4096]{1,0:T(8,128)(2,1)S(1)}, bf16[1280,4096]{1,0:T(8,128)(2,1)}, u32[]{:S(2)}) copy-start(bf16[1280,4096]{1,0:T(8,128)(2,1)} %all-gather.6.cloned.1.call-done) | copy-start | bytes 31457284
  372.0 25.3 %slice-start = ((s8[10485760]{0:T(1024)(128)(4,1)}), s8[4194304]{0:T(1024)(128)(4,1)S(1)}, s32[]{:S(2)}) async-start(s8[10485760]{0:T(1024)(128)(4,1)} %bitcast.68), calls=%async_computation.8 | async-start | bytes 8388608
  372.0 25.3 %slice-start.1 = ((s8[10485760]{0:T(1024)(128)(4,1)}), s8[4194304]{0:T(1024)(128)(4,1)S(1)}, s32[]{:S(2)}) async-start(s8[10485760]{0:T(1024)(128)(4,1)} %bitcast.68), calls=%async_computation.9 | async-start | bytes 8388608
  386.0 11.3 %slice-start.2 = ((s8[10485760]{0:T(1024)(128)(4,1)}), s8[2097152]{0:T(1024)(128)(4,1)S(1)}, s32[]{:S(2)}) async-start(s8[10485760]{0:T(1024)(128)(4,1)} %bitcast.68), calls=%async_computation.10 | async-start | bytes 4194304
  409.9 17.9 %copy-start.8 = (f32[1280,688]{0,1:T(8,128)S(1)}, f32[1280,688]{0,1:T(8,128)}, u32[]{:S(2)}) copy-start(f32[1280,688]{0,1:T(8,128)} %fusion.7) | copy-start | bytes 10567684
  409.9 17.9 %copy-start.9 = (f32[1280,688]{0,1:T(8,128)S(1)}, f32[1280,688]{0,1:T(8,128)}, u32[]{:S(2)}) copy-start(f32[1280,688]{0,1:T(8,128)} %fusion.3) | copy-start | bytes 10567684
  427.8 9.9 %copy-start.1 = (bf16[128,4096]{1,0:T(8,128)(2,1)S(1)}, bf16[128,4096]{1,0:T(8,128)(2,1)}, u32[]{:S(2)}) copy-start(bf16[128,4096]{1,0:T(8,128)(2,1)} %param.17) | copy-start | bytes 3145732
Sparse Core Ops, SparseCore 0:
  10.4 25.3 all-gather.3
  200.7 40.5 all-reduce.4
  243.7 63.2 all-gather.7
  308.7 63.2 all-gather.5
Sparse Core Ops, SparseCore 1:
  11.6 157.4 all-reduce.2
where the time goes:
time: 445 us
  waiting for transfers between devices  292 us (66%)
  matrix products  88.9 us (20%)
  blocking collectives  35.9 us (8%)
  between operations  15.4 us (3%)
  starting transfers between devices  7.39 us (2%)
    psum x1, waiting for transfers between devices, per_device(): lax.psum(attn_weight[0].astype(jnp.float32).astype(jnp.bfloat16), 'branch')  133 us
    all_gather x1, waiting for transfers between devices, per_device(): lax.all_gather(routed_in[0], ('mp', 'dp'), axis=0, tiled=True)  51.3 us
    all_to_all x1, blocking collectives, per_device(): lax.all_to_all(send_in, 'branch', split_axis=0, concat_axis=1, tiled=True)  35.9 us
    all_to_all x1, waiting for transfers between devices, per_device(): lax.all_to_all(send_cot, 'branch', split_axis=0, concat_axis=1, tiled=True)  30.2 us
    all_gather x1, waiting for transfers between devices, per_device(): lax.all_gather(routed_cot[0], ('mp', 'dp'), axis=0, tiled=True)  26.4 us
    all_gather x1, waiting for transfers between devices, per_device(): context_all = lax.all_gather(context, 'dp', axis=0, tiled=True)  24.7 us
    dot_general x1, matrix products, expert_pass(): lax.dot_general(tokens_in, d_gate, contract, preferred_element_type=jnp.f...  17.9 us
    dot_general x1, matrix products, expert_pass(): pre_gate = jnp.dot(tokens_in, w_gate, preferred_element_type=jnp.float32)  13.9 us
  transfers between devices with their start and end apart: 7, of which 7 were waited for; matrix products, arithmetic and copies ran while one was open for 5% of the time, Pallas kernels for 0%

commit v1 on v0

v1 whole, which is shorter than its diff:
```python
import functools

import jax
import jax.numpy as jnp
from jax import lax
from jax.sharding import PartitionSpec as P


def slot_positions(id_block, capacity, experts):
    rows = id_block.shape[0]
    picks = jnp.concatenate([id_block[:, 0], id_block[:, 1]], axis=0)
    onehot = (picks[:, None] == jnp.arange(experts, dtype=jnp.int32)[None, :]).astype(jnp.int32)
    position = jnp.sum((jnp.cumsum(onehot, axis=0) - 1) * onehot, axis=1)
    position = jnp.where(position < capacity, position, -1)
    return jnp.stack([position[:rows], position[rows:]], axis=1)


def shift(value, axis, step):
    size = lax.axis_size(axis)
    return lax.ppermute(value, axis, [(i, (i + step) % size) for i in range(size)])


def flip(value, axis, mask):
    size = lax.axis_size(axis)
    return lax.ppermute(value, axis, [(i, i ^ mask) for i in range(size)])


def after(value, *others):
    return lax.optimization_barrier((value, *others))[0]


def masks(size):
    out, mask = [], size // 2
    while mask >= 1:
        out.append(mask)
        mask //= 2
    return out


def relative_order(size):
    order = [0]
    for mask in masks(size):
        order = order + [o ^ mask for o in order]
    return order


def gather_flips(block, axis, todo):
    for mask in todo:
        block = jnp.concatenate([block, flip(block, axis, mask)], axis=0)
    return block


def line_steps(block, axis):
    size = lax.axis_size(axis)
    up, down, got = block, block, {}
    for k in range(1, size):
        up = got[k] = lax.ppermute(up, axis, [(i, i + 1) for i in range(k - 1, size - 1)])
        down = got[-k] = lax.ppermute(down, axis, [(i + 1, i) for i in range(size - k)])
    return got


def pick_flip(got, axis, mask):
    size, me = lax.axis_size(axis), lax.axis_index(axis)
    value = None
    for k in sorted({i - (i ^ mask) for i in range(size)}, key=abs):
        where = functools.reduce(jnp.logical_or, [me == i for i in range(size) if i - (i ^ mask) == k])
        value = got[k] if value is None else jnp.where(where, got[k], value)
    return value


def plane_gather(block):
    n_mp, n_dp = lax.axis_size("mp"), lax.axis_size("dp")
    half = block.shape[0] // 2
    todo = masks(n_dp)
    across = [block] + [shift(block, "mp", s) for s in range(1, n_mp)]
    if not todo:
        return across
    far = flip(block, "dp", todo[0])
    far_across = [far]
    for s in range(1, n_mp):
        top = shift(far[:half], "mp", s)
        bottom = flip(across[s][half:], "dp", todo[0])
        far_across.append(jnp.concatenate([top, bottom], axis=0))
    across = [jnp.concatenate([a, b], axis=0) for a, b in zip(across, far_across)]
    return [gather_flips(a, "dp", todo[1:]) for a in across]


def whole_columns(across, piece):
    n_mp, n_dp, x = lax.axis_size("mp"), lax.axis_size("dp"), lax.axis_index("mp")
    parts = []
    for p in range(n_mp):
        value = across[0]
        for s in range(1, n_mp):
            value = jnp.where((x - s) % n_mp == p, across[s], value)
        parts.append(value)
    return jnp.concatenate(
        [part[:, k * piece : (k + 1) * piece] for k in range(n_dp) for part in parts], axis=1
    )


def per_device(
    context,
    residual,
    attn_weight,
    norm_gain,
    gate_weight,
    up_weight,
    down_weight,
    cotangent,
    expert_ids,
    gate_fixed,
):
    n_br, n_mp, n_dp = lax.axis_size("branch"), lax.axis_size("mp"), lax.axis_size("dp")
    z, x, d = lax.axis_index("branch"), lax.axis_index("mp"), lax.axis_index("dp")
    tokens, width = residual.shape
    experts = n_br * gate_weight.shape[0]
    capacity = 5 * tokens // (2 * experts)
    piece = width // (n_dp * n_mp)

    def choose(options, index):
        value = options[0]
        for i in range(1, len(options)):
            value = jnp.where(index == i, options[i], value)
        return value

    def cut(value, i):
        return value[:, i * piece : (i + 1) * piece]

    def my_columns(value):
        return jnp.concatenate(
            [choose([cut(value, k * n_mp + p) for p in range(n_mp)], x) for k in range(n_dp)], axis=1
        )

    slots = slot_positions(expert_ids, capacity, experts)
    slot_code = jnp.where(slots >= 0, (expert_ids ^ z) * capacity + slots, -1)
    target = jnp.arange(experts * capacity, dtype=jnp.int32)[:, None]
    matches = [slot_code[:, k][None, :] == target for k in range(2)]
    selector = (matches[0] | matches[1]).astype(jnp.bfloat16)
    gate = gate_fixed.astype(jnp.float32) / 32768.0
    row_gate = sum(jnp.where(matches[k], gate[:, k][None, :], 0.0) for k in range(2))
    row_gate = jnp.sum(row_gate, axis=1, keepdims=True)

    weight = attn_weight[0]
    weight_for = [choose([cut(weight, (p + s) % n_mp) for p in range(n_mp)], x) for s in range(n_mp)]
    steps = line_steps(context, "branch")
    last_steps = (steps[n_br - 1], steps[1 - n_br]) if n_br > 1 else (context,)

    def project(m):
        ctx = context if m == 0 else pick_flip(steps, "branch", m)
        ctx = gather_flips(ctx, "dp", masks(n_dp))
        value = jnp.dot(ctx, weight_for[0], preferred_element_type=jnp.float32)
        for t in range(1, n_mp):
            away = jnp.dot(ctx, weight_for[t], preferred_element_type=jnp.float32).astype(jnp.bfloat16)
            value = value + shift(away, "mp", t).astype(jnp.float32)
        return value

    shares = [project(0)] + [project(m).astype(jnp.bfloat16) for m in range(1, n_br)]

    cot_rows = jnp.dot(selector, my_columns(cotangent), preferred_element_type=jnp.float32)
    send_cot = (cot_rows * row_gate).astype(jnp.bfloat16)
    send_cot = [send_cot[m * capacity : (m + 1) * capacity] for m in range(n_br)]
    send_cot = lax.optimization_barrier((*send_cot, *last_steps))[:n_br]
    cot_slots = [flip(send_cot[m], "branch", m) if m else send_cot[m] for m in range(n_br)]

    back = [flip(shares[m], "branch", m) for m in range(1, n_br)]
    total = shares[0]
    for value in back:
        total = total + value.astype(jnp.float32)
    total = (total / n_br).astype(jnp.bfloat16)

    order = relative_order(n_dp)
    got = [None] * n_dp
    for i, o in enumerate(order):
        block = total[i * tokens : (i + 1) * tokens]
        got[o] = flip(block, "dp", o) if o else block
    attention = jnp.concatenate([choose(got, d ^ k) for k in range(n_dp)], axis=1)
    mixed = my_columns(residual).astype(jnp.float32) + attention.astype(jnp.float32)
    squares = jnp.sum(mixed * mixed, axis=1, keepdims=True)
    all_squares = squares
    for s in range(1, n_mp):
        all_squares = all_squares + shift(squares.reshape(1, tokens), "mp", s).reshape(tokens, 1)
    inv_rms = lax.rsqrt(all_squares / width + 1e-05)
    gain = my_columns(norm_gain[None, :]).astype(jnp.float32)
    normed = (mixed * inv_rms * gain).astype(jnp.bfloat16)
    send_in = jnp.dot(selector, normed, preferred_element_type=jnp.float32).astype(jnp.bfloat16)
    send_in = [send_in[m * capacity : (m + 1) * capacity] for m in range(n_br)]

    near = max(1, n_br // 2)
    bounds = [(lo, hi) for lo, hi in ((0, near), (near, n_br)) if hi > lo]

    def gathered(slots_in):
        return whole_columns(plane_gather(jnp.concatenate(slots_in, axis=0)), piece)

    cot_slots = lax.optimization_barrier((*cot_slots, *shares))[:n_br]
    cotan_rows = jnp.concatenate([gathered(cot_slots[lo:hi]) for lo, hi in bounds], axis=0)
    in_slots = [flip(send_in[m], "branch", m) if m else send_in[m] for m in range(n_br)]
    tokens_in = jnp.concatenate([gathered(in_slots[lo:hi]) for lo, hi in bounds], axis=0)

    w_gate, w_up, w_down = gate_weight[0], up_weight[0], down_weight[0]
    back_grad = lax.dot_general(
        cotan_rows, w_down, (((1,), (1,)), ((), ())), preferred_element_type=jnp.float32
    )
    pre_gate = jnp.dot(tokens_in, w_gate, preferred_element_type=jnp.float32)
    pre_up = jnp.dot(tokens_in, w_up, preferred_element_type=jnp.float32)
    sigmoid_gate = jax.nn.sigmoid(pre_gate)
    active = pre_gate * sigmoid_gate
    hidden = (active * pre_up).astype(jnp.bfloat16)
    d_gate = (back_grad * pre_up * sigmoid_gate * (1.0 + pre_gate * (1.0 - sigmoid_gate))).astype(
        jnp.bfloat16
    )
    d_up = (back_grad * active).astype(jnp.bfloat16)
    contract = (((0,), (0,)), ((), ()))
    grad_gate = lax.dot_general(tokens_in, d_gate, contract, preferred_element_type=jnp.float32)
    grad_up = lax.dot_general(tokens_in, d_up, contract, preferred_element_type=jnp.float32)
    grad_down = lax.dot_general(hidden, cotan_rows, contract, preferred_element_type=jnp.float32)
    return (
        grad_gate.astype(jnp.bfloat16)[None],
        grad_up.astype(jnp.bfloat16)[None],
        grad_down.astype(jnp.bfloat16)[None],
    )


def solution(mesh):
    return jax.shard_map(
        per_device,
        mesh=mesh,
        in_specs=(
            P(("branch", "dp"), "mp"),
            P(("branch", "dp"), None),
            P("branch", "mp", "dp"),
            P(),
            P("branch", None, ("mp", "dp")),
            P("branch", None, ("mp", "dp")),
            P("branch", ("mp", "dp"), None),
            P(("branch", "dp"), None),
            P(("branch", "dp"), None),
            P(("branch", "dp"), None),
        ),
        out_specs=(
            P("branch", None, ("mp", "dp")),
            P("branch", None, ("mp", "dp")),
            P("branch", ("mp", "dp"), None),
        ),
        check_vma=False,
    )
```

time: 445 us -> 378 us (0.85)
  waiting for transfers between devices: 292 us -> 154 us
  starting transfers between devices: 7.39 us -> 50.7 us
  local copies, waits for them, and re-layouts: 2.46 us -> 42.3 us
  blocking collectives: 35.9 us -> 0 us
  other arithmetic: 3.19 us -> 23.3 us
  between operations: 15.4 us -> 2 us
  matrix products: 88.9 us -> 102 us
    ppermute x0 -> x55, waiting for transfers between devices: none -> 154 us  [the longest x36 90.1 us: flip(): return lax.ppermute(value, axis, [(i, i ^ mask) for i in range(size)])]
    psum x2 -> x0, waiting for transfers between devices: 145 us -> none  [the longest x1 133 us: per_device(): lax.psum(attn_weight[0].astype(jnp.float32).astype(jnp.bfloat16), 'branch')]
    all_gather x3 -> x0, waiting for transfers between devices: 102 us -> none  [the longest x1 51.3 us: per_device(): lax.all_gather(routed_in[0], ('mp', 'dp'), axis=0, tiled=True)]
    ppermute x0 -> x55, starting transfers between devices: none -> 50.7 us  [the longest x36 22.6 us: flip(): return lax.ppermute(value, axis, [(i, i ^ mask) for i in range(size)])]
    all_to_all x2 -> x0, waiting for transfers between devices: 42.9 us -> none  [the longest x1 30.2 us: per_device(): lax.all_to_all(send_cot, 'branch', split_axis=0, concat_axis=1, tiled=True)]
    all_to_all x1 -> x0, blocking collectives: 35.9 us -> none  [per_device(): lax.all_to_all(send_in, 'branch', split_axis=0, concat_axis=1, tiled=True)]
    unnamed x26 -> x117, local copies, waits for them, and re-layouts: 1.11 us -> 29.5 us
    dot_general x8 -> x15, matrix products: 87.1 us -> 101 us  [the longest x1 16.1 us: per_device(): lax.dot_general(tokens_in, d_gate, contract, preferred_element_type=jnp.f...]
  transfers between devices with their start and end apart: 7 -> 55, of which waited for: 7 -> 24; matrix products, arithmetic and copies ran while one was open for 5% -> 24% of each run, Pallas kernels for 0% -> 0%
where the time goes in v1:
time: 378 us; the launch traced here: 374 us
  waiting for transfers between devices  154 us (41%)
  matrix products  102 us (27%)
  starting transfers between devices  50.7 us (13%)
  local copies, waits for them, and re-layouts  42.3 us (11%)
  other arithmetic  23.3 us (6%)
    ppermute x36, waiting for transfers between devices, flip(): return lax.ppermute(value, axis, [(i, i ^ mask) for i in range(size)])  90.1 us
    ppermute x13, waiting for transfers between devices, shift(): lax.ppermute(value, axis, [(i, (i + step) % size) for i in range(size)])  46.3 us
    unnamed x117, local copies, waits for them, and re-layouts  29.5 us
    ppermute x36, starting transfers between devices, flip(): return lax.ppermute(value, axis, [(i, i ^ mask) for i in range(size)])  22.6 us
    ppermute x3, waiting for transfers between devices, line_steps(): lax.ppermute(down, axis, [(i + 1, i) for i in range(size - k)])  17.7 us
    ppermute x13, starting transfers between devices, shift(): lax.ppermute(value, axis, [(i, (i + step) % size) for i in range(size)])  17.7 us
    dot_general x1, matrix products, per_device(): lax.dot_general(tokens_in, d_gate, contract, preferred_element_type=jnp.f...  16.1 us
    dot_general x1, matrix products, per_device(): pre_gate = jnp.dot(tokens_in, w_gate, preferred_element_type=jnp.float32)  13.9 us
  transfers between devices with their start and end apart: 55, of which 24 were waited for; matrix products, arithmetic and copies ran while one was open for 24% of the time, Pallas kernels for 0%

profile of v1, /device:TPU:0, one launch (start us, length us, event | category | flops | bytes accessed | tf_op | source)
XLA Modules:
  0.0 374.1 jit_solution(12716530429058266393)
XLA Ops:
  0.6 3.0 collective-permute-start
  3.7 4.3 %collective-permute-start.4 = (bf16[128,2048]{1,0:T(8,128)(2,1)}, bf16[128,2048]{1,0:T(8,128)(2,1)}, u32[]{:S(2)}, u32[]{:S(2)}) collective-permute-start(bf16[128,2048]{1,0:T(8,128)(2,1)} %param.10), channel_id=1, source_target_pairs={{0,8},{8,16},{16,24},{1,9},{9,17},{17,25},{2,10},{10,18},{18,26},{... | collective-permute-start | bytes 1572872 | tf_op jit(solution)/shard_map/ppermute | solution.py:57
  42.2 7.0 %collective-permute-done.9 = bf16[128,2048]{1,0:T(8,128)(2,1)} collective-permute-done((bf16[128,2048]{1,0:T(8,128)(2,1)}, bf16[128,2048]{1,0:T(8,128)(2,1)}, u32[]{:S(2)}, u32[]{:S(2)}) %collective-permute-start.9) | collective-permute-done | bytes 524320 | tf_op jit(solution)/shard_map/ppermute | solution.py:58
  52.4 10.8 %collective-permute-done.15 = bf16[128,2048]{1,0:T(8,128)(2,1)S(1)} collective-permute-done((bf16[128,2048]{1,0:T(8,128)(2,1)}, bf16[128,2048]{1,0:T(8,128)(2,1)S(1)}, u32[]{:S(2)}, u32[]{:S(2)}) %collective-permute-start.15) | collective-permute-done | bytes 524320 | tf_op jit(solution)/shard_map/ppermute | solution.py:58
  72.3 8.1 %collective-permute-done.5 = bf16[128,2048]{1,0:T(8,128)(2,1)} collective-permute-done((bf16[128,2048]{1,0:T(8,128)(2,1)}, bf16[128,2048]{1,0:T(8,128)(2,1)}, u32[]{:S(2)}, u32[]{:S(2)}) %collective-permute-start.5) | collective-permute-done | bytes 524320 | tf_op jit(solution)/shard_map/ppermute | solution.py:25
  81.7 6.1 %collective-permute-done.17 = bf16[128,2048]{1,0:T(8,128)(2,1)} collective-permute-done((bf16[128,2048]{1,0:T(8,128)(2,1)S(1)}, bf16[128,2048]{1,0:T(8,128)(2,1)}, u32[]{:S(2)}, u32[]{:S(2)}) %collective-permute-start.17) | collective-permute-done | bytes 524320 | tf_op jit(solution)/shard_map/ppermute | solution.py:25
  94.3 2.5 convolution_convert_fusion.4
  98.4 2.5 convolution_convert_fusion.5
  103.8 7.9 %collective-permute-done.13 = bf16[512,512]{0,1:T(8,128)(2,1)S(1)} collective-permute-done((bf16[512,512]{0,1:T(8,128)(2,1)S(1)}, bf16[512,512]{0,1:T(8,128)(2,1)S(1)}, u32[]{:S(2)}, u32[]{:S(2)}) %collective-permute-start.13) | collective-permute-done | bytes 524320 | tf_op jit(solution)/shard_map/ppermute | solution.py:20
  113.2 2.5 fusion.15
  115.7 7.2 %collective-permute-done.7 = bf16[512,512]{0,1:T(8,128)(2,1)S(1)} collective-permute-done((bf16[512,512]{0,1:T(8,128)(2,1)S(1)}, bf16[512,512]{0,1:T(8,128)(2,1)S(1)}, u32[]{:S(2)}, u32[]{:S(2)}) %collective-permute-start.7) | collective-permute-done | bytes 524320 | tf_op jit(solution)/shard_map/ppermute | solution.py:20
  123.2 2.5 fusion.14
  125.7 7.3 %collective-permute-done.19 = bf16[512,512]{0,1:T(8,128)(2,1)S(1)} collective-permute-done((bf16[512,512]{0,1:T(8,128)(2,1)S(1)}, bf16[512,512]{0,1:T(8,128)(2,1)S(1)}, u32[]{:S(2)}, u32[]{:S(2)}) %collective-permute-start.19) | collective-permute-done | bytes 524320 | tf_op jit(solution)/shard_map/ppermute | solution.py:20
  139.7 7.9 %collective-permute-done.14 = bf16[512,512]{0,1:T(8,128)(2,1)S(1)} collective-permute-done((bf16[512,512]{0,1:T(8,128)(2,1)S(1)}, bf16[512,512]{0,1:T(8,128)(2,1)S(1)}, u32[]{:S(2)}, u32[]{:S(2)}) %collective-permute-start.14) | collective-permute-done | bytes 524320 | tf_op jit(solution)/shard_map/ppermute | solution.py:25
  147.6 20.5 %collective-permute-done.8 = bf16[512,512]{0,1:T(8,128)(2,1)S(1)} collective-permute-done((bf16[512,512]{0,1:T(8,128)(2,1)S(1)}, bf16[512,512]{0,1:T(8,128)(2,1)S(1)}, u32[]{:S(2)}, u32[]{:S(2)}) %collective-permute-start.8) | collective-permute-done | bytes 524320 | tf_op jit(solution)/shard_map/ppermute | solution.py:25
  171.0 3.9 %collective-permute-done.22 = bf16[128,512]{0,1:T(8,128)(2,1)S(1)} collective-permute-done((bf16[128,512]{0,1:T(8,128)(2,1)S(1)}, bf16[128,512]{0,1:T(8,128)(2,1)S(1)}, u32[]{:S(2)}, u32[]{:S(2)}) %collective-permute-start.22) | collective-permute-done | bytes 131104 | tf_op jit(solution)/shard_map/ppermute | solution.py:25
  180.1 11.6 %collective-permute-done.50 = bf16[160,2048]{1,0:T(8,128)(2,1)S(1)} collective-permute-done((bf16[160,2048]{1,0:T(8,128)(2,1)S(1)}, bf16[160,2048]{1,0:T(8,128)(2,1)S(1)}, u32[]{:S(2)}, u32[]{:S(2)}) %collective-permute-start.50) | collective-permute-done | bytes 655392 | tf_op jit(solution)/shard_map/ppermute | solution.py:25
  195.4 4.2 %collective-permute-done.45 = bf16[80,2048]{1,0:T(8,128)(2,1)S(1)} collective-permute-done((bf16[80,2048]{1,0:T(8,128)(2,1)S(1)}, bf16[80,2048]{1,0:T(8,128)(2,1)S(1)}, u32[]{:S(2)}, u32[]{:S(2)}) %collective-permute-start.45) | collective-permute-done | bytes 327712 | tf_op jit(solution)/shard_map/ppermute | solution.py:20
  202.1 2.7 collective-permute-done.51
  205.9 13.0 %collective-permute-done.25 = bf16[80,2048]{1,0:T(8,128)(2,1)S(1)} collective-permute-done((bf16[80,2048]{1,0:T(8,128)(2,1)S(1)}, bf16[80,2048]{1,0:T(8,128)(2,1)S(1)}, u32[]{:S(2)}, u32[]{:S(2)}) %collective-permute-start.25) | collective-permute-done | bytes 327712 | tf_op jit(solution)/shard_map/ppermute | solution.py:25
  221.0 6.1 %collective-permute-done.32 = bf16[80,2048]{1,0:T(8,128)(2,1)S(1)} collective-permute-done((bf16[80,2048]{1,0:T(8,128)(2,1)S(1)}, bf16[80,2048]{1,0:T(8,128)(2,1)S(1)}, u32[]{:S(2)}, u32[]{:S(2)}) %collective-permute-start.32) | collective-permute-done | bytes 327712 | tf_op jit(solution)/shard_map/ppermute | solution.py:25
  229.4 5.0 %collective-permute-done.26 = bf16[160,2048]{1,0:T(8,128)(2,1)S(1)} collective-permute-done((bf16[160,2048]{1,0:T(8,128)(2,1)S(1)}, bf16[160,2048]{1,0:T(8,128)(2,1)S(1)}, u32[]{:S(2)}, u32[]{:S(2)}) %collective-permute-start.26) | collective-permute-done | bytes 655392 | tf_op jit(solution)/shard_map/ppermute | solution.py:20
  235.0 10.4 %collective-permute-done.35 = bf16[160,2048]{1,0:T(8,128)(2,1)S(1)} collective-permute-done((bf16[160,2048]{1,0:T(8,128)(2,1)S(1)}, bf16[160,2048]{1,0:T(8,128)(2,1)S(1)}, u32[]{:S(2)}, u32[]{:S(2)}) %collective-permute-start.35) | collective-permute-done | bytes 655392 | tf_op jit(solution)/shard_map/ppermute | solution.py:25
  250.4 5.3 %collective-permute-done.28 = bf16[80,2048]{1,0:T(8,128)(2,1)S(1)} collective-permute-done((bf16[80,2048]{1,0:T(8,128)(2,1)S(1)}, bf16[80,2048]{1,0:T(8,128)(2,1)S(1)}, u32[]{:S(2)}, u32[]{:S(2)}) %collective-permute-start.28) | collective-permute-done | bytes 327712 | tf_op jit(solution)/shard_map/ppermute | solution.py:20
  258.8 6.1 %collective-permute-done.36 = bf16[80,2048]{1,0:T(8,128)(2,1)S(1)} collective-permute-done((bf16[80,2048]{1,0:T(8,128)(2,1)S(1)}, bf16[80,2048]{1,0:T(8,128)(2,1)S(1)}, u32[]{:S(2)}, u32[]{:S(2)}) %collective-permute-start.36) | collective-permute-done | bytes 327712 | tf_op jit(solution)/shard_map/ppermute | solution.py:20
  281.2 13.6 %fusion.1 = f32[1280,688]{0,1:T(8,128)} fusion(bf16[640,4096]{1,0:T(8,128)(2,1)S(1)} %bitcast.70, bf16[640,4096]{1,0:T(8,128)(2,1)} %slice_dynamic-update-slice_fusion.24, bf16[1,688,4096]{2,1,0:T(8,128)(2,1)} %param.16), kind=kOutput, calls=%fused_computation.3 | convolution fusion | flops 7235174400 | bytes 19644416 | tf_op jit(solution)/shard_map/dot_general | solution.py:200
  301.0 2.6 broadcast_select_fusion.3
  306.3 13.9 %fusion.6 = f32[1280,688]{0,1:T(8,128)} fusion(bf16[1,4096,688]{1,2,0:T(8,128)(2,1)} %param.14, bf16[640,4096]{1,0:T(8,128)(2,1)S(1)} %copy-done.17, bf16[640,4096]{1,0:T(8,128)(2,1)S(1)} %slice_dynamic-update-slice_fusion.8), kind=kOutput, calls=%fused_computation.10 | convolution fusion | flops 7235174400 | bytes 19644416 | tf_op jit(solution)/shard_map/dot_general | solution.py:203
  320.1 12.0 %fusion.8 = f32[1280,688]{0,1:T(8,128)} fusion(bf16[1,4096,688]{1,2,0:T(8,128)(2,1)} %param.15, bf16[640,4096]{1,0:T(8,128)(2,1)S(1)} %copy-done.17, bf16[640,4096]{1,0:T(8,128)(2,1)S(1)} %slice_dynamic-update-slice_fusion.8), kind=kOutput, calls=%fused_computation.12 | convolution fusion | flops 7235174400 | bytes 19644416 | tf_op jit(solution)/shard_map/dot_general | solution.py:204
  332.2 13.3 %fusion.5 = bf16[1,688,4096]{2,1,0:T(8,128)(2,1)} fusion(bf16[640,4096]{1,0:T(8,128)(2,1)S(1)} %bitcast.70, bf16[640,4096]{1,0:T(8,128)(2,1)} %slice_dynamic-update-slice_fusion.24, f32[1280,688]{0,1:T(8,128)} %fusion.8, f32[1280,688]{0,1:T(8,128)} %fusion.6), kind=kOutput, calls=%fused_computation.9 | convolution fusion | flops 7243276288 | bytes 23166976 | tf_op jit(solution)/shard_map/dot_general | solution.py:215
  345.5 16.1 %fusion.3 = bf16[1,4096,688]{1,2,0:T(8,128)(2,1)} fusion(f32[1280,688]{0,1:T(8,128)} %fusion.6, f32[1280,688]{0,1:T(8,128)S(1)} %copy-done.20, f32[1280,688]{0,1:T(8,128)} %fusion.8, bf16[640,4096]{1,0:T(8,128)(2,1)} %copy-done.16, bf16[640,4096]{1,0:T(8,128)(2,1)} %copy-done.18), kind=kOutput, calls=%fused_computation.7 | convolution fusion | flops 7246798848 | bytes 26689536 | tf_op jit(solution)/shard_map/dot_general | solution.py:213
  361.6 12.2 %fusion.4 = bf16[1,4096,688]{1,2,0:T(8,128)(2,1)} fusion(f32[1280,688]{0,1:T(8,128)S(1)} %copy-done.20, f32[1280,688]{0,1:T(8,128)} %fusion.6, bf16[640,4096]{1,0:T(8,128)(2,1)S(1)} %bitcast.72, bf16[640,4096]{1,0:T(8,128)(2,1)} %copy-done.18), kind=kOutput, calls=%fused_computation.8 | convolution fusion | flops 7243276288 | bytes 23166976 | tf_op jit(solution)/shard_map/dot_general | solution.py:214
  (287 shorter events, 120.2 us)
Async XLA Ops:
  0.6 40.7 %collective-permute-start = (bf16[128,2048]{1,0:T(8,128)(2,1)}, bf16[128,2048]{1,0:T(8,128)(2,1)S(1)}, u32[]{:S(2)}, u32[]{:S(2)}) collective-permute-start(bf16[128,2048]{1,0:T(8,128)(2,1)} %param.10), channel_id=1, source_target_pairs={{0,2},{1,3},{2,0},{3,1},{4,6},{5,7},{6,4},{7,5},{8,10},{9,11},{10,... | collective-permute-start | bytes 1572872 | tf_op jit(solution)/shard_map/ppermute | solution.py:25
  3.7 26.4 %collective-permute-start.4 = (bf16[128,2048]{1,0:T(8,128)(2,1)}, bf16[128,2048]{1,0:T(8,128)(2,1)}, u32[]{:S(2)}, u32[]{:S(2)}) collective-permute-start(bf16[128,2048]{1,0:T(8,128)(2,1)} %param.10), channel_id=1, source_target_pairs={{0,8},{8,16},{16,24},{1,9},{9,17},{17,25},{2,10},{10,18},{18,26},{... | collective-permute-start | bytes 1572872 | tf_op jit(solution)/shard_map/ppermute | solution.py:57
  8.0 23.5 %collective-permute-start.3 = (bf16[128,2048]{1,0:T(8,128)(2,1)}, bf16[128,2048]{1,0:T(8,128)(2,1)}, u32[]{:S(2)}, u32[]{:S(2)}) collective-permute-start(bf16[128,2048]{1,0:T(8,128)(2,1)} %param.10), channel_id=1, source_target_pairs={{8,0},{16,8},{24,16},{9,1},{17,9},{25,17},{10,2},{18,10},{26,18},{... | collective-permute-start | bytes 1572872 | tf_op jit(solution)/shard_map/ppermute | solution.py:58
  31.5 17.7 %collective-permute-start.9 = (bf16[128,2048]{1,0:T(8,128)(2,1)}, bf16[128,2048]{1,0:T(8,128)(2,1)}, u32[]{:S(2)}, u32[]{:S(2)}) collective-permute-start(bf16[128,2048]{1,0:T(8,128)(2,1)} %collective-permute-done.3), channel_id=1, source_target_pairs={{8,0},{16,8},{9,1},{17,9},{10,2},{18,10},{11,3},{19,11},{12,4},{20... | collective-permute-start | bytes 1572872 | tf_op jit(solution)/shard_map/ppermute | solution.py:58
  41.4 27.0 %collective-permute-start.1 = (bf16[256,2048]{1,0:T(8,128)(2,1)S(1)}, bf16[256,2048]{1,0:T(8,128)(2,1)S(1)}, u32[]{:S(2)}, u32[]{:S(2)}) collective-permute-start(bf16[256,2048]{1,0:T(8,128)(2,1)S(1)} %pad_maximum_fusion.20), channel_id=1, source_target_pairs={{0,1},{1,0},{2,3},{3,2},{4,5},{5,4},{6,7},{7,6},{8,9},{9,8},{10,11... | collective-permute-start | bytes 3145736 | tf_op jit(solution)/shard_map/ppermute | solution.py:25
  65.8 22.0 %collective-permute-start.17 = (bf16[128,2048]{1,0:T(8,128)(2,1)S(1)}, bf16[128,2048]{1,0:T(8,128)(2,1)}, u32[]{:S(2)}, u32[]{:S(2)}) collective-permute-start(bf16[128,2048]{1,0:T(8,128)(2,1)S(1)} %get-tuple-element.58), channel_id=1, source_target_pairs={{0,2},{1,3},{2,0},{3,1},{4,6},{5,7},{6,4},{7,5},{8,10},{9,11},{10,... | collective-permute-start | bytes 1572872 | tf_op jit(solution)/shard_map/ppermute | solution.py:25
  68.4 23.6 %collective-permute-start.12 = (bf16[256,2048]{1,0:T(8,128)(2,1)}, bf16[256,2048]{1,0:T(8,128)(2,1)}, u32[]{:S(2)}, u32[]{:S(2)}) collective-permute-start(bf16[256,2048]{1,0:T(8,128)(2,1)} %pad_maximum_fusion.22), channel_id=1, source_target_pairs={{0,1},{1,0},{2,3},{3,2},{4,5},{5,4},{6,7},{7,6},{8,9},{9,8},{10,11... | collective-permute-start | bytes 3145736 | tf_op jit(solution)/shard_map/ppermute | solution.py:25
  70.6 18.3 %collective-permute-start.2 = (bf16[512,512]{0,1:T(8,128)(2,1)}, bf16[512,512]{0,1:T(8,128)(2,1)}, u32[]{:S(2)}, u32[]{:S(2)}) collective-permute-start(bf16[512,512]{0,1:T(8,128)(2,1)} %convolution_convert_fusion.6), channel_id=1, source_target_pairs={{0,4},{4,0},{1,5},{5,1},{2,6},{6,2},{3,7},{7,3},{8,12},{12,8},{9,1... | collective-permute-start | bytes 1572872 | tf_op jit(solution)/shard_map/ppermute | solution.py:20
  72.1 63.2 %collective-permute-start.40 = (bf16[80,2048]{1,0:T(8,128)(2,1)}, bf16[80,2048]{1,0:T(8,128)(2,1)S(1)}, u32[]{:S(2)}, u32[]{:S(2)}) collective-permute-start(bf16[80,2048]{1,0:T(8,128)(2,1)} %get-tuple-element.12), channel_id=1, source_target_pairs={{0,8},{8,0},{16,24},{24,16},{1,9},{9,1},{17,25},{25,17},{2,10},{10... | collective-permute-start | bytes 983048 | tf_op jit(solution)/shard_map/ppermute | solution.py:25
  80.4 56.6 %collective-permute-start.41 = (bf16[80,2048]{1,0:T(8,128)(2,1)}, bf16[80,2048]{1,0:T(8,128)(2,1)S(1)}, u32[]{:S(2)}, u32[]{:S(2)}) collective-permute-start(bf16[80,2048]{1,0:T(8,128)(2,1)} %get-tuple-element.13), channel_id=1, source_target_pairs={{0,16},{8,24},{16,0},{24,8},{1,17},{9,25},{17,1},{25,9},{2,18},{10... | collective-permute-start | bytes 983048 | tf_op jit(solution)/shard_map/ppermute | solution.py:25
  92.0 45.0 %collective-permute-start.42 = (bf16[80,2048]{1,0:T(8,128)(2,1)S(1)}, bf16[80,2048]{1,0:T(8,128)(2,1)S(1)}, u32[]{:S(2)}, u32[]{:S(2)}) collective-permute-start(bf16[80,2048]{1,0:T(8,128)(2,1)S(1)} %copy-done.11), channel_id=1, source_target_pairs={{0,24},{8,16},{16,8},{24,0},{1,25},{9,17},{17,9},{25,1},{2,26},{10... | collective-permute-start | bytes 983048 | tf_op jit(solution)/shard_map/ppermute | solution.py:25
  100.9 22.1 %collective-permute-start.7 = (bf16[512,512]{0,1:T(8,128)(2,1)S(1)}, bf16[512,512]{0,1:T(8,128)(2,1)S(1)}, u32[]{:S(2)}, u32[]{:S(2)}) collective-permute-start(bf16[512,512]{0,1:T(8,128)(2,1)S(1)} %convolution_convert_fusion.5), channel_id=1, source_target_pairs={{0,4},{4,0},{1,5},{5,1},{2,6},{6,2},{3,7},{7,3},{8,12},{12,8},{9,1... | collective-permute-start | bytes 1572872 | tf_op jit(solution)/shard_map/ppermute | solution.py:20
  111.7 21.2 %collective-permute-start.19 = (bf16[512,512]{0,1:T(8,128)(2,1)S(1)}, bf16[512,512]{0,1:T(8,128)(2,1)S(1)}, u32[]{:S(2)}, u32[]{:S(2)}) collective-permute-start(bf16[512,512]{0,1:T(8,128)(2,1)S(1)} %convolution_convert_fusion.3), channel_id=1, source_target_pairs={{0,4},{4,0},{1,5},{5,1},{2,6},{6,2},{3,7},{7,3},{8,12},{12,8},{9,1... | collective-permute-start | bytes 1572872 | tf_op jit(solution)/shard_map/ppermute | solution.py:20
  123.0 24.6 %collective-permute-start.14 = (bf16[512,512]{0,1:T(8,128)(2,1)S(1)}, bf16[512,512]{0,1:T(8,128)(2,1)S(1)}, u32[]{:S(2)}, u32[]{:S(2)}) collective-permute-start(bf16[512,512]{0,1:T(8,128)(2,1)S(1)} %fusion.15), channel_id=1, source_target_pairs={{0,16},{8,24},{16,0},{24,8},{1,17},{9,25},{17,1},{25,9},{2,18},{10... | collective-permute-start | bytes 1572872 | tf_op jit(solution)/shard_map/ppermute | solution.py:25
  133.0 35.1 %collective-permute-start.8 = (bf16[512,512]{0,1:T(8,128)(2,1)S(1)}, bf16[512,512]{0,1:T(8,128)(2,1)S(1)}, u32[]{:S(2)}, u32[]{:S(2)}) collective-permute-start(bf16[512,512]{0,1:T(8,128)(2,1)S(1)} %fusion.14), channel_id=1, source_target_pairs={{0,8},{8,0},{16,24},{24,16},{1,9},{9,1},{17,25},{25,17},{2,10},{10... | collective-permute-start | bytes 1572872 | tf_op jit(solution)/shard_map/ppermute | solution.py:25
  135.3 32.7 %collective-permute-start.20 = (bf16[512,512]{0,1:T(8,128)(2,1)S(1)}, bf16[512,512]{0,1:T(8,128)(2,1)S(1)}, u32[]{:S(2)}, u32[]{:S(2)}) collective-permute-start(bf16[512,512]{0,1:T(8,128)(2,1)S(1)} %fusion.16), channel_id=1, source_target_pairs={{0,24},{8,16},{16,8},{24,0},{1,25},{9,17},{17,9},{25,1},{2,26},{10... | collective-permute-start | bytes 1572872 | tf_op jit(solution)/shard_map/ppermute | solution.py:25
  137.6 41.1 %collective-permute-start.44 = (bf16[160,2048]{1,0:T(8,128)(2,1)S(1)}, bf16[160,2048]{1,0:T(8,128)(2,1)S(1)}, u32[]{:S(2)}, u32[]{:S(2)}) collective-permute-start(bf16[160,2048]{1,0:T(8,128)(2,1)S(1)} %get-tuple-element.67), channel_id=1, source_target_pairs={{0,2},{1,3},{2,0},{3,1},{4,6},{5,7},{6,4},{7,5},{8,10},{9,11},{10,... | collective-permute-start | bytes 1966088 | tf_op jit(solution)/shard_map/ppermute | solution.py:25
  138.1 41.2 %collective-permute-start.43 = (bf16[160,2048]{1,0:T(8,128)(2,1)S(1)}, bf16[160,2048]{1,0:T(8,128)(2,1)S(1)}, u32[]{:S(2)}, u32[]{:S(2)}) collective-permute-start(bf16[160,2048]{1,0:T(8,128)(2,1)S(1)} %get-tuple-element.67), channel_id=1, source_target_pairs={{0,4},{4,0},{1,5},{5,1},{2,6},{6,2},{3,7},{7,3},{8,12},{12,8},{9,1... | collective-permute-start | bytes 1966088 | tf_op jit(solution)/shard_map/ppermute | solution.py:20
  170.4 21.3 %collective-permute-start.50 = (bf16[160,2048]{1,0:T(8,128)(2,1)S(1)}, bf16[160,2048]{1,0:T(8,128)(2,1)S(1)}, u32[]{:S(2)}, u32[]{:S(2)}) collective-permute-start(bf16[160,2048]{1,0:T(8,128)(2,1)S(1)} %get-tuple-element.71), channel_id=1, source_target_pairs={{0,2},{1,3},{2,0},{3,1},{4,6},{5,7},{6,4},{7,5},{8,10},{9,11},{10,... | collective-permute-start | bytes 1966088 | tf_op jit(solution)/shard_map/ppermute | solution.py:25
  178.8 20.8 %collective-permute-start.45 = (bf16[80,2048]{1,0:T(8,128)(2,1)S(1)}, bf16[80,2048]{1,0:T(8,128)(2,1)S(1)}, u32[]{:S(2)}, u32[]{:S(2)}) collective-permute-start(bf16[80,2048]{1,0:T(8,128)(2,1)S(1)} %slice.361), channel_id=1, source_target_pairs={{0,4},{4,0},{1,5},{5,1},{2,6},{6,2},{3,7},{7,3},{8,12},{12,8},{9,1... | collective-permute-start | bytes 983048 | tf_op jit(solution)/shard_map/ppermute | solution.py:20
  179.4 21.8 %collective-permute-start.46 = (bf16[80,2048]{1,0:T(8,128)(2,1)S(1)}, bf16[80,2048]{1,0:T(8,128)(2,1)S(1)}, u32[]{:S(2)}, u32[]{:S(2)}) collective-permute-start(bf16[80,2048]{1,0:T(8,128)(2,1)S(1)} %slice.362), channel_id=1, source_target_pairs={{0,2},{1,3},{2,0},{3,1},{4,6},{5,7},{6,4},{7,5},{8,10},{9,11},{10,... | collective-permute-start | bytes 983048 | tf_op jit(solution)/shard_map/ppermute | solution.py:25
  191.7 56.8 %collective-permute-start.48 = (bf16[320,2048]{1,0:T(8,128)(2,1)S(1)}, bf16[320,2048]{1,0:T(8,128)(2,1)S(1)}, u32[]{:S(2)}, u32[]{:S(2)}) collective-permute-start(bf16[320,2048]{1,0:T(8,128)(2,1)S(1)} %pad_maximum_fusion.13), channel_id=1, source_target_pairs={{0,1},{1,0},{2,3},{3,2},{4,5},{5,4},{6,7},{7,6},{8,9},{9,8},{10,11... | collective-permute-start | bytes 3932168 | tf_op jit(solution)/shard_map/ppermute | solution.py:25
  199.6 27.6 %collective-permute-start.33 = (bf16[80,2048]{1,0:T(8,128)(2,1)S(1)}, bf16[80,2048]{1,0:T(8,128)(2,1)S(1)}, u32[]{:S(2)}, u32[]{:S(2)}) collective-permute-start(bf16[80,2048]{1,0:T(8,128)(2,1)S(1)} %get-tuple-element.38), channel_id=1, source_target_pairs={{0,24},{8,16},{16,8},{24,0},{1,25},{9,17},{17,9},{25,1},{2,26},{10... | collective-permute-start | bytes 983048 | tf_op jit(solution)/shard_map/ppermute | solution.py:25
  201.2 25.9 %collective-permute-start.32 = (bf16[80,2048]{1,0:T(8,128)(2,1)S(1)}, bf16[80,2048]{1,0:T(8,128)(2,1)S(1)}, u32[]{:S(2)}, u32[]{:S(2)}) collective-permute-start(bf16[80,2048]{1,0:T(8,128)(2,1)S(1)} %get-tuple-element.39), channel_id=1, source_target_pairs={{0,16},{8,24},{16,0},{24,8},{1,17},{9,25},{17,1},{25,9},{2,18},{10... | collective-permute-start | bytes 983048 | tf_op jit(solution)/shard_map/ppermute | solution.py:25
  227.3 18.2 %collective-permute-start.35 = (bf16[160,2048]{1,0:T(8,128)(2,1)S(1)}, bf16[160,2048]{1,0:T(8,128)(2,1)S(1)}, u32[]{:S(2)}, u32[]{:S(2)}) collective-permute-start(bf16[160,2048]{1,0:T(8,128)(2,1)S(1)} %get-tuple-element.75), channel_id=1, source_target_pairs={{0,2},{1,3},{2,0},{3,1},{4,6},{5,7},{6,4},{7,5},{8,10},{9,11},{10,... | collective-permute-start | bytes 1966088 | tf_op jit(solution)/shard_map/ppermute | solution.py:25
  227.8 17.8 %collective-permute-start.34 = (bf16[160,2048]{1,0:T(8,128)(2,1)S(1)}, bf16[160,2048]{1,0:T(8,128)(2,1)S(1)}, u32[]{:S(2)}, u32[]{:S(2)}) collective-permute-start(bf16[160,2048]{1,0:T(8,128)(2,1)S(1)} %get-tuple-element.75), channel_id=1, source_target_pairs={{0,4},{4,0},{1,5},{5,1},{2,6},{6,2},{3,7},{7,3},{8,12},{12,8},{9,1... | collective-permute-start | bytes 1966088 | tf_op jit(solution)/shard_map/ppermute | solution.py:20
  234.4 37.8 %collective-permute-start.47 = (bf16[320,2048]{1,0:T(8,128)(2,1)S(1)}, bf16[320,2048]{1,0:T(8,128)(2,1)}, u32[]{:S(2)}, u32[]{:S(2)}) collective-permute-start(bf16[320,2048]{1,0:T(8,128)(2,1)S(1)} %pad_maximum_fusion.12), channel_id=1, source_target_pairs={{0,1},{1,0},{2,3},{3,2},{4,5},{5,4},{6,7},{7,6},{8,9},{9,8},{10,11... | collective-permute-start | bytes 3932168 | tf_op jit(solution)/shard_map/ppermute | solution.py:25
  245.4 22.9 %collective-permute-start.53 = (bf16[320,2048]{1,0:T(8,128)(2,1)S(1)}, bf16[320,2048]{1,0:T(8,128)(2,1)S(1)}, u32[]{:S(2)}, u32[]{:S(2)}) collective-permute-start(bf16[320,2048]{1,0:T(8,128)(2,1)S(1)} %pad_maximum_fusion.14), channel_id=1, source_target_pairs={{0,1},{1,0},{2,3},{3,2},{4,5},{5,4},{6,7},{7,6},{8,9},{9,8},{10,11... | collective-permute-start | bytes 3932168 | tf_op jit(solution)/shard_map/ppermute | solution.py:25
  250.2 50.8 %collective-permute-start.31 = (bf16[320,2048]{1,0:T(8,128)(2,1)S(1)}, bf16[320,2048]{1,0:T(8,128)(2,1)}, u32[]{:S(2)}, u32[]{:S(2)}) collective-permute-start(bf16[320,2048]{1,0:T(8,128)(2,1)S(1)} %pad_maximum_fusion.17), channel_id=1, source_target_pairs={{0,1},{1,0},{2,3},{3,2},{4,5},{5,4},{6,7},{7,6},{8,9},{9,8},{10,11... | collective-permute-start | bytes 3932168 | tf_op jit(solution)/shard_map/ppermute | solution.py:25
  264.9 29.9 %collective-permute-start.39 = (bf16[320,2048]{1,0:T(8,128)(2,1)}, bf16[320,2048]{1,0:T(8,128)(2,1)}, u32[]{:S(2)}, u32[]{:S(2)}) collective-permute-start(bf16[320,2048]{1,0:T(8,128)(2,1)} %pad_maximum_fusion.19), channel_id=1, source_target_pairs={{0,1},{1,0},{2,3},{3,2},{4,5},{5,4},{6,7},{7,6},{8,9},{9,8},{10,11... | collective-permute-start | bytes 3932168 | tf_op jit(solution)/shard_map/ppermute | solution.py:25
  267.1 31.5 %collective-permute-start.30 = (bf16[320,2048]{1,0:T(8,128)(2,1)}, bf16[320,2048]{1,0:T(8,128)(2,1)}, u32[]{:S(2)}, u32[]{:S(2)}) collective-permute-start(bf16[320,2048]{1,0:T(8,128)(2,1)} %pad_maximum_fusion.16), channel_id=1, source_target_pairs={{0,1},{1,0},{2,3},{3,2},{4,5},{5,4},{6,7},{7,6},{8,9},{9,8},{10,11... | collective-permute-start | bytes 3932168 | tf_op jit(solution)/shard_map/ppermute | solution.py:25
  268.3 27.9 %collective-permute-start.38 = (bf16[320,2048]{1,0:T(8,128)(2,1)}, bf16[320,2048]{1,0:T(8,128)(2,1)}, u32[]{:S(2)}, u32[]{:S(2)}) collective-permute-start(bf16[320,2048]{1,0:T(8,128)(2,1)} %pad_maximum_fusion.18), channel_id=1, source_target_pairs={{0,1},{1,0},{2,3},{3,2},{4,5},{5,4},{6,7},{7,6},{8,9},{9,8},{10,11... | collective-permute-start | bytes 3932168 | tf_op jit(solution)/shard_map/ppermute | solution.py:25
  (48 other events, 584.8 us)

commit v2 on v1

v2 whole, which is shorter than its diff:
```python
import functools

import jax
import jax.numpy as jnp
from jax import lax
from jax.experimental import pallas as pl
from jax.experimental.pallas import tpu as pltpu
from jax.sharding import PartitionSpec as P


def slot_positions(id_block, capacity, experts):
    rows = id_block.shape[0]
    picks = jnp.concatenate([id_block[:, 0], id_block[:, 1]], axis=0)
    onehot = (picks[:, None] == jnp.arange(experts, dtype=jnp.int32)[None, :]).astype(jnp.int32)
    position = jnp.sum((jnp.cumsum(onehot, axis=0) - 1) * onehot, axis=1)
    position = jnp.where(position < capacity, position, -1)
    return jnp.stack([position[:rows], position[rows:]], axis=1)


def shift(value, axis, step):
    size = lax.axis_size(axis)
    return lax.ppermute(value, axis, [(i, (i + step) % size) for i in range(size)])


def flip(value, axis, mask):
    size = lax.axis_size(axis)
    return lax.ppermute(value, axis, [(i, i ^ mask) for i in range(size)])


def masks(size):
    out, mask = [], size // 2
    while mask >= 1:
        out.append(mask)
        mask //= 2
    return out


def relative_order(size):
    order = [0]
    for mask in masks(size):
        order = order + [o ^ mask for o in order]
    return order


def gather_flips(block, axis, todo):
    for mask in todo:
        block = jnp.concatenate([block, flip(block, axis, mask)], axis=0)
    return block


def pick_flip(got, axis, mask):
    size, me = lax.axis_size(axis), lax.axis_index(axis)
    value = None
    for k in sorted({i - (i ^ mask) for i in range(size)}, key=abs):
        where = functools.reduce(jnp.logical_or, [me == i for i in range(size) if i - (i ^ mask) == k])
        value = got[k] if value is None else jnp.where(where, got[k], value)
    return value


def column_kernel(_, value_ref, out_ref):
    out_ref[...] = value_ref[...]


def pick_columns(value, piece, count, stride, first):
    rows = value.shape[0]
    tile = rows if rows <= 512 else 512
    return pl.pallas_call(
        column_kernel,
        grid_spec=pltpu.PrefetchScalarGridSpec(
            num_scalar_prefetch=1,
            grid=(rows // tile, count),
            in_specs=[pl.BlockSpec((tile, piece), lambda i, k, at: (i, k * stride + at[0]))],
            out_specs=pl.BlockSpec((tile, piece), lambda i, k, at: (i, k)),
        ),
        out_shape=jax.ShapeDtypeStruct((rows, count * piece), value.dtype),
    )(jnp.full((1,), first, jnp.int32), value)


def order_kernel(n_mp, n_dp, piece, sources, at, *refs):
    out_ref = refs[-1]
    turn = at[n_mp + pl.program_id(0)]
    for c in range(sources):

        @pl.when(turn == c)
        def _():
            for p in range(n_mp):
                step = at[p]
                for k in range(n_dp):
                    first = (k * n_mp + p) * piece
                    out_ref[:, first : first + piece] = refs[c][step, 0, 0, :, k * piece : (k + 1) * piece]


def order_rows(values, groups, n_dp, piece):
    n_mp, x = values[0].shape[0], lax.axis_index("mp")
    sources, part = len(values), n_dp // len(values)
    slots = sum(len(g) for g in groups)
    rows = values[0].shape[1] // (part * slots)
    places = [(j // part, j % part, m) for g in groups for j in range(n_dp) for m in g]
    count = len(places)
    columns = [[c for c, _, _ in places]]
    for c in range(sources):
        held = next((j, m) for i, j, m in places if i == c)
        kept = []
        for i, j, m in places:
            held = (j, m) if i == c else held
            kept.append(held)
        columns += [[j for j, _ in kept], [m for _, m in kept]]
    steps = (x - jnp.arange(n_mp, dtype=jnp.int32)) % n_mp
    table = jnp.concatenate([steps, jnp.asarray(sum(columns, []), jnp.int32)])

    def spec(c):
        base = n_mp + count * (1 + 2 * c)
        return pl.BlockSpec(
            (n_mp, 1, 1, rows, n_dp * piece), lambda i, at: (0, at[base + i], at[base + count + i], 0, 0)
        )

    return pl.pallas_call(
        functools.partial(order_kernel, n_mp, n_dp, piece, sources),
        grid_spec=pltpu.PrefetchScalarGridSpec(
            num_scalar_prefetch=1,
            grid=(count,),
            in_specs=[spec(c) for c in range(sources)],
            out_specs=pl.BlockSpec((rows, n_mp * n_dp * piece), lambda i, at: (i, 0)),
        ),
        out_shape=jax.ShapeDtypeStruct((count * rows, n_mp * n_dp * piece), values[0].dtype),
        compiler_params=pltpu.CompilerParams(vmem_limit_bytes=32 << 20),
    )(table, *[v.reshape(n_mp, part, slots, rows, n_dp * piece) for v in values])


def whole_columns(across, piece):
    n_mp, n_dp, x = lax.axis_size("mp"), lax.axis_size("dp"), lax.axis_index("mp")
    parts = []
    for p in range(n_mp):
        value = across[0]
        for s in range(1, n_mp):
            value = jnp.where((x - s) % n_mp == p, across[s], value)
        parts.append(value)
    return jnp.concatenate(
        [part[:, k * piece : (k + 1) * piece] for k in range(n_dp) for part in parts], axis=1
    )


def per_device(
    context,
    residual,
    attn_weight,
    norm_gain,
    gate_weight,
    up_weight,
    down_weight,
    cotangent,
    expert_ids,
    gate_fixed,
):
    n_br, n_mp, n_dp = lax.axis_size("branch"), lax.axis_size("mp"), lax.axis_size("dp")
    z, x, d = lax.axis_index("branch"), lax.axis_index("mp"), lax.axis_index("dp")
    tokens, width = residual.shape
    experts = n_br * gate_weight.shape[0]
    capacity = 5 * tokens // (2 * experts)
    piece = width // (n_dp * n_mp)
    hidden_width = gate_weight.shape[2]
    padded_width = -(-hidden_width // 128) * 128

    def choose(options, index):
        value = options[0]
        for i in range(1, len(options)):
            value = jnp.where(index == i, options[i], value)
        return value

    def my_columns(value):
        return pick_columns(value, piece, n_dp, n_mp, x)

    def choose(options, index):
        value = options[0]
        for i in range(1, len(options)):
            value = jnp.where(index == i, options[i], value)
        return value

    far_masks = masks(n_dp)[:1]
    core_masks = masks(n_dp)[1:]
    near = n_br // 2
    groups = [g for g in ([0], list(range(1, near + 1)), list(range(near + 1, n_br))) if g]

    live = {}

    def fence():
        names = sorted(live)
        for name, value in zip(names, lax.optimization_barrier(tuple(live[n] for n in names))):
            live[name] = value

    def hop_plane(name, g):
        for m in groups[g]:
            if m:
                live[f"{name}{m}"] = flip(live[f"{name}{m}"], "branch", m)

    def hop_near(name, g):
        block = jnp.concatenate([live.pop(f"{name}{m}") for m in groups[g]], axis=0)
        live[f"{name}a{g}_0"] = block
        for s in range(1, n_mp):
            live[f"{name}a{g}_{s}"] = shift(block, "mp", s)
        for mask in far_masks:
            live[f"{name}f{g}"] = flip(block, "dp", mask)

    def hop_far(name, g):
        across = [live.pop(f"{name}a{g}_{t}") for t in range(n_mp)]
        parts = [across[0]]
        if far_masks:
            far = live.pop(f"{name}f{g}")
            half = far.shape[0] // 2
            parts += [far]
            for t in range(1, n_mp):
                parts += [across[t], shift(far[:half], "mp", t), flip(across[t][half:], "dp", far_masks[0])]
        else:
            parts += across[1:]
        live[f"{name}a{g}"] = jnp.concatenate(parts, axis=0)

    def hop_rest(name, g):
        block = live[f"{name}a{g}"]
        block = block.reshape(n_mp, -1, block.shape[1])
        for mask in core_masks:
            block = jnp.concatenate([block, flip(block, "dp", mask)], axis=1)
        live[f"{name}a{g}"] = block

    def finish(name, g):
        block = live.pop(f"{name}a{g}")
        return whole_columns([block[t] for t in range(n_mp)], piece)

    def cascade(name, at):
        for g in range(len(groups)):
            for lag, hop in ((0, hop_plane), (1, hop_near), (2, hop_far), (3, hop_rest)):
                if at == g - 1 + lag:
                    hop(name, g)

    slots = slot_positions(expert_ids, capacity, experts)
    slot_code = jnp.where(slots >= 0, (expert_ids ^ z) * capacity + slots, -1)
    target = jnp.arange(experts * capacity, dtype=jnp.int32)[:, None]
    matches = [slot_code[:, k][None, :] == target for k in range(2)]
    selector = (matches[0] | matches[1]).astype(jnp.bfloat16)
    gate = gate_fixed.astype(jnp.float32) / 32768.0
    row_gate = sum(jnp.where(matches[k], gate[:, k][None, :], 0.0) for k in range(2))
    row_gate = jnp.sum(row_gate, axis=1, keepdims=True)

    live["weight"] = attn_weight[0]
    live["selector"], live["row_gate"] = selector, row_gate
    live["up0"], live["down0"], live["ctx0"] = context, context, context
    live["cotangent"], live["residual"], live["gain"] = cotangent, residual, norm_gain[None, :]

    def distance(m):
        return max(abs(i - (i ^ m)) for i in range(n_br))

    for r in range(n_br + 3):
        if r + 1 < n_br:
            k = r + 1
            live[f"up{k}"] = lax.ppermute(live[f"up{r}"], "branch", [(i, i + 1) for i in range(r, n_br - 1)])
            live[f"down{k}"] = lax.ppermute(live[f"down{r}"], "branch", [(i + 1, i) for i in range(n_br - k)])
        for m in range(n_br):
            s = distance(m)
            if r == s and m:
                got = {k: live[f"up{k}" if k > 0 else f"down{-k}"] for k in {i - (i ^ m) for i in range(n_br)}}
                live[f"ctx{m}"] = pick_flip(got, "branch", m)
            if r == s:
                live[f"ctx{m}"] = gather_flips(live[f"ctx{m}"], "dp", far_masks)
            if r == s + 1:
                live[f"ctx{m}"] = gather_flips(live[f"ctx{m}"], "dp", core_masks)
            if r == s + 2:
                ctx = live.pop(f"ctx{m}")
                for t in list(range(1, n_mp)) + [0]:
                    product = jnp.dot(ctx, live[f"weight{t}"], preferred_element_type=jnp.float32)
                    product = product.astype(jnp.bfloat16)
                    live[f"part{m}_{t}"] = shift(product, "mp", t) if t else product
            if r == s + 3 or (r == n_br + 2 and s + 3 > r):
                share = sum(live.pop(f"part{m}_{t}").astype(jnp.float32) for t in range(n_mp))
                live[f"share{m}"] = flip(share.astype(jnp.bfloat16), "branch", m) if m else share
        if r == 1:
            weight = live.pop("weight")
            cut = [weight[:, p * piece : (p + 1) * piece] for p in range(n_mp)]
            for t in range(n_mp):
                live[f"weight{t}"] = choose([cut[(p + t) % n_mp] for p in range(n_mp)], x)
        if r == 2:
            rows = jnp.dot(live["selector"], my_columns(live.pop("cotangent")), preferred_element_type=jnp.float32)
            rows = (rows * live.pop("row_gate")).astype(jnp.bfloat16)
            for m in range(n_br):
                live[f"cot{m}"] = rows[m * capacity : (m + 1) * capacity]
        if r == n_br + 2:
            pad = jnp.zeros((width, padded_width - hidden_width), gate_weight.dtype)
            live["gate_up"] = jnp.concatenate([gate_weight[0], pad, up_weight[0]], axis=1)
        if r == n_br:
            live["residual"] = my_columns(live["residual"])
            live["gain"] = my_columns(live["gain"])
        if n_br - 1 <= r < n_br + 1 and r - n_br + 2 < len(groups):
            hop_plane("cot", r - n_br + 2)
        if r == n_br:
            block = live["cot_first"] = jnp.concatenate([live.pop(f"cot{m}") for m in range(near + 1)], axis=0)
            live["cot_first_far"] = flip(block, "dp", far_masks[0])
        if r == n_br + 1:
            block = jnp.concatenate([live.pop(f"cot{m}") for m in range(near + 1, n_br)], axis=0)
            far = jnp.concatenate([live.pop("cot_first_far"), flip(block, "dp", far_masks[0])], axis=0)
            block = jnp.concatenate([live.pop("cot_first"), block], axis=0)
            live["cot"], live["cot_far"] = block, far
            for t in range(1, n_mp):
                live[f"cot_top{t}"] = shift(block[: near * capacity], "mp", t)
        if r == n_br + 2:
            block, far = live.pop("cot"), live.pop("cot_far")
            parts = [block, far]
            first = (near + 1) * capacity
            both = jnp.concatenate([block[near * capacity :], far[near * capacity : first]], axis=0)
            rest = block.shape[0] - near * capacity
            for t in range(1, n_mp):
                top = live.pop(f"cot_top{t}")
                across = shift(both, "mp", t)
                parts += [top, across[:rest], flip(top, "dp", far_masks[0]), across[rest:]]
                live[f"cot_end{t}"] = far[first:]
            live["cota0"] = jnp.concatenate(parts[:2], axis=0)
            live["cota_across"] = jnp.concatenate(parts[2:], axis=0)
        fence()

    total = sum(live.pop(f"share{m}").astype(jnp.float32) for m in range(n_br))
    total = (total / n_br).astype(jnp.bfloat16)
    got = [None] * n_dp
    for i, o in enumerate(relative_order(n_dp)):
        block = total[i * tokens : (i + 1) * tokens]
        got[o] = flip(block, "dp", o) if o else block
    parts, across = [live.pop("cota0")], live.pop("cota_across")
    size = across.shape[0] // (n_mp - 1) if n_mp > 1 else 0
    for t in range(1, n_mp):
        parts += [across[(t - 1) * size : t * size], shift(live.pop(f"cot_end{t}"), "mp", t)]
    for i, part in enumerate(parts):
        live[f"cot_part{i}"] = part
    cot_parts = len(parts)
    live["attention"] = jnp.concatenate([choose(got, d ^ k) for k in range(n_dp)], axis=1)
    fence()

    mixed = live.pop("residual").astype(jnp.float32) + live.pop("attention").astype(jnp.float32)
    squares = jnp.sum(mixed * mixed, axis=1, keepdims=True)
    all_squares = squares
    for s in range(1, n_mp):
        all_squares = all_squares + shift(squares.reshape(1, tokens), "mp", s).reshape(tokens, 1)
    live["mixed"], live["squares"] = mixed, all_squares
    fence()

    inv_rms = lax.rsqrt(live.pop("squares") / width + 1e-05)
    normed = (live.pop("mixed") * inv_rms * live.pop("gain").astype(jnp.float32)).astype(jnp.bfloat16)
    send_in = jnp.dot(live.pop("selector"), normed, preferred_element_type=jnp.float32).astype(jnp.bfloat16)
    for m in range(n_br):
        live[f"in{m}"] = send_in[m * capacity : (m + 1) * capacity]
    for r in range(len(groups) + 2):
        cascade("in", r)
        if r == 0:
            live["cota0"] = jnp.concatenate([live.pop(f"cot_part{i}") for i in range(cot_parts)], axis=0)
            for c in range(1, 1 << len(core_masks)):
                live[f"cota{c}"] = flip(live["cota0"], "dp", sum(v for i, v in enumerate(core_masks) if c >> i & 1))
        if r == 1:
            blocks = [live.pop(f"cota{c}") for c in range(1 << len(core_masks))]
            live["cotan"] = order_rows([v.reshape(n_mp, -1, n_dp * piece) for v in blocks], groups, n_dp, piece)
        if r == 2:
            live["back"] = lax.dot_general(
                live["cotan"], down_weight[0], (((1,), (1,)), ((), ())), preferred_element_type=jnp.float32
            )
        fence()
    cotan_rows, back_grad = live.pop("cotan"), live.pop("back")
    tokens_in = jnp.concatenate([finish("in", g) for g in range(len(groups))], axis=0)
    pre = jnp.dot(tokens_in, live.pop("gate_up"), preferred_element_type=jnp.float32)
    pre_gate, pre_up = pre[:, :hidden_width], pre[:, padded_width:]
    sigmoid_gate = jax.nn.sigmoid(pre_gate)
    active = pre_gate * sigmoid_gate
    hidden = (active * pre_up).astype(jnp.bfloat16)
    d_gate = (back_grad * pre_up * sigmoid_gate * (1.0 + pre_gate * (1.0 - sigmoid_gate))).astype(jnp.bfloat16)
    d_up = (back_grad * active).astype(jnp.bfloat16)
    contract = (((0,), (0,)), ((), ()))
    grads = []
    for left, right in ((tokens_in, d_gate), (tokens_in, d_up), (hidden, cotan_rows)):
        grad = lax.dot_general(left, right, contract, preferred_element_type=jnp.float32)
        grads.append(grad.astype(jnp.bfloat16)[None])
    return tuple(grads)


def solution(mesh):
    return jax.shard_map(
        per_device,
        mesh=mesh,
        in_specs=(
            P(("branch", "dp"), "mp"),
            P(("branch", "dp"), None),
            P("branch", "mp", "dp"),
            P(),
            P("branch", None, ("mp", "dp")),
            P("branch", None, ("mp", "dp")),
            P("branch", ("mp", "dp"), None),
            P(("branch", "dp"), None),
            P(("branch", "dp"), None),
            P(("branch", "dp"), None),
        ),
        out_specs=(
            P("branch", None, ("mp", "dp")),
            P("branch", None, ("mp", "dp")),
            P("branch", ("mp", "dp"), None),
        ),
        check_vma=False,
    )
```

time: 378 us -> 350 us (0.926)
  waiting for transfers between devices: 154 us -> 114 us
  local copies, waits for them, and re-layouts: 42.3 us -> 17.8 us
  other arithmetic: 23.3 us -> 46.3 us
  starting transfers between devices: 50.7 us -> 64.4 us
  matrix products: 102 us -> 89.4 us
  Pallas kernels: 0 us -> 11.8 us
    concatenate x9 -> x11, other arithmetic: 4.02 us -> 26.9 us  [the longest x1 16 us: per_device(): jnp.concatenate([gate_weight[0], pad, up_weight[0]], axis=1)]
    unnamed x117 -> x92, local copies, waits for them, and re-layouts: 29.5 us -> 12 us
    ppermute x6, waiting for transfers between devices: 17.8 us -> 2.19 us  [the longest x3 2.18 us: per_device(): lax.ppermute(live[f'up{r}'], 'branch', [(i, i + 1) for i in range(r, n_br...]
    ppermute x36 -> x33, starting transfers between devices: 22.6 us -> 35.6 us  [flip(): return lax.ppermute(value, axis, [(i, i ^ mask) for i in range(size)])]
    ppermute x13 -> x14, waiting for transfers between devices: 46.3 us -> 33.9 us  [shift(): lax.ppermute(value, axis, [(i, (i + step) % size) for i in range(size)])]
    dot_general x16 -> x15, matrix products: 102 us -> 89.4 us  [the longest x3 43.3 us: per_device(): lax.dot_general(left, right, contract, preferred_element_type=jnp.float32)]
    ppermute x36 -> x33, waiting for transfers between devices: 90.1 us -> 78.2 us  [flip(): return lax.ppermute(value, axis, [(i, i ^ mask) for i in range(size)])]
    pallas_call x0 -> x4, Pallas kernels: none -> 11.8 us  [the longest x3 9.02 us: pick_columns(): pl.pallas_call(column_kernel, grid_spec=pltpu.PrefetchScalarGridSpec(num_...]
  transfers between devices with their start and end apart: 55 -> 53, of which waited for: 24 -> 22; matrix products, arithmetic and copies ran while one was open for 24% -> 21% of each run, Pallas kernels for 0% -> 3%
where the time goes in v2:
time: 350 us; the launch traced here: 346 us
  waiting for transfers between devices  114 us (33%)
  matrix products  89.4 us (26%)
  starting transfers between devices  64.4 us (18%)
  other arithmetic  46.3 us (13%)
  local copies, waits for them, and re-layouts  17.8 us (5%)
  Pallas kernels  11.8 us (3%)
    ppermute x33, waiting for transfers between devices, flip(): return lax.ppermute(value, axis, [(i, i ^ mask) for i in range(size)])  78.2 us
    dot_general x3, matrix products, per_device(): lax.dot_general(left, right, contract, preferred_element_type=jnp.float32)  43.3 us
    ppermute x33, starting transfers between devices, flip(): return lax.ppermute(value, axis, [(i, i ^ mask) for i in range(size)])  35.6 us
    ppermute x14, waiting for transfers between devices, shift(): lax.ppermute(value, axis, [(i, (i + step) % size) for i in range(size)])  33.9 us
    dot_general x1, matrix products, per_device(): jnp.dot(tokens_in, live.pop('gate_up'), preferred_element_type=jnp.float32)  20 us
    ppermute x14, starting transfers between devices, shift(): lax.ppermute(value, axis, [(i, (i + step) % size) for i in range(size)])  17.4 us
    concatenate x1, other arithmetic, per_device(): jnp.concatenate([gate_weight[0], pad, up_weight[0]], axis=1)  16 us
    dot_general x8, matrix products, per_device(): jnp.dot(ctx, live[f'weight{t}'], preferred_element_type=jnp.float32)  13.2 us
  transfers between devices with their start and end apart: 53, of which 22 were waited for; matrix products, arithmetic and copies ran while one was open for 21% of the time, Pallas kernels for 3%

profile of v2, /device:TPU:0, one launch (start us, length us, event | category | flops | bytes accessed | tf_op | source)
XLA Modules:
  0.0 346.0 jit_solution(7489305858127329835)
XLA Ops:
  1.9 3.0 collective-permute-start
  5.0 4.6 %collective-permute-start.2 = (bf16[128,2048]{1,0:T(8,128)(2,1)}, bf16[128,2048]{1,0:T(8,128)(2,1)S(1)}, u32[]{:S(2)}, u32[]{:S(2)}) collective-permute-start(bf16[128,2048]{1,0:T(8,128)(2,1)} %param.11), channel_id=1, source_target_pairs={{0,8},{8,16},{16,24},{1,9},{9,17},{17,25},{2,10},{10,18},{18,26},{... | collective-permute-start | bytes 1572872 | tf_op jit(solution)/shard_map/ppermute | solution.py:254
  23.7 2.5 broadcast_select_fusion
  26.2 11.5 %collective-permute-done.4 = bf16[128,2048]{1,0:T(8,128)(2,1)S(1)} collective-permute-done((bf16[128,2048]{1,0:T(8,128)(2,1)S(1)}, bf16[128,2048]{1,0:T(8,128)(2,1)S(1)}, u32[]{:S(2)}, u32[]{:S(2)}) %collective-permute-start.4) | collective-permute-done | bytes 524320 | tf_op jit(solution)/shard_map/ppermute | solution.py:27
  47.0 3.3 shard_map.130
  51.9 8.6 %collective-permute-done.8 = bf16[128,2048]{1,0:T(8,128)(2,1)} collective-permute-done((bf16[128,2048]{1,0:T(8,128)(2,1)S(1)}, bf16[128,2048]{1,0:T(8,128)(2,1)}, u32[]{:S(2)}, u32[]{:S(2)}) %collective-permute-start.8) | collective-permute-done | bytes 524320 | tf_op jit(solution)/shard_map/ppermute | solution.py:27
  63.4 7.1 %collective-permute-start.12 = (bf16[80,2048]{1,0:T(8,128)(2,1)S(1)}, bf16[80,2048]{1,0:T(8,128)(2,1)S(1)}, u32[]{:S(2)}, u32[]{:S(2)}) collective-permute-start(bf16[80,2048]{1,0:T(8,128)(2,1)S(1)} %get-tuple-element.166), channel_id=1, source_target_pairs={{0,8},{8,0},{16,24},{24,16},{1,9},{9,1},{17,25},{25,17},{2,10},{10... | collective-permute-start | bytes 983048 | tf_op jit(solution)/shard_map/ppermute | solution.py:27
  77.6 10.3 %collective-permute-done.15 = bf16[128,2048]{1,0:T(8,128)(2,1)S(1)} collective-permute-done((bf16[128,2048]{1,0:T(8,128)(2,1)S(1)}, bf16[128,2048]{1,0:T(8,128)(2,1)S(1)}, u32[]{:S(2)}, u32[]{:S(2)}) %collective-permute-start.15) | collective-permute-done | bytes 524320 | tf_op jit(solution)/shard_map/ppermute | solution.py:27
  88.4 2.5 collective-permute-start.17
  98.1 2.5 shard_map.131
  100.6 3.2 shard_map.132
  103.9 4.2 %collective-permute-done.20 = bf16[512,512]{1,0:T(8,128)(2,1)} collective-permute-done((bf16[512,512]{1,0:T(8,128)(2,1)}, bf16[512,512]{1,0:T(8,128)(2,1)}, u32[]{:S(2)}, u32[]{:S(2)}) %collective-permute-start.20) | collective-permute-done | bytes 524320 | tf_op jit(solution)/shard_map/ppermute | solution.py:22
  108.1 2.8 collective-permute-done.21
  110.9 3.1 collective-permute-done.18
  124.0 6.6 %collective-permute-done.24 = bf16[512,512]{1,0:T(8,128)(2,1)S(1)} collective-permute-done((bf16[512,512]{1,0:T(8,128)(2,1)S(1)}, bf16[512,512]{1,0:T(8,128)(2,1)S(1)}, u32[]{:S(2)}, u32[]{:S(2)}) %collective-permute-start.24) | collective-permute-done | bytes 524320 | tf_op jit(solution)/shard_map/ppermute | solution.py:22
  130.6 11.6 %collective-permute-done.25 = bf16[512,512]{1,0:T(8,128)(2,1)S(1)} collective-permute-done((bf16[512,512]{1,0:T(8,128)(2,1)S(1)}, bf16[512,512]{1,0:T(8,128)(2,1)S(1)}, u32[]{:S(2)}, u32[]{:S(2)}) %collective-permute-start.25) | collective-permute-done | bytes 524320 | tf_op jit(solution)/shard_map/ppermute | solution.py:27
  145.6 16.0 %pad_maximum_fusion = bf16[4096,1456]{0,1:T(8,128)(2,1)} fusion(bf16[4096,688]{0,1:T(8,128)(2,1)S(1)} %bitcast.99, bf16[4096,688]{0,1:T(8,128)(2,1)S(1)} %bitcast.102, bf16[1456]{0:T(1024)(128)(2,1)S(1)} %copy-done.17), kind=kLoop, calls=%fused_computation | loop fusion | flops 35782656 | bytes 23202656 | tf_op jit(solution)/shard_map/concatenate | solution.py:286
  163.5 3.9 %collective-permute-done.26 = bf16[240,2048]{1,0:T(8,128)(2,1)S(1)} collective-permute-done((bf16[240,2048]{1,0:T(8,128)(2,1)S(1)}, bf16[240,2048]{1,0:T(8,128)(2,1)S(1)}, u32[]{:S(2)}, u32[]{:S(2)}) %collective-permute-start.26) | collective-permute-done | bytes 983072 | tf_op jit(solution)/shard_map/ppermute | solution.py:22
  169.2 7.0 %collective-permute-done.28 = bf16[512,512]{1,0:T(8,128)(2,1)S(1)} collective-permute-done((bf16[512,512]{1,0:T(8,128)(2,1)S(1)}, bf16[512,512]{1,0:T(8,128)(2,1)S(1)}, u32[]{:S(2)}, u32[]{:S(2)}) %collective-permute-start.28) | collective-permute-done | bytes 524320 | tf_op jit(solution)/shard_map/ppermute | solution.py:27
  182.3 3.4 collective-permute-done.30
  197.9 8.9 %collective-permute-start.36 = (bf16[80,2048]{1,0:T(8,128)(2,1)S(1)}, bf16[80,2048]{1,0:T(8,128)(2,1)S(1)}, u32[]{:S(2)}, u32[]{:S(2)}) collective-permute-start(bf16[80,2048]{1,0:T(8,128)(2,1)S(1)} %get-tuple-element.293), channel_id=1, source_target_pairs={{0,16},{8,24},{16,0},{24,8},{1,17},{9,25},{17,1},{25,9},{2,18},{10... | collective-permute-start | bytes 983048 | tf_op jit(solution)/shard_map/ppermute | solution.py:27
  208.7 13.3 %collective-permute-done.36 = bf16[80,2048]{1,0:T(8,128)(2,1)S(1)} collective-permute-done((bf16[80,2048]{1,0:T(8,128)(2,1)S(1)}, bf16[80,2048]{1,0:T(8,128)(2,1)S(1)}, u32[]{:S(2)}, u32[]{:S(2)}) %collective-permute-start.36) | collective-permute-done | bytes 327712 | tf_op jit(solution)/shard_map/ppermute | solution.py:27
  227.7 2.7 shard_map.133
  230.5 11.5 %collective-permute-done.40 = bf16[40,2048]{1,0:T(8,128)(2,1)S(1)} collective-permute-done((bf16[40,2048]{1,0:T(8,128)(2,1)S(1)}, bf16[40,2048]{1,0:T(8,128)(2,1)S(1)}, u32[]{:S(2)}, u32[]{:S(2)}) %collective-permute-start.40) | collective-permute-done | bytes 163872 | tf_op jit(solution)/shard_map/ppermute | solution.py:22
  246.3 10.8 %fusion.3 = f32[1280,688]{0,1:T(8,128)} fusion(bf16[1280,4096]{1,0:T(8,128)(2,1)S(1)} %shard_map.133, bf16[1,688,4096]{2,1,0:T(8,128)(2,1)} %param.17), kind=kOutput, calls=%fused_computation.8 | convolution fusion | flops 7214202880 | bytes 19644416 | tf_op jit(solution)/shard_map/dot_general | solution.py:356
  263.5 2.4 collective-permute-done.50
  267.3 3.2 pad_maximum_fusion.2
  270.5 3.4 collective-permute-done.52
  282.5 20.0 %fusion.21 = f32[1280,1456]{0,1:T(8,128)} fusion(bf16[4096,1456]{0,1:T(8,128)(2,1)S(1)} %bitcast.96, bf16[320,4096]{1,0:T(8,128)(2,1)} %copy-done.15, bf16[640,4096]{1,0:T(8,128)(2,1)S(1)} %slice_dynamic-update-slice_fusion, bf16[320,4096]{1,0:T(8,128)(2,1)S(1)} %slice_dynamic-update-slice_fusion.16), kind=kOutput, calls=%fused_computation.151 | convolution fusion | flops 15298723840 | bytes 29868032 | tf_op jit(solution)/shard_map/dot_general | solution.py:362
  302.5 16.1 %fusion.1 = bf16[1,4096,688]{1,2,0:T(8,128)(2,1)} fusion(f32[1280,688]{0,1:T(8,128)} %fusion.3, f32[1280,1456]{0,1:T(8,128)} %fusion.21, bf16[320,4096]{1,0:T(8,128)(2,1)} %copy-done.15, bf16[640,4096]{1,0:T(8,128)(2,1)S(1)} %slice_dynamic-update-slice_fusion, bf16[320,4096]{1,0:T(8,128)(2,1)} %copy-done.14), kind=kOutput, calls=%fused_computation.6 | convolution fusion | flops 7257284608 | bytes 26689536 | tf_op jit(solution)/shard_map/dot_general | solution.py:372
  318.6 13.2 %fusion.2 = bf16[1,4096,688]{1,2,0:T(8,128)(2,1)} fusion(f32[1280,688]{0,1:T(8,128)} %fusion.3, f32[1280,1456]{0,1:T(8,128)} %fusion.21, bf16[320,4096]{1,0:T(8,128)(2,1)} %copy-done.15, bf16[640,4096]{1,0:T(8,128)(2,1)S(1)} %slice_dynamic-update-slice_fusion, bf16[320,4096]{1,0:T(8,128)(2,1)} %copy-done.14), kind=kOutput, calls=%fused_computation.7 | convolution fusion | flops 7253762048 | bytes 23166976 | tf_op jit(solution)/shard_map/dot_general | solution.py:372
  331.8 14.0 %fusion = bf16[1,688,4096]{2,1,0:T(8,128)(2,1)} fusion(bf16[1280,4096]{1,0:T(8,128)(2,1)} %copy-done, f32[1280,1456]{0,1:T(8,128)} %fusion.21), kind=kOutput, calls=%fused_computation.5 | convolution fusion | flops 7222304768 | bytes 23166976 | tf_op jit(solution)/shard_map/dot_general | solution.py:372
  (271 shorter events, 106.6 us)
Async XLA Ops:
  0.6 17.6 %collective-permute-start.1 = (bf16[128,2048]{1,0:T(8,128)(2,1)}, bf16[128,2048]{1,0:T(8,128)(2,1)S(1)}, u32[]{:S(2)}, u32[]{:S(2)}) collective-permute-start(bf16[128,2048]{1,0:T(8,128)(2,1)} %param.11), channel_id=1, source_target_pairs={{8,0},{16,8},{24,16},{9,1},{17,9},{25,17},{10,2},{18,10},{26,18},{... | collective-permute-start | bytes 1572872 | tf_op jit(solution)/shard_map/ppermute | solution.py:255
  1.9 15.2 %collective-permute-start = (bf16[128,2048]{1,0:T(8,128)(2,1)}, bf16[128,2048]{1,0:T(8,128)(2,1)S(1)}, u32[]{:S(2)}, u32[]{:S(2)}) collective-permute-start(bf16[128,2048]{1,0:T(8,128)(2,1)} %param.11), channel_id=1, source_target_pairs={{0,2},{1,3},{2,0},{3,1},{4,6},{5,7},{6,4},{7,5},{8,10},{9,11},{10,... | collective-permute-start | bytes 1572872 | tf_op jit(solution)/shard_map/ppermute | solution.py:27
  5.0 15.5 %collective-permute-start.2 = (bf16[128,2048]{1,0:T(8,128)(2,1)}, bf16[128,2048]{1,0:T(8,128)(2,1)S(1)}, u32[]{:S(2)}, u32[]{:S(2)}) collective-permute-start(bf16[128,2048]{1,0:T(8,128)(2,1)} %param.11), channel_id=1, source_target_pairs={{0,8},{8,16},{16,24},{1,9},{9,17},{17,25},{2,10},{10,18},{18,26},{... | collective-permute-start | bytes 1572872 | tf_op jit(solution)/shard_map/ppermute | solution.py:254
  20.4 17.5 %collective-permute-start.5 = (bf16[128,2048]{1,0:T(8,128)(2,1)S(1)}, bf16[128,2048]{1,0:T(8,128)(2,1)S(1)}, u32[]{:S(2)}, u32[]{:S(2)}) collective-permute-start(bf16[128,2048]{1,0:T(8,128)(2,1)S(1)} %collective-permute-done.1), channel_id=1, source_target_pairs={{8,0},{16,8},{9,1},{17,9},{10,2},{18,10},{11,3},{19,11},{12,4},{20... | collective-permute-start | bytes 1572872 | tf_op jit(solution)/shard_map/ppermute | solution.py:255
  21.7 16.2 %collective-permute-start.6 = (bf16[128,2048]{1,0:T(8,128)(2,1)S(1)}, bf16[128,2048]{1,0:T(8,128)(2,1)}, u32[]{:S(2)}, u32[]{:S(2)}) collective-permute-start(bf16[128,2048]{1,0:T(8,128)(2,1)S(1)} %collective-permute-done.2), channel_id=1, source_target_pairs={{8,16},{16,24},{9,17},{17,25},{10,18},{18,26},{11,19},{19,27},{12,... | collective-permute-start | bytes 1572872 | tf_op jit(solution)/shard_map/ppermute | solution.py:254
  37.9 25.4 %collective-permute-start.9 = (bf16[128,2048]{1,0:T(8,128)(2,1)S(1)}, bf16[128,2048]{1,0:T(8,128)(2,1)}, u32[]{:S(2)}, u32[]{:S(2)}) collective-permute-start(bf16[128,2048]{1,0:T(8,128)(2,1)S(1)} %collective-permute-done.5), channel_id=1, source_target_pairs={{8,0},{9,1},{10,2},{11,3},{12,4},{13,5},{14,6},{15,7}} | collective-permute-start | bytes 1572872 | tf_op jit(solution)/shard_map/ppermute | solution.py:255
  39.2 24.2 %collective-permute-start.11 = (bf16[128,2048]{1,0:T(8,128)(2,1)}, bf16[128,2048]{1,0:T(8,128)(2,1)}, u32[]{:S(2)}, u32[]{:S(2)}) collective-permute-start(bf16[128,2048]{1,0:T(8,128)(2,1)} %collective-permute-done.6), channel_id=1, source_target_pairs={{16,24},{17,25},{18,26},{19,27},{20,28},{21,29},{22,30},{23,31}} | collective-permute-start | bytes 1572872 | tf_op jit(solution)/shard_map/ppermute | solution.py:254
  40.8 21.0 %collective-permute-start.7 = (bf16[256,2048]{1,0:T(8,128)(2,1)S(1)}, bf16[256,2048]{1,0:T(8,128)(2,1)}, u32[]{:S(2)}, u32[]{:S(2)}) collective-permute-start(bf16[256,2048]{1,0:T(8,128)(2,1)S(1)} %pad_maximum_fusion.14), channel_id=1, source_target_pairs={{0,1},{1,0},{2,3},{3,2},{4,5},{5,4},{6,7},{7,6},{8,9},{9,8},{10,11... | collective-permute-start | bytes 3145736 | tf_op jit(solution)/shard_map/ppermute | solution.py:27
  44.9 18.4 %collective-permute-start.10 = (bf16[512,512]{1,0:T(8,128)(2,1)}, bf16[512,512]{1,0:T(8,128)(2,1)}, u32[]{:S(2)}, u32[]{:S(2)}) collective-permute-start(bf16[512,512]{1,0:T(8,128)(2,1)} %convolution_convert_fusion.10), channel_id=1, source_target_pairs={{0,4},{4,0},{1,5},{5,1},{2,6},{6,2},{3,7},{7,3},{8,12},{12,8},{9,1... | collective-permute-start | bytes 1572872 | tf_op jit(solution)/shard_map/ppermute | solution.py:22
  63.4 24.9 %collective-permute-start.12 = (bf16[80,2048]{1,0:T(8,128)(2,1)S(1)}, bf16[80,2048]{1,0:T(8,128)(2,1)S(1)}, u32[]{:S(2)}, u32[]{:S(2)}) collective-permute-start(bf16[80,2048]{1,0:T(8,128)(2,1)S(1)} %get-tuple-element.166), channel_id=1, source_target_pairs={{0,8},{8,0},{16,24},{24,16},{1,9},{9,1},{17,25},{25,17},{2,10},{10... | collective-permute-start | bytes 983048 | tf_op jit(solution)/shard_map/ppermute | solution.py:27
  70.5 17.8 %collective-permute-start.13 = (bf16[80,2048]{1,0:T(8,128)(2,1)S(1)}, bf16[80,2048]{1,0:T(8,128)(2,1)S(1)}, u32[]{:S(2)}, u32[]{:S(2)}) collective-permute-start(bf16[80,2048]{1,0:T(8,128)(2,1)S(1)} %get-tuple-element.167), channel_id=1, source_target_pairs={{0,16},{8,24},{16,0},{24,8},{1,17},{9,25},{17,1},{25,9},{2,18},{10... | collective-permute-start | bytes 983048 | tf_op jit(solution)/shard_map/ppermute | solution.py:27
  71.8 16.5 %collective-permute-start.16 = (bf16[512,512]{1,0:T(8,128)(2,1)S(1)}, bf16[512,512]{1,0:T(8,128)(2,1)S(1)}, u32[]{:S(2)}, u32[]{:S(2)}) collective-permute-start(bf16[512,512]{1,0:T(8,128)(2,1)S(1)} %convolution_convert_fusion.8), channel_id=1, source_target_pairs={{0,4},{4,0},{1,5},{5,1},{2,6},{6,2},{3,7},{7,3},{8,12},{12,8},{9,1... | collective-permute-start | bytes 1572872 | tf_op jit(solution)/shard_map/ppermute | solution.py:22
  72.4 15.7 %collective-permute-start.14 = (bf16[256,2048]{1,0:T(8,128)(2,1)S(1)}, bf16[256,2048]{1,0:T(8,128)(2,1)S(1)}, u32[]{:S(2)}, u32[]{:S(2)}) collective-permute-start(bf16[256,2048]{1,0:T(8,128)(2,1)S(1)} %pad_maximum_fusion.15), channel_id=1, source_target_pairs={{0,1},{1,0},{2,3},{3,2},{4,5},{5,4},{6,7},{7,6},{8,9},{9,8},{10,11... | collective-permute-start | bytes 3145736 | tf_op jit(solution)/shard_map/ppermute | solution.py:27
  88.4 15.6 %collective-permute-start.17 = (bf16[80,2048]{1,0:T(8,128)(2,1)S(1)}, bf16[80,2048]{1,0:T(8,128)(2,1)}, u32[]{:S(2)}, u32[]{:S(2)}) collective-permute-start(bf16[80,2048]{1,0:T(8,128)(2,1)S(1)} %get-tuple-element.182), channel_id=1, source_target_pairs={{0,24},{8,16},{16,8},{24,0},{1,25},{9,17},{17,9},{25,1},{2,26},{10... | collective-permute-start | bytes 983048 | tf_op jit(solution)/shard_map/ppermute | solution.py:27
  90.9 23.1 %collective-permute-start.18 = (bf16[240,2048]{1,0:T(8,128)(2,1)S(1)}, bf16[240,2048]{1,0:T(8,128)(2,1)}, u32[]{:S(2)}, u32[]{:S(2)}) collective-permute-start(bf16[240,2048]{1,0:T(8,128)(2,1)S(1)} %constant_dynamic-update-slice_fusion), channel_id=1, source_target_pairs={{0,2},{1,3},{2,0},{3,1},{4,6},{5,7},{6,4},{7,5},{8,10},{9,11},{10,... | collective-permute-start | bytes 2949128 | tf_op jit(solution)/shard_map/ppermute | solution.py:27
  115.6 14.9 %collective-permute-start.24 = (bf16[512,512]{1,0:T(8,128)(2,1)S(1)}, bf16[512,512]{1,0:T(8,128)(2,1)S(1)}, u32[]{:S(2)}, u32[]{:S(2)}) collective-permute-start(bf16[512,512]{1,0:T(8,128)(2,1)S(1)} %convolution_convert_fusion.4), channel_id=1, source_target_pairs={{0,4},{4,0},{1,5},{5,1},{2,6},{6,2},{3,7},{7,3},{8,12},{12,8},{9,1... | collective-permute-start | bytes 1572872 | tf_op jit(solution)/shard_map/ppermute | solution.py:22
  118.8 23.4 %collective-permute-start.25 = (bf16[512,512]{1,0:T(8,128)(2,1)S(1)}, bf16[512,512]{1,0:T(8,128)(2,1)S(1)}, u32[]{:S(2)}, u32[]{:S(2)}) collective-permute-start(bf16[512,512]{1,0:T(8,128)(2,1)S(1)} %add_convert_fusion.1), channel_id=1, source_target_pairs={{0,16},{8,24},{16,0},{24,8},{1,17},{9,25},{17,1},{25,9},{2,18},{10... | collective-permute-start | bytes 1572872 | tf_op jit(solution)/shard_map/ppermute | solution.py:27
  118.9 23.3 %collective-permute-start.23 = (bf16[160,2048]{1,0:T(8,128)(2,1)S(1)}, bf16[160,2048]{1,0:T(8,128)(2,1)S(1)}, u32[]{:S(2)}, u32[]{:S(2)}) collective-permute-start(bf16[160,2048]{1,0:T(8,128)(2,1)S(1)} %slice.220), channel_id=1, source_target_pairs={{0,4},{4,0},{1,5},{5,1},{2,6},{6,2},{3,7},{7,3},{8,12},{12,8},{9,1... | collective-permute-start | bytes 1966088 | tf_op jit(solution)/shard_map/ppermute | solution.py:22
  142.3 25.2 %collective-permute-start.27 = (bf16[160,2048]{1,0:T(8,128)(2,1)S(1)}, bf16[160,2048]{1,0:T(8,128)(2,1)S(1)}, u32[]{:S(2)}, u32[]{:S(2)}) collective-permute-start(bf16[160,2048]{1,0:T(8,128)(2,1)S(1)} %collective-permute-done.23), channel_id=1, source_target_pairs={{0,2},{1,3},{2,0},{3,1},{4,6},{5,7},{6,4},{7,5},{8,10},{9,11},{10,... | collective-permute-start | bytes 1966088 | tf_op jit(solution)/shard_map/ppermute | solution.py:27
  144.0 23.5 %collective-permute-start.26 = (bf16[240,2048]{1,0:T(8,128)(2,1)S(1)}, bf16[240,2048]{1,0:T(8,128)(2,1)S(1)}, u32[]{:S(2)}, u32[]{:S(2)}) collective-permute-start(bf16[240,2048]{1,0:T(8,128)(2,1)S(1)} %pad_maximum_fusion.17), channel_id=1, source_target_pairs={{0,4},{4,0},{1,5},{5,1},{2,6},{6,2},{3,7},{7,3},{8,12},{12,8},{9,1... | collective-permute-start | bytes 2949128 | tf_op jit(solution)/shard_map/ppermute | solution.py:22
  196.8 25.3 %collective-permute-start.34 = (bf16[1280,2048]{1,0:T(8,128)(2,1)S(1)}, bf16[1280,2048]{1,0:T(8,128)(2,1)S(1)}, u32[]{:S(2)}, u32[]{:S(2)}) collective-permute-start(bf16[1280,2048]{1,0:T(8,128)(2,1)S(1)} %constant_dynamic-update-slice_fusion.3), channel_id=1, source_target_pairs={{0,1},{1,0},{2,3},{3,2},{4,5},{5,4},{6,7},{7,6},{8,9},{9,8},{10,11... | collective-permute-start | bytes 15728648 | tf_op jit(solution)/shard_map/ppermute | solution.py:27
  197.9 24.1 %collective-permute-start.36 = (bf16[80,2048]{1,0:T(8,128)(2,1)S(1)}, bf16[80,2048]{1,0:T(8,128)(2,1)S(1)}, u32[]{:S(2)}, u32[]{:S(2)}) collective-permute-start(bf16[80,2048]{1,0:T(8,128)(2,1)S(1)} %get-tuple-element.293), channel_id=1, source_target_pairs={{0,16},{8,24},{16,0},{24,8},{1,17},{9,25},{17,1},{25,9},{2,18},{10... | collective-permute-start | bytes 983048 | tf_op jit(solution)/shard_map/ppermute | solution.py:27
  206.8 15.3 %collective-permute-start.35 = (bf16[80,2048]{1,0:T(8,128)(2,1)S(1)}, bf16[80,2048]{1,0:T(8,128)(2,1)S(1)}, u32[]{:S(2)}, u32[]{:S(2)}) collective-permute-start(bf16[80,2048]{1,0:T(8,128)(2,1)S(1)} %get-tuple-element.294), channel_id=1, source_target_pairs={{0,8},{8,0},{16,24},{24,16},{1,9},{9,1},{17,25},{25,17},{2,10},{10... | collective-permute-start | bytes 983048 | tf_op jit(solution)/shard_map/ppermute | solution.py:27
  206.8 15.3 %collective-permute-start.38 = (bf16[80,2048]{1,0:T(8,128)(2,1)S(1)}, bf16[80,2048]{1,0:T(8,128)(2,1)S(1)}, u32[]{:S(2)}, u32[]{:S(2)}) collective-permute-start(bf16[80,2048]{1,0:T(8,128)(2,1)S(1)} %get-tuple-element.251), channel_id=1, source_target_pairs={{0,2},{1,3},{2,0},{3,1},{4,6},{5,7},{6,4},{7,5},{8,10},{9,11},{10,... | collective-permute-start | bytes 983048 | tf_op jit(solution)/shard_map/ppermute | solution.py:27
  207.1 15.0 %collective-permute-start.37 = (bf16[80,2048]{1,0:T(8,128)(2,1)S(1)}, bf16[80,2048]{1,0:T(8,128)(2,1)S(1)}, u32[]{:S(2)}, u32[]{:S(2)}) collective-permute-start(bf16[80,2048]{1,0:T(8,128)(2,1)S(1)} %get-tuple-element.251), channel_id=1, source_target_pairs={{0,4},{4,0},{1,5},{5,1},{2,6},{6,2},{3,7},{7,3},{8,12},{12,8},{9,1... | collective-permute-start | bytes 983048 | tf_op jit(solution)/shard_map/ppermute | solution.py:22
  222.2 19.9 %collective-permute-start.43 = (bf16[160,2048]{1,0:T(8,128)(2,1)S(1)}, bf16[160,2048]{1,0:T(8,128)(2,1)S(1)}, u32[]{:S(2)}, u32[]{:S(2)}) collective-permute-start(bf16[160,2048]{1,0:T(8,128)(2,1)S(1)} %constant_dynamic-update-slice_fusion.11), channel_id=1, source_target_pairs={{0,2},{1,3},{2,0},{3,1},{4,6},{5,7},{6,4},{7,5},{8,10},{9,11},{10,... | collective-permute-start | bytes 1966088 | tf_op jit(solution)/shard_map/ppermute | solution.py:27
  222.4 19.7 %collective-permute-start.42 = (bf16[160,2048]{1,0:T(8,128)(2,1)S(1)}, bf16[160,2048]{1,0:T(8,128)(2,1)S(1)}, u32[]{:S(2)}, u32[]{:S(2)}) collective-permute-start(bf16[160,2048]{1,0:T(8,128)(2,1)S(1)} %constant_dynamic-update-slice_fusion.11), channel_id=1, source_target_pairs={{0,4},{4,0},{1,5},{5,1},{2,6},{6,2},{3,7},{7,3},{8,12},{12,8},{9,1... | collective-permute-start | bytes 1966088 | tf_op jit(solution)/shard_map/ppermute | solution.py:22
  223.9 18.1 %collective-permute-start.41 = (bf16[40,2048]{1,0:T(8,128)(2,1)S(1)}, bf16[40,2048]{1,0:T(8,128)(2,1)S(1)}, u32[]{:S(2)}, u32[]{:S(2)}) collective-permute-start(bf16[40,2048]{1,0:T(8,128)(2,1)S(1)} %slice.235), channel_id=1, source_target_pairs={{0,2},{1,3},{2,0},{3,1},{4,6},{5,7},{6,4},{7,5},{8,10},{9,11},{10,... | collective-permute-start | bytes 491528 | tf_op jit(solution)/shard_map/ppermute | solution.py:27
  225.5 16.5 %collective-permute-start.40 = (bf16[40,2048]{1,0:T(8,128)(2,1)S(1)}, bf16[40,2048]{1,0:T(8,128)(2,1)S(1)}, u32[]{:S(2)}, u32[]{:S(2)}) collective-permute-start(bf16[40,2048]{1,0:T(8,128)(2,1)S(1)} %slice.234), channel_id=1, source_target_pairs={{0,4},{4,0},{1,5},{5,1},{2,6},{6,2},{3,7},{7,3},{8,12},{12,8},{9,1... | collective-permute-start | bytes 491528 | tf_op jit(solution)/shard_map/ppermute | solution.py:22
  226.4 15.7 %collective-permute-start.39 = (bf16[80,2048]{1,0:T(8,128)(2,1)S(1)}, bf16[80,2048]{1,0:T(8,128)(2,1)S(1)}, u32[]{:S(2)}, u32[]{:S(2)}) collective-permute-start(bf16[80,2048]{1,0:T(8,128)(2,1)S(1)} %get-tuple-element.250), channel_id=1, source_target_pairs={{0,24},{8,16},{16,8},{24,0},{1,25},{9,17},{17,9},{25,1},{2,26},{10... | collective-permute-start | bytes 983048 | tf_op jit(solution)/shard_map/ppermute | solution.py:27
  242.1 16.7 %collective-permute-start.48 = (bf16[80,2048]{1,0:T(8,128)(2,1)S(1)}, bf16[80,2048]{1,0:T(8,128)(2,1)S(1)}, u32[]{:S(2)}, u32[]{:S(2)}) collective-permute-start(bf16[80,2048]{1,0:T(8,128)(2,1)S(1)} %collective-permute-done.39), channel_id=1, source_target_pairs={{0,2},{1,3},{2,0},{3,1},{4,6},{5,7},{6,4},{7,5},{8,10},{9,11},{10,... | collective-permute-start | bytes 983048 | tf_op jit(solution)/shard_map/ppermute | solution.py:27
  243.8 15.0 %collective-permute-start.47 = (bf16[80,2048]{1,0:T(8,128)(2,1)S(1)}, bf16[80,2048]{1,0:T(8,128)(2,1)S(1)}, u32[]{:S(2)}, u32[]{:S(2)}) collective-permute-start(bf16[80,2048]{1,0:T(8,128)(2,1)S(1)} %collective-permute-done.39), channel_id=1, source_target_pairs={{0,4},{4,0},{1,5},{5,1},{2,6},{6,2},{3,7},{7,3},{8,12},{12,8},{9,1... | collective-permute-start | bytes 983048 | tf_op jit(solution)/shard_map/ppermute | solution.py:22
  (48 other events, 508.4 us)

commit v3 on v2

--- a/solution.py
+++ b/solution.py
@@ -90,15 +90,22 @@
                     out_ref[:, first : first + piece] = refs[c][step, 0, 0, :, k * piece : (k + 1) * piece]
 
 
-def order_rows(values, groups, n_dp, piece):
-    n_mp, x = values[0].shape[0], lax.axis_index("mp")
-    sources, part = len(values), n_dp // len(values)
-    slots = sum(len(g) for g in groups)
-    rows = values[0].shape[1] // (part * slots)
-    places = [(j // part, j % part, m) for g in groups for j in range(n_dp) for m in g]
+def order_rows(sources, groups, n_dp, piece):
+    values, where = [], {}
+    for slots, parts in sources:
+        share = n_dp // len(parts)
+        for c, value in enumerate(parts):
+            for j in range(share):
+                for i, m in enumerate(slots):
+                    where[c * share + j, m] = (len(values), j, i)
+            n_mp, columns = value.shape[0], value.shape[2]
+            values.append(value.reshape(n_mp, share, len(slots), -1, columns))
+    rows = values[0].shape[3]
+    x = lax.axis_index("mp")
+    places = [where[j, m] for g in groups for j in range(n_dp) for m in g]
     count = len(places)
     columns = [[c for c, _, _ in places]]
-    for c in range(sources):
+    for c in range(len(values)):
         held = next((j, m) for i, j, m in places if i == c)
         kept = []
         for i, j, m in places:
@@ -115,29 +122,73 @@
         )
 
     return pl.pallas_call(
-        functools.partial(order_kernel, n_mp, n_dp, piece, sources),
+        functools.partial(order_kernel, n_mp, n_dp, piece, len(values)),
         grid_spec=pltpu.PrefetchScalarGridSpec(
             num_scalar_prefetch=1,
             grid=(count,),
-            in_specs=[spec(c) for c in range(sources)],
+            in_specs=[spec(c) for c in range(len(values))],
             out_specs=pl.BlockSpec((rows, n_mp * n_dp * piece), lambda i, at: (i, 0)),
         ),
         out_shape=jax.ShapeDtypeStruct((count * rows, n_mp * n_dp * piece), values[0].dtype),
-        compiler_params=pltpu.CompilerParams(vmem_limit_bytes=32 << 20),
-    )(table, *[v.reshape(n_mp, part, slots, rows, n_dp * piece) for v in values])
-
-
-def whole_columns(across, piece):
-    n_mp, n_dp, x = lax.axis_size("mp"), lax.axis_size("dp"), lax.axis_index("mp")
-    parts = []
-    for p in range(n_mp):
-        value = across[0]
-        for s in range(1, n_mp):
-            value = jnp.where((x - s) % n_mp == p, across[s], value)
-        parts.append(value)
-    return jnp.concatenate(
-        [part[:, k * piece : (k + 1) * piece] for k in range(n_dp) for part in parts], axis=1
-    )
+        compiler_params=pltpu.CompilerParams(vmem_limit_bytes=40 << 20),
+    )(table, *values)
+
+
+def forward_kernel(rows_ref, gate_ref, up_ref, back_ref, hidden_ref, d_gate_ref, d_up_ref):
+    contract = (((1,), (1,)), ((), ()))
+    rows = rows_ref[...]
+    pre_gate = lax.dot_general(gate_ref[...], rows, contract, preferred_element_type=jnp.float32)
+    pre_up = lax.dot_general(up_ref[...], rows, contract, preferred_element_type=jnp.float32)
+    back = back_ref[...]
+    sigmoid_gate = jax.nn.sigmoid(pre_gate)
+    active = pre_gate * sigmoid_gate
+    hidden_ref[...] = (active * pre_up).astype(jnp.bfloat16)
+    d_gate = back * pre_up * sigmoid_gate * (1.0 + pre_gate * (1.0 - sigmoid_gate))
+    d_gate_ref[...] = d_gate.astype(jnp.bfloat16)
+    d_up_ref[...] = (back * active).astype(jnp.bfloat16)
+
+
+def fitting(size, most):
+    return next((t for t in range(most, 127, -128) if size % t == 0), size)
+
+
+def forward(rows, gate_t, up_t, back):
+    count, width = rows.shape
+    units = gate_t.shape[0]
+    tile = fitting(count, 256)
+    weights = pl.BlockSpec((units, width), lambda i: (0, 0))
+    part = pl.BlockSpec((units, tile), lambda i: (0, i))
+    return pl.pallas_call(
+        forward_kernel,
+        grid=(count // tile,),
+        in_specs=[pl.BlockSpec((tile, width), lambda i: (i, 0)), weights, weights, part],
+        out_specs=[part] * 3,
+        out_shape=[jax.ShapeDtypeStruct((units, count), jnp.bfloat16)] * 3,
+        compiler_params=pltpu.CompilerParams(vmem_limit_bytes=56 << 20),
+    )(rows, gate_t, up_t, back)
+
+
+def gradient_kernel(rows_ref, cot_ref, hidden_ref, d_gate_ref, d_up_ref, gate_ref, up_ref, down_ref):
+    rows = rows_ref[...]
+    pairs = ((d_gate_ref[...], rows, gate_ref), (d_up_ref[...], rows, up_ref), (hidden_ref[...], cot_ref[...], down_ref))
+    for left, right, out_ref in pairs:
+        out_ref[...] = jnp.dot(left, right, preferred_element_type=jnp.float32).astype(jnp.bfloat16)
+
+
+def gradients(rows, cot, hidden, d_gate, d_up):
+    count, width = rows.shape
+    units = hidden.shape[0]
+    tile = fitting(width, 512)
+    columns = pl.BlockSpec((count, tile), lambda i: (0, i))
+    held = pl.BlockSpec((units, count), lambda i: (0, 0))
+    return pl.pallas_call(
+        gradient_kernel,
+        grid=(width // tile,),
+        in_specs=[columns, columns, held, held, held],
+        out_specs=[pl.BlockSpec((units, tile), lambda i: (0, i))] * 3,
+        out_shape=[jax.ShapeDtypeStruct((units, width), jnp.bfloat16)] * 3,
+        compiler_params=pltpu.CompilerParams(vmem_limit_bytes=56 << 20),
+    )(rows, cot, hidden, d_gate, d_up)
 
 
 def per_device(
@@ -158,8 +209,6 @@
     experts = n_br * gate_weight.shape[0]
     capacity = 5 * tokens // (2 * experts)
     piece = width // (n_dp * n_mp)
-    hidden_width = gate_weight.shape[2]
-    padded_width = -(-hidden_width // 128) * 128
 
     def choose(options, index):
         value = options[0]
@@ -214,16 +263,17 @@
             parts += across[1:]
         live[f"{name}a{g}"] = jnp.concatenate(parts, axis=0)
 
+    def core_flips(block):
+        flips = [sum(v for i, v in enumerate(core_masks) if c >> i & 1) for c in range(1 << len(core_masks))]
+        return [flip(block, "dp", mask) if mask else block for mask in flips]
+
     def hop_rest(name, g):
-        block = live[f"{name}a{g}"]
-        block = block.reshape(n_mp, -1, block.shape[1])
-        for mask in core_masks:
-            block = jnp.concatenate([block, flip(block, "dp", mask)], axis=1)
-        live[f"{name}a{g}"] = block
-
-    def finish(name, g):
-        block = live.pop(f"{name}a{g}")
-        return whole_columns([block[t] for t in range(n_mp)], piece)
+        for c, block in enumerate(core_flips(live.pop(f"{name}a{g}"))):
+            live[f"{name}a{g}_{c}"] = block
+
+    def taken(name):
+        blocks = [live.pop(f"{name}_{c}") for c in range(1 << len(core_masks))]
+        return [v.reshape(n_mp, -1, v.shape[1]) for v in blocks]
 
     def cascade(name, at):
         for g in range(len(groups)):
@@ -281,9 +331,6 @@
             rows = (rows * live.pop("row_gate")).astype(jnp.bfloat16)
             for m in range(n_br):
                 live[f"cot{m}"] = rows[m * capacity : (m + 1) * capacity]
-        if r == n_br + 2:
-            pad = jnp.zeros((width, padded_width - hidden_width), gate_weight.dtype)
-            live["gate_up"] = jnp.concatenate([gate_weight[0], pad, up_weight[0]], axis=1)
         if r == n_br:
             live["residual"] = my_columns(live["residual"])
             live["gain"] = my_columns(live["gain"])
@@ -347,31 +394,21 @@
         cascade("in", r)
         if r == 0:
             live["cota0"] = jnp.concatenate([live.pop(f"cot_part{i}") for i in range(cot_parts)], axis=0)
-            for c in range(1, 1 << len(core_masks)):
-                live[f"cota{c}"] = flip(live["cota0"], "dp", sum(v for i, v in enumerate(core_masks) if c >> i & 1))
+            for c, block in enumerate(core_flips(live.pop("cota0"))):
+                live[f"cota_{c}"] = block
         if r == 1:
-            blocks = [live.pop(f"cota{c}") for c in range(1 << len(core_masks))]
-            live["cotan"] = order_rows([v.reshape(n_mp, -1, n_dp * piece) for v in blocks], groups, n_dp, piece)
+            live["cotan"] = order_rows([(list(range(n_br)), taken("cota"))], groups, n_dp, piece)
         if r == 2:
             live["back"] = lax.dot_general(
-                live["cotan"], down_weight[0], (((1,), (1,)), ((), ())), preferred_element_type=jnp.float32
+                down_weight[0], live["cotan"], (((1,), (1,)), ((), ())), preferred_element_type=jnp.float32
             )
         fence()
     cotan_rows, back_grad = live.pop("cotan"), live.pop("back")
-    tokens_in = jnp.concatenate([finish("in", g) for g in range(len(groups))], axis=0)
-    pre = jnp.dot(tokens_in, live.pop("gate_up"), preferred_element_type=jnp.float32)
-    pre_gate, pre_up = pre[:, :hidden_width], pre[:, padded_width:]
-    sigmoid_gate = jax.nn.sigmoid(pre_gate)
-    active = pre_gate * sigmoid_gate
-    hidden = (active * pre_up).astype(jnp.bfloat16)
-    d_gate = (back_grad * pre_up * sigmoid_gate * (1.0 + pre_gate * (1.0 - sigmoid_gate))).astype(jnp.bfloat16)
-    d_up = (back_grad * active).astype(jnp.bfloat16)
-    contract = (((0,), (0,)), ((), ()))
-    grads = []
-    for left, right in ((tokens_in, d_gate), (tokens_in, d_up), (hidden, cotan_rows)):
-        grad = lax.dot_general(left, right, contract, preferred_element_type=jnp.float32)
-        grads.append(grad.astype(jnp.bfloat16)[None])
-    return tuple(grads)
+    sources = [(slots_of, taken(f"ina{g}")) for g, slots_of in enumerate(groups)]
+    tokens_in = order_rows(sources, groups, n_dp, piece)
+    hidden, d_gate, d_up = forward(tokens_in, gate_weight[0].T, up_weight[0].T, back_grad)
+    grad_gate, grad_up, grad_down = gradients(tokens_in, cotan_rows, hidden, d_gate, d_up)
+    return (grad_gate.T[None], grad_up.T[None], grad_down[None])
 
 
 def solution(mesh):

time: 350 us -> 315 us (0.900)
  Pallas kernels: 11.8 us -> 77.1 us
  matrix products: 89.4 us -> 27.3 us
  other arithmetic: 46.3 us -> 23.1 us
  local copies, waits for them, and re-layouts: 17.8 us -> 7.23 us
  waiting for transfers between devices: 114 us -> 122 us
  starting transfers between devices: 64.4 us -> 56.6 us
    pallas_call x1 -> x4, Pallas kernels: 2.74 us -> 68 us  [the longest x1 27.6 us: gradients(): pl.pallas_call(gradient_kernel, grid=(width // tile,), in_specs=[columns,...]
    dot_general x5 -> x1, matrix products: 74.1 us -> 12 us  [per_device(): lax.dot_general(down_weight[0], live['cotan'], (((1,), (1,)), ((), ())),...]
    concatenate x4 -> x0, other arithmetic: 21.3 us -> none  [the longest x1 16 us: per_device(): jnp.concatenate([gate_weight[0], pad, up_weight[0]], axis=1)]
    ppermute x14, waiting for transfers between devices: 33.9 us -> 46 us  [shift(): lax.ppermute(value, axis, [(i, (i + step) % size) for i in range(size)])]
    unnamed x92 -> x51, local copies, waits for them, and re-layouts: 12 us -> 3.5 us
    ppermute x33, waiting for transfers between devices: 78.2 us -> 73.4 us  [flip(): return lax.ppermute(value, axis, [(i, i ^ mask) for i in range(size)])]
    ppermute x14, starting transfers between devices: 17.4 us -> 13.1 us  [shift(): lax.ppermute(value, axis, [(i, (i + step) % size) for i in range(size)])]
    ppermute x33, starting transfers between devices: 35.6 us -> 32.1 us  [flip(): return lax.ppermute(value, axis, [(i, i ^ mask) for i in range(size)])]
  transfers between devices with their start and end apart: 53 -> 53, of which waited for: 22 -> 21; matrix products, arithmetic and copies ran while one was open for 21% -> 17% of each run, Pallas kernels for 3% -> 6%
where the time goes in v3:
time: 315 us; the launch traced here: 314 us
  waiting for transfers between devices  122 us (39%)
  Pallas kernels  77.1 us (24%)
  starting transfers between devices  56.6 us (18%)
  matrix products  27.3 us (9%)
  other arithmetic  23.1 us (7%)
  local copies, waits for them, and re-layouts  7.23 us (2%)
    ppermute x33, waiting for transfers between devices, flip(): return lax.ppermute(value, axis, [(i, i ^ mask) for i in range(size)])  73.4 us
    ppermute x14, waiting for transfers between devices, shift(): lax.ppermute(value, axis, [(i, (i + step) % size) for i in range(size)])  46 us
    ppermute x33, starting transfers between devices, flip(): return lax.ppermute(value, axis, [(i, i ^ mask) for i in range(size)])  32.1 us
    pallas_call x1, Pallas kernels, gradients(): pl.pallas_call(gradient_kernel, grid=(width // tile,), in_specs=[columns,...  27.6 us
    pallas_call x1, Pallas kernels, forward(): pl.pallas_call(forward_kernel, grid=(count // tile,), in_specs=[pl.BlockS...  22.4 us
    pallas_call x2, Pallas kernels, order_rows(): pl.pallas_call(functools.partial(order_kernel, n_mp, n_dp, piece, len(val...  18 us
    dot_general x8, matrix products, per_device(): jnp.dot(ctx, live[f'weight{t}'], preferred_element_type=jnp.float32)  13.2 us
    ppermute x14, starting transfers between devices, shift(): lax.ppermute(value, axis, [(i, (i + step) % size) for i in range(size)])  13.1 us
  transfers between devices with their start and end apart: 53, of which 21 were waited for; matrix products, arithmetic and copies ran while one was open for 17% of the time, Pallas kernels for 6%

profile of v3, /device:TPU:0, one launch (start us, length us, event | category | flops | bytes accessed | tf_op | source)
XLA Modules:
  0.0 314.4 jit_solution(2333980466479406366)
XLA Ops:
  1.9 3.0 collective-permute-start
  5.0 4.6 %collective-permute-start.2 = (bf16[128,2048]{1,0:T(8,128)(2,1)}, bf16[128,2048]{1,0:T(8,128)(2,1)S(1)}, u32[]{:S(2)}, u32[]{:S(2)}) collective-permute-start(bf16[128,2048]{1,0:T(8,128)(2,1)} %param.12), channel_id=1, source_target_pairs={{0,8},{8,16},{16,24},{1,9},{9,17},{17,25},{2,10},{10,18},{18,26},{... | collective-permute-start | bytes 1572872 | tf_op jit(solution)/shard_map/ppermute | solution.py:304
  14.9 2.2 collective-permute-done
  18.2 2.2 collective-permute-done.2
  23.7 2.5 broadcast_select_fusion
  26.2 11.5 %collective-permute-done.4 = bf16[128,2048]{1,0:T(8,128)(2,1)S(1)} collective-permute-done((bf16[128,2048]{1,0:T(8,128)(2,1)S(1)}, bf16[128,2048]{1,0:T(8,128)(2,1)S(1)}, u32[]{:S(2)}, u32[]{:S(2)}) %collective-permute-start.4) | collective-permute-done | bytes 524320 | tf_op jit(solution)/shard_map/ppermute | solution.py:27
  42.9 2.1 convolution_convert_fusion.8
  47.0 3.4 %shard_map.139 = bf16[128,2048]{1,0:T(8,128)(2,1)} custom-call(s32[1]{0:T(128)} %bitcast.12._, bf16[128,4096]{1,0:T(8,128)(2,1)} %value_ref), custom_call_target="tpu_custom_call" | custom-call | tf_op jit(solution)/shard_map/pallas_call | solution.py:67
  52.0 8.6 %collective-permute-done.8 = bf16[128,2048]{1,0:T(8,128)(2,1)} collective-permute-done((bf16[128,2048]{1,0:T(8,128)(2,1)S(1)}, bf16[128,2048]{1,0:T(8,128)(2,1)}, u32[]{:S(2)}, u32[]{:S(2)}) %collective-permute-start.8) | collective-permute-done | bytes 524320 | tf_op jit(solution)/shard_map/ppermute | solution.py:27
  63.3 7.1 %collective-permute-start.12 = (bf16[80,2048]{1,0:T(8,128)(2,1)S(1)}, bf16[80,2048]{1,0:T(8,128)(2,1)S(1)}, u32[]{:S(2)}, u32[]{:S(2)}) collective-permute-start(bf16[80,2048]{1,0:T(8,128)(2,1)S(1)} %get-tuple-element.170), channel_id=1, source_target_pairs={{0,8},{8,0},{16,24},{24,16},{1,9},{9,1},{17,25},{25,17},{2,10},{10... | collective-permute-start | bytes 983048 | tf_op jit(solution)/shard_map/ppermute | solution.py:27
  74.1 2.2 convert_add_fusion.1
  77.6 10.3 %collective-permute-done.15 = bf16[128,2048]{1,0:T(8,128)(2,1)S(1)} collective-permute-done((bf16[128,2048]{1,0:T(8,128)(2,1)S(1)}, bf16[128,2048]{1,0:T(8,128)(2,1)S(1)}, u32[]{:S(2)}, u32[]{:S(2)}) %collective-permute-start.15) | collective-permute-done | bytes 524320 | tf_op jit(solution)/shard_map/ppermute | solution.py:27
  88.3 2.5 collective-permute-start.17
  98.0 2.5 shard_map.140
  100.5 3.2 %shard_map.141 = bf16[128,2048]{1,0:T(8,128)(2,1)} custom-call(s32[1]{0:T(128)} %bitcast.12._, bf16[128,4096]{1,0:T(8,128)(2,1)} %value_ref.1), custom_call_target="tpu_custom_call" | custom-call | tf_op jit(solution)/shard_map/pallas_call | solution.py:67
  103.9 4.1 %collective-permute-done.20 = bf16[512,512]{1,0:T(8,128)(2,1)} collective-permute-done((bf16[512,512]{1,0:T(8,128)(2,1)}, bf16[512,512]{1,0:T(8,128)(2,1)}, u32[]{:S(2)}, u32[]{:S(2)}) %collective-permute-start.20) | collective-permute-done | bytes 524320 | tf_op jit(solution)/shard_map/ppermute | solution.py:22
  108.0 2.8 collective-permute-done.21
  110.8 3.1 collective-permute-done.18
  123.5 7.0 %collective-permute-done.24 = bf16[512,512]{1,0:T(8,128)(2,1)S(1)} collective-permute-done((bf16[512,512]{1,0:T(8,128)(2,1)S(1)}, bf16[512,512]{1,0:T(8,128)(2,1)S(1)}, u32[]{:S(2)}, u32[]{:S(2)}) %collective-permute-start.24) | collective-permute-done | bytes 524320 | tf_op jit(solution)/shard_map/ppermute | solution.py:22
  130.4 11.7 %collective-permute-done.25 = bf16[512,512]{1,0:T(8,128)(2,1)S(1)} collective-permute-done((bf16[512,512]{1,0:T(8,128)(2,1)S(1)}, bf16[512,512]{1,0:T(8,128)(2,1)S(1)}, u32[]{:S(2)}, u32[]{:S(2)}) %collective-permute-start.25) | collective-permute-done | bytes 524320 | tf_op jit(solution)/shard_map/ppermute | solution.py:27
  147.2 18.9 %collective-permute-done.26 = bf16[240,2048]{1,0:T(8,128)(2,1)S(1)} collective-permute-done((bf16[240,2048]{1,0:T(8,128)(2,1)S(1)}, bf16[240,2048]{1,0:T(8,128)(2,1)S(1)}, u32[]{:S(2)}, u32[]{:S(2)}) %collective-permute-start.26) | collective-permute-done | bytes 983072 | tf_op jit(solution)/shard_map/ppermute | solution.py:22
  173.1 4.2 %collective-permute-done.30 = bf16[128,512]{1,0:T(8,128)(2,1)} collective-permute-done((bf16[128,512]{1,0:T(8,128)(2,1)}, bf16[128,512]{1,0:T(8,128)(2,1)}, u32[]{:S(2)}, u32[]{:S(2)}) %collective-permute-start.30) | collective-permute-done | bytes 131104 | tf_op jit(solution)/shard_map/ppermute | solution.py:27
  183.3 3.0 collective-permute-done.33
  193.9 13.1 %collective-permute-done.36 = bf16[80,2048]{1,0:T(8,128)(2,1)S(1)} collective-permute-done((bf16[80,2048]{1,0:T(8,128)(2,1)S(1)}, bf16[80,2048]{1,0:T(8,128)(2,1)S(1)}, u32[]{:S(2)}, u32[]{:S(2)}) %collective-permute-start.36) | collective-permute-done | bytes 327712 | tf_op jit(solution)/shard_map/ppermute | solution.py:27
  213.4 8.8 %shard_map.142.cot_ref = bf16[1280,4096]{1,0:T(8,128)(2,1)} custom-call(s32[82]{0:T(128)S(1)} %pad_add_fusion.3.at, bf16[2,2,4,80,2048]{4,3,2,1,0:T(8,128)(2,1)S(1)} %bitcast.91, bf16[2,2,4,80,2048]{4,3,2,1,0:T(8,128)(2,1)S(1)} %bitcast.92), custom_call_target="tpu_custom_call" | custom-call | tf_op jit(solution)/shard_map/pallas_call | solution.py:124
  222.2 5.7 %collective-permute-done.40 = bf16[40,2048]{1,0:T(8,128)(2,1)S(1)} collective-permute-done((bf16[40,2048]{1,0:T(8,128)(2,1)S(1)}, bf16[40,2048]{1,0:T(8,128)(2,1)S(1)}, u32[]{:S(2)}, u32[]{:S(2)}) %collective-permute-start.40) | collective-permute-done | bytes 163872 | tf_op jit(solution)/shard_map/ppermute | solution.py:22
  232.3 12.0 %fusion.2.back_ref = f32[688,1280]{1,0:T(8,128)} fusion(bf16[1280,4096]{1,0:T(8,128)(2,1)} %shard_map.142.cot_ref, bf16[1,688,4096]{2,1,0:T(8,128)(2,1)S(1)} %bitcast.106), kind=kOutput, calls=%fused_computation.2 | convolution fusion | flops 7214202880 | bytes 19644416 | tf_op jit(solution)/shard_map/dot_general | solution.py:402
  246.8 5.3 %collective-permute-done.50 = bf16[40,2048]{1,0:T(8,128)(2,1)S(1)} collective-permute-done((bf16[40,2048]{1,0:T(8,128)(2,1)S(1)}, bf16[40,2048]{1,0:T(8,128)(2,1)S(1)}, u32[]{:S(2)}, u32[]{:S(2)}) %collective-permute-start.50) | collective-permute-done | bytes 163872 | tf_op jit(solution)/shard_map/ppermute | solution.py:22
  252.3 2.9 collective-permute-done.52
  255.3 9.2 %shard_map.143.rows_ref = bf16[1280,4096]{1,0:T(8,128)(2,1)} custom-call(s32[210]{0:T(256)S(1)} %pad_add_fusion.at, bf16[2,2,1,80,2048]{4,3,2,1,0:T(8,128)(2,1)S(1)} %bitcast.95, bf16[2,2,1,80,2048]{4,3,2,1,0:T(8,128)(2,1)S(1)} %bitcast.97, bf16[2,2,2,80,2048]{4,3,2,1,0:T(8,128)(2,1)S(1)} %bitcast.93, bf16[2,2,2,80,2048]{4,3,2,1,0:T(8,128)(2,1)S(1)} %bitcast.94, ...), custom_call_target="tpu_custom_call" | custom-call | tf_op jit(solution)/shard_map/pallas_call | solution.py:124
  264.4 22.4 %shard_map.144 = (bf16[688,1280]{1,0:T(8,128)(2,1)}, bf16[688,1280]{1,0:T(8,128)(2,1)}, bf16[688,1280]{1,0:T(8,128)(2,1)}) custom-call(bf16[1280,4096]{1,0:T(8,128)(2,1)} %shard_map.143.rows_ref, bf16[688,4096]{1,0:T(8,128)(2,1)} %bitcast.99, bf16[688,4096]{1,0:T(8,128)(2,1)} %bitcast.100, f32[688,1280]{1,0:T(8,128)} %fusion.2.back_ref), custom_call_target="tpu_custom_call" | custom-call | tf_op jit(solution)/shard_map/pallas_call | solution.py:161
  286.9 27.6 %shard_map.145 = (bf16[688,4096]{1,0:T(8,128)(2,1)}, bf16[688,4096]{1,0:T(8,128)(2,1)}, bf16[688,4096]{1,0:T(8,128)(2,1)}) custom-call(bf16[1280,4096]{1,0:T(8,128)(2,1)} %shard_map.143.rows_ref, bf16[1280,4096]{1,0:T(8,128)(2,1)} %shard_map.142.cot_ref, bf16[688,1280]{1,0:T(8,128)(2,1)} %get-tuple-element.285.hidden_ref, ...), custom_call_target="tpu_custom_call" | custom-call | tf_op jit(solution)/shard_map/pallas_call | solution.py:184
  (217 shorter events, 83.1 us)
Async XLA Ops:
  0.6 17.6 %collective-permute-start.1 = (bf16[128,2048]{1,0:T(8,128)(2,1)}, bf16[128,2048]{1,0:T(8,128)(2,1)S(1)}, u32[]{:S(2)}, u32[]{:S(2)}) collective-permute-start(bf16[128,2048]{1,0:T(8,128)(2,1)} %param.12), channel_id=1, source_target_pairs={{8,0},{16,8},{24,16},{9,1},{17,9},{25,17},{10,2},{18,10},{26,18},{... | collective-permute-start | bytes 1572872 | tf_op jit(solution)/shard_map/ppermute | solution.py:305
  1.9 15.2 %collective-permute-start = (bf16[128,2048]{1,0:T(8,128)(2,1)}, bf16[128,2048]{1,0:T(8,128)(2,1)S(1)}, u32[]{:S(2)}, u32[]{:S(2)}) collective-permute-start(bf16[128,2048]{1,0:T(8,128)(2,1)} %param.12), channel_id=1, source_target_pairs={{0,2},{1,3},{2,0},{3,1},{4,6},{5,7},{6,4},{7,5},{8,10},{9,11},{10,... | collective-permute-start | bytes 1572872 | tf_op jit(solution)/shard_map/ppermute | solution.py:27
  5.0 15.5 %collective-permute-start.2 = (bf16[128,2048]{1,0:T(8,128)(2,1)}, bf16[128,2048]{1,0:T(8,128)(2,1)S(1)}, u32[]{:S(2)}, u32[]{:S(2)}) collective-permute-start(bf16[128,2048]{1,0:T(8,128)(2,1)} %param.12), channel_id=1, source_target_pairs={{0,8},{8,16},{16,24},{1,9},{9,17},{17,25},{2,10},{10,18},{18,26},{... | collective-permute-start | bytes 1572872 | tf_op jit(solution)/shard_map/ppermute | solution.py:304
  20.4 17.5 %collective-permute-start.5 = (bf16[128,2048]{1,0:T(8,128)(2,1)S(1)}, bf16[128,2048]{1,0:T(8,128)(2,1)S(1)}, u32[]{:S(2)}, u32[]{:S(2)}) collective-permute-start(bf16[128,2048]{1,0:T(8,128)(2,1)S(1)} %collective-permute-done.1), channel_id=1, source_target_pairs={{8,0},{16,8},{9,1},{17,9},{10,2},{18,10},{11,3},{19,11},{12,4},{20... | collective-permute-start | bytes 1572872 | tf_op jit(solution)/shard_map/ppermute | solution.py:305
  21.7 16.2 %collective-permute-start.6 = (bf16[128,2048]{1,0:T(8,128)(2,1)S(1)}, bf16[128,2048]{1,0:T(8,128)(2,1)}, u32[]{:S(2)}, u32[]{:S(2)}) collective-permute-start(bf16[128,2048]{1,0:T(8,128)(2,1)S(1)} %collective-permute-done.2), channel_id=1, source_target_pairs={{8,16},{16,24},{9,17},{17,25},{10,18},{18,26},{11,19},{19,27},{12,... | collective-permute-start | bytes 1572872 | tf_op jit(solution)/shard_map/ppermute | solution.py:304
  37.9 25.4 %collective-permute-start.9 = (bf16[128,2048]{1,0:T(8,128)(2,1)S(1)}, bf16[128,2048]{1,0:T(8,128)(2,1)}, u32[]{:S(2)}, u32[]{:S(2)}) collective-permute-start(bf16[128,2048]{1,0:T(8,128)(2,1)S(1)} %collective-permute-done.5), channel_id=1, source_target_pairs={{8,0},{9,1},{10,2},{11,3},{12,4},{13,5},{14,6},{15,7}} | collective-permute-start | bytes 1572872 | tf_op jit(solution)/shard_map/ppermute | solution.py:305
  39.2 24.1 %collective-permute-start.11 = (bf16[128,2048]{1,0:T(8,128)(2,1)}, bf16[128,2048]{1,0:T(8,128)(2,1)}, u32[]{:S(2)}, u32[]{:S(2)}) collective-permute-start(bf16[128,2048]{1,0:T(8,128)(2,1)} %collective-permute-done.6), channel_id=1, source_target_pairs={{16,24},{17,25},{18,26},{19,27},{20,28},{21,29},{22,30},{23,31}} | collective-permute-start | bytes 1572872 | tf_op jit(solution)/shard_map/ppermute | solution.py:304
  40.7 21.0 %collective-permute-start.7 = (bf16[256,2048]{1,0:T(8,128)(2,1)S(1)}, bf16[256,2048]{1,0:T(8,128)(2,1)}, u32[]{:S(2)}, u32[]{:S(2)}) collective-permute-start(bf16[256,2048]{1,0:T(8,128)(2,1)S(1)} %pad_maximum_fusion.9), channel_id=1, source_target_pairs={{0,1},{1,0},{2,3},{3,2},{4,5},{5,4},{6,7},{7,6},{8,9},{9,8},{10,11... | collective-permute-start | bytes 3145736 | tf_op jit(solution)/shard_map/ppermute | solution.py:27
  45.0 18.3 %collective-permute-start.10 = (bf16[512,512]{1,0:T(8,128)(2,1)}, bf16[512,512]{1,0:T(8,128)(2,1)}, u32[]{:S(2)}, u32[]{:S(2)}) collective-permute-start(bf16[512,512]{1,0:T(8,128)(2,1)} %convolution_convert_fusion.7), channel_id=1, source_target_pairs={{0,4},{4,0},{1,5},{5,1},{2,6},{6,2},{3,7},{7,3},{8,12},{12,8},{9,1... | collective-permute-start | bytes 1572872 | tf_op jit(solution)/shard_map/ppermute | solution.py:22
  63.3 24.9 %collective-permute-start.12 = (bf16[80,2048]{1,0:T(8,128)(2,1)S(1)}, bf16[80,2048]{1,0:T(8,128)(2,1)S(1)}, u32[]{:S(2)}, u32[]{:S(2)}) collective-permute-start(bf16[80,2048]{1,0:T(8,128)(2,1)S(1)} %get-tuple-element.170), channel_id=1, source_target_pairs={{0,8},{8,0},{16,24},{24,16},{1,9},{9,1},{17,25},{25,17},{2,10},{10... | collective-permute-start | bytes 983048 | tf_op jit(solution)/shard_map/ppermute | solution.py:27
  70.5 17.8 %collective-permute-start.13 = (bf16[80,2048]{1,0:T(8,128)(2,1)S(1)}, bf16[80,2048]{1,0:T(8,128)(2,1)S(1)}, u32[]{:S(2)}, u32[]{:S(2)}) collective-permute-start(bf16[80,2048]{1,0:T(8,128)(2,1)S(1)} %get-tuple-element.171), channel_id=1, source_target_pairs={{0,16},{8,24},{16,0},{24,8},{1,17},{9,25},{17,1},{25,9},{2,18},{10... | collective-permute-start | bytes 983048 | tf_op jit(solution)/shard_map/ppermute | solution.py:27
  71.7 16.5 %collective-permute-start.16 = (bf16[512,512]{1,0:T(8,128)(2,1)S(1)}, bf16[512,512]{1,0:T(8,128)(2,1)S(1)}, u32[]{:S(2)}, u32[]{:S(2)}) collective-permute-start(bf16[512,512]{1,0:T(8,128)(2,1)S(1)} %convolution_convert_fusion.5), channel_id=1, source_target_pairs={{0,4},{4,0},{1,5},{5,1},{2,6},{6,2},{3,7},{7,3},{8,12},{12,8},{9,1... | collective-permute-start | bytes 1572872 | tf_op jit(solution)/shard_map/ppermute | solution.py:22
  72.3 15.6 %collective-permute-start.14 = (bf16[256,2048]{1,0:T(8,128)(2,1)S(1)}, bf16[256,2048]{1,0:T(8,128)(2,1)S(1)}, u32[]{:S(2)}, u32[]{:S(2)}) collective-permute-start(bf16[256,2048]{1,0:T(8,128)(2,1)S(1)} %pad_maximum_fusion.10), channel_id=1, source_target_pairs={{0,1},{1,0},{2,3},{3,2},{4,5},{5,4},{6,7},{7,6},{8,9},{9,8},{10,11... | collective-permute-start | bytes 3145736 | tf_op jit(solution)/shard_map/ppermute | solution.py:27
  88.3 15.6 %collective-permute-start.17 = (bf16[80,2048]{1,0:T(8,128)(2,1)S(1)}, bf16[80,2048]{1,0:T(8,128)(2,1)}, u32[]{:S(2)}, u32[]{:S(2)}) collective-permute-start(bf16[80,2048]{1,0:T(8,128)(2,1)S(1)} %get-tuple-element.186), channel_id=1, source_target_pairs={{0,24},{8,16},{16,8},{24,0},{1,25},{9,17},{17,9},{25,1},{2,26},{10... | collective-permute-start | bytes 983048 | tf_op jit(solution)/shard_map/ppermute | solution.py:27
  90.9 23.1 %collective-permute-start.18 = (bf16[240,2048]{1,0:T(8,128)(2,1)S(1)}, bf16[240,2048]{1,0:T(8,128)(2,1)}, u32[]{:S(2)}, u32[]{:S(2)}) collective-permute-start(bf16[240,2048]{1,0:T(8,128)(2,1)S(1)} %constant_dynamic-update-slice_fusion), channel_id=1, source_target_pairs={{0,2},{1,3},{2,0},{3,1},{4,6},{5,7},{6,4},{7,5},{8,10},{9,11},{10,... | collective-permute-start | bytes 2949128 | tf_op jit(solution)/shard_map/ppermute | solution.py:27
  118.6 23.4 %collective-permute-start.25 = (bf16[512,512]{1,0:T(8,128)(2,1)S(1)}, bf16[512,512]{1,0:T(8,128)(2,1)S(1)}, u32[]{:S(2)}, u32[]{:S(2)}) collective-permute-start(bf16[512,512]{1,0:T(8,128)(2,1)S(1)} %add_convert_fusion.1), channel_id=1, source_target_pairs={{0,16},{8,24},{16,0},{24,8},{1,17},{9,25},{17,1},{25,9},{2,18},{10... | collective-permute-start | bytes 1572872 | tf_op jit(solution)/shard_map/ppermute | solution.py:27
  118.8 23.3 %collective-permute-start.23 = (bf16[160,2048]{1,0:T(8,128)(2,1)S(1)}, bf16[160,2048]{1,0:T(8,128)(2,1)S(1)}, u32[]{:S(2)}, u32[]{:S(2)}) collective-permute-start(bf16[160,2048]{1,0:T(8,128)(2,1)S(1)} %slice.124), channel_id=1, source_target_pairs={{0,4},{4,0},{1,5},{5,1},{2,6},{6,2},{3,7},{7,3},{8,12},{12,8},{9,1... | collective-permute-start | bytes 1966088 | tf_op jit(solution)/shard_map/ppermute | solution.py:22
  142.3 23.7 %collective-permute-start.26 = (bf16[240,2048]{1,0:T(8,128)(2,1)S(1)}, bf16[240,2048]{1,0:T(8,128)(2,1)S(1)}, u32[]{:S(2)}, u32[]{:S(2)}) collective-permute-start(bf16[240,2048]{1,0:T(8,128)(2,1)S(1)} %pad_maximum_fusion.12), channel_id=1, source_target_pairs={{0,4},{4,0},{1,5},{5,1},{2,6},{6,2},{3,7},{7,3},{8,12},{12,8},{9,1... | collective-permute-start | bytes 2949128 | tf_op jit(solution)/shard_map/ppermute | solution.py:22
  143.9 22.3 %collective-permute-start.27 = (bf16[160,2048]{1,0:T(8,128)(2,1)S(1)}, bf16[160,2048]{1,0:T(8,128)(2,1)S(1)}, u32[]{:S(2)}, u32[]{:S(2)}) collective-permute-start(bf16[160,2048]{1,0:T(8,128)(2,1)S(1)} %collective-permute-done.23), channel_id=1, source_target_pairs={{0,2},{1,3},{2,0},{3,1},{4,6},{5,7},{6,4},{7,5},{8,10},{9,11},{10,... | collective-permute-start | bytes 1966088 | tf_op jit(solution)/shard_map/ppermute | solution.py:27
  145.5 22.3 %collective-permute-start.28 = (bf16[512,512]{1,0:T(8,128)(2,1)S(1)}, bf16[512,512]{1,0:T(8,128)(2,1)S(1)}, u32[]{:S(2)}, u32[]{:S(2)}) collective-permute-start(bf16[512,512]{1,0:T(8,128)(2,1)S(1)} %add_convert_fusion), channel_id=1, source_target_pairs={{0,24},{8,16},{16,8},{24,0},{1,25},{9,17},{17,9},{25,1},{2,26},{10... | collective-permute-start | bytes 1572872 | tf_op jit(solution)/shard_map/ppermute | solution.py:27
  188.3 18.8 %collective-permute-start.34 = (bf16[1280,2048]{1,0:T(8,128)(2,1)S(1)}, bf16[1280,2048]{1,0:T(8,128)(2,1)S(1)}, u32[]{:S(2)}, u32[]{:S(2)}) collective-permute-start(bf16[1280,2048]{1,0:T(8,128)(2,1)S(1)} %constant_dynamic-update-slice_fusion.3), channel_id=1, source_target_pairs={{0,1},{1,0},{2,3},{3,2},{4,5},{5,4},{6,7},{7,6},{8,9},{9,8},{10,11... | collective-permute-start | bytes 15728648 | tf_op jit(solution)/shard_map/ppermute | solution.py:27
  189.5 17.5 %collective-permute-start.36 = (bf16[80,2048]{1,0:T(8,128)(2,1)S(1)}, bf16[80,2048]{1,0:T(8,128)(2,1)S(1)}, u32[]{:S(2)}, u32[]{:S(2)}) collective-permute-start(bf16[80,2048]{1,0:T(8,128)(2,1)S(1)} %get-tuple-element.295), channel_id=1, source_target_pairs={{0,16},{8,24},{16,0},{24,8},{1,17},{9,25},{17,1},{25,9},{2,18},{10... | collective-permute-start | bytes 983048 | tf_op jit(solution)/shard_map/ppermute | solution.py:27
  190.6 16.5 %collective-permute-start.35 = (bf16[80,2048]{1,0:T(8,128)(2,1)S(1)}, bf16[80,2048]{1,0:T(8,128)(2,1)S(1)}, u32[]{:S(2)}, u32[]{:S(2)}) collective-permute-start(bf16[80,2048]{1,0:T(8,128)(2,1)S(1)} %get-tuple-element.296), channel_id=1, source_target_pairs={{0,8},{8,0},{16,24},{24,16},{1,9},{9,1},{17,25},{25,17},{2,10},{10... | collective-permute-start | bytes 983048 | tf_op jit(solution)/shard_map/ppermute | solution.py:27
  191.8 15.3 %collective-permute-start.38 = (bf16[80,2048]{1,0:T(8,128)(2,1)S(1)}, bf16[80,2048]{1,0:T(8,128)(2,1)S(1)}, u32[]{:S(2)}, u32[]{:S(2)}) collective-permute-start(bf16[80,2048]{1,0:T(8,128)(2,1)S(1)} %get-tuple-element.251), channel_id=1, source_target_pairs={{0,2},{1,3},{2,0},{3,1},{4,6},{5,7},{6,4},{7,5},{8,10},{9,11},{10,... | collective-permute-start | bytes 983048 | tf_op jit(solution)/shard_map/ppermute | solution.py:27
  207.2 20.9 %collective-permute-start.43 = (bf16[160,2048]{1,0:T(8,128)(2,1)S(1)}, bf16[160,2048]{1,0:T(8,128)(2,1)S(1)}, u32[]{:S(2)}, u32[]{:S(2)}) collective-permute-start(bf16[160,2048]{1,0:T(8,128)(2,1)S(1)} %constant_dynamic-update-slice_fusion.11), channel_id=1, source_target_pairs={{0,2},{1,3},{2,0},{3,1},{4,6},{5,7},{6,4},{7,5},{8,10},{9,11},{10,... | collective-permute-start | bytes 1966088 | tf_op jit(solution)/shard_map/ppermute | solution.py:27
  208.3 19.8 %collective-permute-start.42 = (bf16[160,2048]{1,0:T(8,128)(2,1)S(1)}, bf16[160,2048]{1,0:T(8,128)(2,1)S(1)}, u32[]{:S(2)}, u32[]{:S(2)}) collective-permute-start(bf16[160,2048]{1,0:T(8,128)(2,1)S(1)} %constant_dynamic-update-slice_fusion.11), channel_id=1, source_target_pairs={{0,4},{4,0},{1,5},{5,1},{2,6},{6,2},{3,7},{7,3},{8,12},{12,8},{9,1... | collective-permute-start | bytes 1966088 | tf_op jit(solution)/shard_map/ppermute | solution.py:22
  209.1 18.9 %collective-permute-start.41 = (bf16[40,2048]{1,0:T(8,128)(2,1)S(1)}, bf16[40,2048]{1,0:T(8,128)(2,1)S(1)}, u32[]{:S(2)}, u32[]{:S(2)}) collective-permute-start(bf16[40,2048]{1,0:T(8,128)(2,1)S(1)} %slice.139), channel_id=1, source_target_pairs={{0,2},{1,3},{2,0},{3,1},{4,6},{5,7},{6,4},{7,5},{8,10},{9,11},{10,... | collective-permute-start | bytes 491528 | tf_op jit(solution)/shard_map/ppermute | solution.py:27
  210.0 17.9 %collective-permute-start.40 = (bf16[40,2048]{1,0:T(8,128)(2,1)S(1)}, bf16[40,2048]{1,0:T(8,128)(2,1)S(1)}, u32[]{:S(2)}, u32[]{:S(2)}) collective-permute-start(bf16[40,2048]{1,0:T(8,128)(2,1)S(1)} %slice.138), channel_id=1, source_target_pairs={{0,4},{4,0},{1,5},{5,1},{2,6},{6,2},{3,7},{7,3},{8,12},{12,8},{9,1... | collective-permute-start | bytes 491528 | tf_op jit(solution)/shard_map/ppermute | solution.py:22
  211.4 16.6 %collective-permute-start.39 = (bf16[80,2048]{1,0:T(8,128)(2,1)S(1)}, bf16[80,2048]{1,0:T(8,128)(2,1)S(1)}, u32[]{:S(2)}, u32[]{:S(2)}) collective-permute-start(bf16[80,2048]{1,0:T(8,128)(2,1)S(1)} %get-tuple-element.250), channel_id=1, source_target_pairs={{0,24},{8,16},{16,8},{24,0},{1,25},{9,17},{17,9},{25,1},{2,26},{10... | collective-permute-start | bytes 983048 | tf_op jit(solution)/shard_map/ppermute | solution.py:27
  228.0 16.5 %collective-permute-start.48 = (bf16[80,2048]{1,0:T(8,128)(2,1)S(1)}, bf16[80,2048]{1,0:T(8,128)(2,1)S(1)}, u32[]{:S(2)}, u32[]{:S(2)}) collective-permute-start(bf16[80,2048]{1,0:T(8,128)(2,1)S(1)} %collective-permute-done.39), channel_id=1, source_target_pairs={{0,2},{1,3},{2,0},{3,1},{4,6},{5,7},{6,4},{7,5},{8,10},{9,11},{10,... | collective-permute-start | bytes 983048 | tf_op jit(solution)/shard_map/ppermute | solution.py:27
  229.1 15.5 %collective-permute-start.47 = (bf16[80,2048]{1,0:T(8,128)(2,1)S(1)}, bf16[80,2048]{1,0:T(8,128)(2,1)S(1)}, u32[]{:S(2)}, u32[]{:S(2)}) collective-permute-start(bf16[80,2048]{1,0:T(8,128)(2,1)S(1)} %collective-permute-done.39), channel_id=1, source_target_pairs={{0,4},{4,0},{1,5},{5,1},{2,6},{6,2},{3,7},{7,3},{8,12},{12,8},{9,1... | collective-permute-start | bytes 983048 | tf_op jit(solution)/shard_map/ppermute | solution.py:22
  229.5 15.0 %collective-permute-start.46 = (bf16[80,2048]{1,0:T(8,128)(2,1)S(1)}, bf16[80,2048]{1,0:T(8,128)(2,1)S(1)}, u32[]{:S(2)}, u32[]{:S(2)}) collective-permute-start(bf16[80,2048]{1,0:T(8,128)(2,1)S(1)} %slice.141), channel_id=1, source_target_pairs={{0,2},{1,3},{2,0},{3,1},{4,6},{5,7},{6,4},{7,5},{8,10},{9,11},{10,... | collective-permute-start | bytes 983048 | tf_op jit(solution)/shard_map/ppermute | solution.py:27
  (38 other events, 361.9 us)

commit v4 on v3

--- a/solution.py
+++ b/solution.py
@@ -76,62 +76,53 @@
     )(jnp.full((1,), first, jnp.int32), value)
 
 
-def order_kernel(n_mp, n_dp, piece, sources, at, *refs):
+def order_kernel(n_mp, n_dp, piece, steps, at, *refs):
     out_ref = refs[-1]
-    turn = at[n_mp + pl.program_id(0)]
-    for c in range(sources):
-
-        @pl.when(turn == c)
-        def _():
-            for p in range(n_mp):
-                step = at[p]
+    count = pl.num_programs(0)
+    for p in range(n_mp):
+        for c, step in enumerate(steps):
+
+            @pl.when((at[p] == step) & (at[n_mp + step * count + pl.program_id(0)] == c))
+            def _():
                 for k in range(n_dp):
                     first = (k * n_mp + p) * piece
-                    out_ref[:, first : first + piece] = refs[c][step, 0, 0, :, k * piece : (k + 1) * piece]
-
-
-def order_rows(sources, groups, n_dp, piece):
-    values, where = [], {}
-    for slots, parts in sources:
-        share = n_dp // len(parts)
-        for c, value in enumerate(parts):
-            for j in range(share):
-                for i, m in enumerate(slots):
-                    where[c * share + j, m] = (len(values), j, i)
-            n_mp, columns = value.shape[0], value.shape[2]
-            values.append(value.reshape(n_mp, share, len(slots), -1, columns))
-    rows = values[0].shape[3]
-    x = lax.axis_index("mp")
-    places = [where[j, m] for g in groups for j in range(n_dp) for m in g]
+                    out_ref[:, first : first + piece] = refs[c][0, :, k * piece : (k + 1) * piece]
+
+
+def order_rows(sources, groups, n_dp, piece, first=0, total=None, whole=None):
+    rows = sources[0][1].shape[1]
+    n_mp, x = lax.axis_size("mp"), lax.axis_index("mp")
+    places = [(j, m) for g in groups for j in range(n_dp) for m in g]
     count = len(places)
-    columns = [[c for c, _, _ in places]]
-    for c in range(len(values)):
-        held = next((j, m) for i, j, m in places if i == c)
-        kept = []
-        for i, j, m in places:
-            held = (j, m) if i == c else held
-            kept.append(held)
-        columns += [[j for j, _ in kept], [m for _, m in kept]]
-    steps = (x - jnp.arange(n_mp, dtype=jnp.int32)) % n_mp
-    table = jnp.concatenate([steps, jnp.asarray(sum(columns, []), jnp.int32)])
+    steps = [step for step, _, _ in sources]
+    columns = []
+    for step in range(n_mp):
+        mine = [c for c, other in enumerate(steps) if other == step]
+        columns += [next(c for c in mine if place in sources[c][2]) for place in places]
+    for _, _, blocks in sources:
+        held = next(blocks[place] for place in places if place in blocks)
+        for place in places:
+            held = blocks.get(place, held)
+            columns.append(held)
+    table = jnp.concatenate([(x - jnp.arange(n_mp, dtype=jnp.int32)) % n_mp, jnp.asarray(columns, jnp.int32)])
 
     def spec(c):
-        base = n_mp + count * (1 + 2 * c)
-        return pl.BlockSpec(
-            (n_mp, 1, 1, rows, n_dp * piece), lambda i, at: (0, at[base + i], at[base + count + i], 0, 0)
-        )
-
+        base = n_mp + count * (n_mp + c)
+        return pl.BlockSpec((1, rows, n_dp * piece), lambda i, at: (at[base + i], 0, 0))
+
+    more = [] if whole is None else [whole]
     return pl.pallas_call(
-        functools.partial(order_kernel, n_mp, n_dp, piece, len(values)),
+        functools.partial(order_kernel, n_mp, n_dp, piece, steps),
         grid_spec=pltpu.PrefetchScalarGridSpec(
             num_scalar_prefetch=1,
             grid=(count,),
-            in_specs=[spec(c) for c in range(len(values))],
-            out_specs=pl.BlockSpec((rows, n_mp * n_dp * piece), lambda i, at: (i, 0)),
+            in_specs=[spec(c) for c in range(len(sources))] + [pl.BlockSpec(memory_space=pltpu.HBM)] * len(more),
+            out_specs=pl.BlockSpec((rows, n_mp * n_dp * piece), lambda i, at: (first + i, 0)),
         ),
-        out_shape=jax.ShapeDtypeStruct((count * rows, n_mp * n_dp * piece), values[0].dtype),
+        out_shape=pltpu.HBM(((total or count) * rows, n_mp * n_dp * piece), sources[0][1].dtype),
+        input_output_aliases={1 + len(sources): 0} if more else {},
         compiler_params=pltpu.CompilerParams(vmem_limit_bytes=40 << 20),
-    )(table, *values)
+    )(table, *[value for _, value, _ in sources], *more)
 
 
 def forward_kernel(rows_ref, gate_ref, up_ref, back_ref, hidden_ref, d_gate_ref, d_up_ref):
@@ -273,7 +264,7 @@
 
     def taken(name):
         blocks = [live.pop(f"{name}_{c}") for c in range(1 << len(core_masks))]
-        return [v.reshape(n_mp, -1, v.shape[1]) for v in blocks]
+        return [v.reshape(-1, capacity, v.shape[1]) for v in blocks]
 
     def cascade(name, at):
         for g in range(len(groups)):
@@ -331,34 +322,24 @@
             rows = (rows * live.pop("row_gate")).astype(jnp.bfloat16)
             for m in range(n_br):
                 live[f"cot{m}"] = rows[m * capacity : (m + 1) * capacity]
-        if r == n_br:
+        if r == n_br + 2:
             live["residual"] = my_columns(live["residual"])
             live["gain"] = my_columns(live["gain"])
         if n_br - 1 <= r < n_br + 1 and r - n_br + 2 < len(groups):
             hop_plane("cot", r - n_br + 2)
         if r == n_br:
-            block = live["cot_first"] = jnp.concatenate([live.pop(f"cot{m}") for m in range(near + 1)], axis=0)
-            live["cot_first_far"] = flip(block, "dp", far_masks[0])
+            block = live["cot_near"] = jnp.concatenate([live.pop(f"cot{m}") for m in range(near)], axis=0)
+            live["cot_near_far"] = flip(block, "dp", far_masks[0])
         if r == n_br + 1:
-            block = jnp.concatenate([live.pop(f"cot{m}") for m in range(near + 1, n_br)], axis=0)
-            far = jnp.concatenate([live.pop("cot_first_far"), flip(block, "dp", far_masks[0])], axis=0)
-            block = jnp.concatenate([live.pop("cot_first"), block], axis=0)
-            live["cot"], live["cot_far"] = block, far
+            block = live["cot_rest"] = jnp.concatenate([live.pop(f"cot{m}") for m in range(near, n_br)], axis=0)
+            live["cot_rest_far"] = flip(block, "dp", far_masks[0])
             for t in range(1, n_mp):
-                live[f"cot_top{t}"] = shift(block[: near * capacity], "mp", t)
+                live[f"cot_near_{t}"] = shift(live["cot_near"], "mp", t)
         if r == n_br + 2:
-            block, far = live.pop("cot"), live.pop("cot_far")
-            parts = [block, far]
-            first = (near + 1) * capacity
-            both = jnp.concatenate([block[near * capacity :], far[near * capacity : first]], axis=0)
-            rest = block.shape[0] - near * capacity
+            both = jnp.concatenate([live["cot_rest"], live["cot_rest_far"][:capacity]], axis=0)
             for t in range(1, n_mp):
-                top = live.pop(f"cot_top{t}")
-                across = shift(both, "mp", t)
-                parts += [top, across[:rest], flip(top, "dp", far_masks[0]), across[rest:]]
-                live[f"cot_end{t}"] = far[first:]
-            live["cota0"] = jnp.concatenate(parts[:2], axis=0)
-            live["cota_across"] = jnp.concatenate(parts[2:], axis=0)
+                live[f"cot_both_{t}"] = shift(both, "mp", t)
+                live[f"cot_near_far_{t}"] = flip(live[f"cot_near_{t}"], "dp", far_masks[0])
         fence()
 
     total = sum(live.pop(f"share{m}").astype(jnp.float32) for m in range(n_br))
@@ -367,13 +348,18 @@
     for i, o in enumerate(relative_order(n_dp)):
         block = total[i * tokens : (i + 1) * tokens]
         got[o] = flip(block, "dp", o) if o else block
-    parts, across = [live.pop("cota0")], live.pop("cota_across")
-    size = across.shape[0] // (n_mp - 1) if n_mp > 1 else 0
+    split = n_br - near > 1
+    if split:
+        for t in range(1, n_mp):
+            live[f"cot_end_{t}"] = shift(live["cot_rest_far"][capacity:], "mp", t)
+    parts = [live[f"cot_{name}"] for name in ("near", "rest", "near_far", "rest_far")]
+    rest = parts[1].shape[0]
     for t in range(1, n_mp):
-        parts += [across[(t - 1) * size : t * size], shift(live.pop(f"cot_end{t}"), "mp", t)]
-    for i, part in enumerate(parts):
-        live[f"cot_part{i}"] = part
-    cot_parts = len(parts)
+        both = live.pop(f"cot_both_{t}")
+        parts += [live.pop(f"cot_near_{t}"), both[:rest], live.pop(f"cot_near_far_{t}"), both[rest:]]
+    live["cota"] = jnp.concatenate(parts, axis=0)
+    for name in ("near", "rest", "near_far", "rest_far"):
+        del live[f"cot_{name}"]
     live["attention"] = jnp.concatenate([choose(got, d ^ k) for k in range(n_dp)], axis=1)
     fence()
 
@@ -383,6 +369,10 @@
     for s in range(1, n_mp):
         all_squares = all_squares + shift(squares.reshape(1, tokens), "mp", s).reshape(tokens, 1)
     live["mixed"], live["squares"] = mixed, all_squares
+    if split:
+        ends = jnp.concatenate([live.pop(f"cot_end_{t}") for t in range(1, n_mp)], axis=0)
+        for c, block in enumerate(core_flips(ends)):
+            live[f"cotend_{c}"] = block
     fence()
 
     inv_rms = lax.rsqrt(live.pop("squares") / width + 1e-05)
@@ -390,22 +380,49 @@
     send_in = jnp.dot(live.pop("selector"), normed, preferred_element_type=jnp.float32).astype(jnp.bfloat16)
     for m in range(n_br):
         live[f"in{m}"] = send_in[m * capacity : (m + 1) * capacity]
+
+    def order_group(g):
+        first = n_dp * sum(len(other) for other in groups[:g])
+        slots_of, share = groups[g], 1 + len(far_masks)
+        sources = []
+        for c, value in enumerate(taken(f"ina{g}")):
+            for t in range(n_mp):
+                at = {
+                    (c * share + y, m): (t * share + y) * len(slots_of) + i
+                    for y in range(share)
+                    for i, m in enumerate(slots_of)
+                }
+                sources.append((t, value, at))
+        live["in"] = order_rows(sources, [slots_of], n_dp, piece, first, n_dp * n_br, live.get("in"))
+
     for r in range(len(groups) + 2):
+        if 0 <= r - 3 < len(groups):
+            order_group(r - 3)
         cascade("in", r)
         if r == 0:
-            live["cota0"] = jnp.concatenate([live.pop(f"cot_part{i}") for i in range(cot_parts)], axis=0)
-            for c, block in enumerate(core_flips(live.pop("cota0"))):
+            for c, block in enumerate(core_flips(live.pop("cota"))):
                 live[f"cota_{c}"] = block
         if r == 1:
-            live["cotan"] = order_rows([(list(range(n_br)), taken("cota"))], groups, n_dp, piece)
+            sources = []
+            for c, value in enumerate(taken("cota")):
+                for t in range(n_mp):
+                    base = t * (n_br + near + 1) + (n_br - near - 1 if t else 0)
+                    at = {(2 * c, m): base + m for m in range(n_br)}
+                    at.update({(2 * c + 1, m): base + n_br + m for m in range(near + 1 if t else n_br)})
+                    sources.append((t, value, at))
+            for c, value in enumerate(taken("cotend") if split else []):
+                for t in range(1, n_mp):
+                    base = (t - 1) * (n_br - near - 1) - near - 1
+                    sources.append((t, value, {(2 * c + 1, m): base + m for m in range(near + 1, n_br)}))
+            live["cotan"] = order_rows(sources, groups, n_dp, piece)
         if r == 2:
             live["back"] = lax.dot_general(
                 down_weight[0], live["cotan"], (((1,), (1,)), ((), ())), preferred_element_type=jnp.float32
             )
         fence()
     cotan_rows, back_grad = live.pop("cotan"), live.pop("back")
-    sources = [(slots_of, taken(f"ina{g}")) for g, slots_of in enumerate(groups)]
-    tokens_in = order_rows(sources, groups, n_dp, piece)
+    order_group(len(groups) - 1)
+    tokens_in = live.pop("in")
     hidden, d_gate, d_up = forward(tokens_in, gate_weight[0].T, up_weight[0].T, back_grad)
     grad_gate, grad_up, grad_down = gradients(tokens_in, cotan_rows, hidden, d_gate, d_up)
     return (grad_gate.T[None], grad_up.T[None], grad_down[None])

time: 315 us -> 305 us (0.968)
  waiting for transfers between devices: 122 us -> 109 us
  starting transfers between devices: 56.6 us -> 64.7 us
  other arithmetic: 23.1 us -> 17 us
    ppermute x14, waiting for transfers between devices: 46 us -> 30.3 us  [shift(): lax.ppermute(value, axis, [(i, (i + step) % size) for i in range(size)])]
    ppermute x33 -> x34, starting transfers between devices: 32.1 us -> 37.7 us  [flip(): return lax.ppermute(value, axis, [(i, i ^ mask) for i in range(size)])]
    ppermute x33 -> x34, waiting for transfers between devices: 73.4 us -> 76.7 us  [flip(): return lax.ppermute(value, axis, [(i, i ^ mask) for i in range(size)])]
    concatenate x7 -> x4, other arithmetic: 4.49 us -> 1.3 us  [the longest x1 1.07 us: per_device(): jnp.concatenate([live['cot_rest'], live['cot_rest_far'][:capacity]], axis=0)]
    pallas_call x2 -> x4, Pallas kernels: 18 us -> 18.6 us  [order_rows(): pl.pallas_call(functools.partial(order_kernel, n_mp, n_dp, piece, steps),...]
  transfers between devices with their start and end apart: 53 -> 54, of which waited for: 21 -> 19; matrix products, arithmetic and copies ran while one was open for 17% -> 16% of each run, Pallas kernels for 6% -> 8%
where the time goes in v4:
time: 305 us; the launch traced here: 304 us
  waiting for transfers between devices  109 us (36%)
  Pallas kernels  77.8 us (26%)
  starting transfers between devices  64.7 us (21%)
  matrix products  25.6 us (8%)
  other arithmetic  17 us (6%)
  local copies, waits for them, and re-layouts  8 us (3%)
    ppermute x34, waiting for transfers between devices, flip(): return lax.ppermute(value, axis, [(i, i ^ mask) for i in range(size)])  76.7 us
    ppermute x34, starting transfers between devices, flip(): return lax.ppermute(value, axis, [(i, i ^ mask) for i in range(size)])  37.7 us
    ppermute x14, waiting for transfers between devices, shift(): lax.ppermute(value, axis, [(i, (i + step) % size) for i in range(size)])  30.3 us
    pallas_call x1, Pallas kernels, gradients(): pl.pallas_call(gradient_kernel, grid=(width // tile,), in_specs=[columns,...  27.6 us
    pallas_call x1, Pallas kernels, forward(): pl.pallas_call(forward_kernel, grid=(count // tile,), in_specs=[pl.BlockS...  22.5 us
    pallas_call x4, Pallas kernels, order_rows(): pl.pallas_call(functools.partial(order_kernel, n_mp, n_dp, piece, steps),...  18.6 us
    ppermute x14, starting transfers between devices, shift(): lax.ppermute(value, axis, [(i, (i + step) % size) for i in range(size)])  15.6 us
    dot_general x1, matrix products, per_device(): lax.dot_general(down_weight[0], live['cotan'], (((1,), (1,)), ((), ())),...  12 us
  transfers between devices with their start and end apart: 54, of which 19 were waited for; matrix products, arithmetic and copies ran while one was open for 16% of the time, Pallas kernels for 8%

profile of v4, /device:TPU:0, one launch (start us, length us, event | category | flops | bytes accessed | tf_op | source)
XLA Modules:
  0.0 303.9 jit_solution(17255965677409012874)
XLA Ops:
  1.9 3.0 collective-permute-start
  5.0 4.6 %collective-permute-start.2 = (bf16[128,2048]{1,0:T(8,128)(2,1)}, bf16[128,2048]{1,0:T(8,128)(2,1)S(1)}, u32[]{:S(2)}, u32[]{:S(2)}) collective-permute-start(bf16[128,2048]{1,0:T(8,128)(2,1)} %param.14), channel_id=1, source_target_pairs={{0,8},{8,16},{16,24},{1,9},{9,17},{17,25},{2,10},{10,18},{18,26},{... | collective-permute-start | bytes 1572872 | tf_op jit(solution)/shard_map/ppermute | solution.py:295
  14.9 2.2 collective-permute-done
  18.2 2.2 collective-permute-done.2
  23.7 2.5 broadcast_select_fusion
  26.2 11.5 %collective-permute-done.4 = bf16[128,2048]{1,0:T(8,128)(2,1)S(1)} collective-permute-done((bf16[128,2048]{1,0:T(8,128)(2,1)S(1)}, bf16[128,2048]{1,0:T(8,128)(2,1)S(1)}, u32[]{:S(2)}, u32[]{:S(2)}) %collective-permute-start.4) | collective-permute-done | bytes 524320 | tf_op jit(solution)/shard_map/ppermute | solution.py:27
  48.0 3.4 %shard_map.157 = bf16[128,2048]{1,0:T(8,128)(2,1)} custom-call(s32[1]{0:T(128)} %bitcast.12._, bf16[128,4096]{1,0:T(8,128)(2,1)} %value_ref), custom_call_target="tpu_custom_call" | custom-call | tf_op jit(solution)/shard_map/pallas_call | solution.py:67
  53.0 8.6 %collective-permute-done.8 = bf16[128,2048]{1,0:T(8,128)(2,1)} collective-permute-done((bf16[128,2048]{1,0:T(8,128)(2,1)S(1)}, bf16[128,2048]{1,0:T(8,128)(2,1)}, u32[]{:S(2)}, u32[]{:S(2)}) %collective-permute-start.8) | collective-permute-done | bytes 524320 | tf_op jit(solution)/shard_map/ppermute | solution.py:27
  64.4 7.1 %collective-permute-start.12 = (bf16[80,2048]{1,0:T(8,128)(2,1)S(1)}, bf16[80,2048]{1,0:T(8,128)(2,1)S(1)}, u32[]{:S(2)}, u32[]{:S(2)}) collective-permute-start(bf16[80,2048]{1,0:T(8,128)(2,1)S(1)} %get-tuple-element.174), channel_id=1, source_target_pairs={{0,8},{8,0},{16,24},{24,16},{1,9},{9,1},{17,25},{25,17},{2,10},{10... | collective-permute-start | bytes 983048 | tf_op jit(solution)/shard_map/ppermute | solution.py:27
  76.3 11.5 %collective-permute-done.15 = bf16[128,2048]{1,0:T(8,128)(2,1)S(1)} collective-permute-done((bf16[128,2048]{1,0:T(8,128)(2,1)S(1)}, bf16[128,2048]{1,0:T(8,128)(2,1)S(1)}, u32[]{:S(2)}, u32[]{:S(2)}) %collective-permute-start.15) | collective-permute-done | bytes 524320 | tf_op jit(solution)/shard_map/ppermute | solution.py:27
  88.2 3.5 %collective-permute-start.17 = (bf16[80,2048]{1,0:T(8,128)(2,1)S(1)}, bf16[80,2048]{1,0:T(8,128)(2,1)S(1)}, u32[]{:S(2)}, u32[]{:S(2)}) collective-permute-start(bf16[80,2048]{1,0:T(8,128)(2,1)S(1)} %get-tuple-element.191), channel_id=1, source_target_pairs={{0,24},{8,16},{16,8},{24,0},{1,25},{9,17},{17,9},{25,1},{2,26},{10... | collective-permute-start | bytes 983048 | tf_op jit(solution)/shard_map/ppermute | solution.py:27
  97.5 3.2 %collective-permute-done.17 = bf16[80,2048]{1,0:T(8,128)(2,1)S(1)} collective-permute-done((bf16[80,2048]{1,0:T(8,128)(2,1)S(1)}, bf16[80,2048]{1,0:T(8,128)(2,1)S(1)}, u32[]{:S(2)}, u32[]{:S(2)}) %collective-permute-start.17) | collective-permute-done | bytes 327712 | tf_op jit(solution)/shard_map/ppermute | solution.py:27
  100.7 5.5 %collective-permute-done.20 = bf16[512,512]{1,0:T(8,128)(2,1)S(1)} collective-permute-done((bf16[512,512]{1,0:T(8,128)(2,1)S(1)}, bf16[512,512]{1,0:T(8,128)(2,1)S(1)}, u32[]{:S(2)}, u32[]{:S(2)}) %collective-permute-start.20) | collective-permute-done | bytes 524320 | tf_op jit(solution)/shard_map/ppermute | solution.py:22
  106.2 4.6 %collective-permute-done.21 = bf16[512,512]{1,0:T(8,128)(2,1)S(1)} collective-permute-done((bf16[512,512]{1,0:T(8,128)(2,1)S(1)}, bf16[512,512]{1,0:T(8,128)(2,1)S(1)}, u32[]{:S(2)}, u32[]{:S(2)}) %collective-permute-start.21) | collective-permute-done | bytes 524320 | tf_op jit(solution)/shard_map/ppermute | solution.py:27
  118.1 10.1 %collective-permute-done.24 = bf16[512,512]{1,0:T(8,128)(2,1)S(1)} collective-permute-done((bf16[512,512]{1,0:T(8,128)(2,1)S(1)}, bf16[512,512]{1,0:T(8,128)(2,1)S(1)}, u32[]{:S(2)}, u32[]{:S(2)}) %collective-permute-start.24) | collective-permute-done | bytes 524320 | tf_op jit(solution)/shard_map/ppermute | solution.py:22
  128.2 12.9 %collective-permute-done.25 = bf16[512,512]{1,0:T(8,128)(2,1)S(1)} collective-permute-done((bf16[512,512]{1,0:T(8,128)(2,1)S(1)}, bf16[512,512]{1,0:T(8,128)(2,1)S(1)}, u32[]{:S(2)}, u32[]{:S(2)}) %collective-permute-start.25) | collective-permute-done | bytes 524320 | tf_op jit(solution)/shard_map/ppermute | solution.py:27
  145.2 2.5 collective-permute-start.28
  147.7 2.5 shard_map.158
  150.2 3.2 %shard_map.159 = bf16[128,2048]{1,0:T(8,128)(2,1)} custom-call(s32[1]{0:T(128)} %bitcast.12._, bf16[128,4096]{1,0:T(8,128)(2,1)} %value_ref.1), custom_call_target="tpu_custom_call" | custom-call | tf_op jit(solution)/shard_map/pallas_call | solution.py:67
  153.4 6.4 %collective-permute-done.28 = bf16[512,512]{1,0:T(8,128)(2,1)} collective-permute-done((bf16[512,512]{1,0:T(8,128)(2,1)}, bf16[512,512]{1,0:T(8,128)(2,1)}, u32[]{:S(2)}, u32[]{:S(2)}) %collective-permute-start.28) | collective-permute-done | bytes 524320 | tf_op jit(solution)/shard_map/ppermute | solution.py:27
  159.8 5.5 %collective-permute-done.26 = bf16[240,2048]{1,0:T(8,128)(2,1)} collective-permute-done((bf16[240,2048]{1,0:T(8,128)(2,1)}, bf16[240,2048]{1,0:T(8,128)(2,1)}, u32[]{:S(2)}, u32[]{:S(2)}) %collective-permute-start.26) | collective-permute-done | bytes 983072 | tf_op jit(solution)/shard_map/ppermute | solution.py:22
  181.1 4.4 %collective-permute-start.37 = (bf16[80,2048]{1,0:T(8,128)(2,1)S(1)}, bf16[80,2048]{1,0:T(8,128)(2,1)S(1)}, u32[]{:S(2)}, u32[]{:S(2)}) collective-permute-start(bf16[80,2048]{1,0:T(8,128)(2,1)S(1)} %get-tuple-element.303), channel_id=1, source_target_pairs={{0,16},{8,24},{16,0},{24,8},{1,17},{9,25},{17,1},{25,9},{2,18},{10... | collective-permute-start | bytes 983048 | tf_op jit(solution)/shard_map/ppermute | solution.py:27
  188.7 12.2 %collective-permute-done.37 = bf16[80,2048]{1,0:T(8,128)(2,1)S(1)} collective-permute-done((bf16[80,2048]{1,0:T(8,128)(2,1)S(1)}, bf16[80,2048]{1,0:T(8,128)(2,1)S(1)}, u32[]{:S(2)}, u32[]{:S(2)}) %collective-permute-start.37) | collective-permute-done | bytes 327712 | tf_op jit(solution)/shard_map/ppermute | solution.py:27
  205.2 2.9 collective-permute-start.40
  208.2 8.7 %shard_map.160.cot_ref = bf16[1280,4096]{1,0:T(8,128)(2,1)} custom-call(s32[130]{0:T(256)S(1)} %pad_add_fusion.at, bf16[15,80,2048]{2,1,0:T(8,128)(2,1)S(1)} %bitcast.93, bf16[15,80,2048]{2,1,0:T(8,128)(2,1)S(1)} %bitcast.94, bf16[15,80,2048]{2,1,0:T(8,128)(2,1)S(1)} %bitcast.95, bf16[15,80,2048]{2,1,0:T(8,128)(2,1)S(1)} %bitcast.96, ...), custom_call_target="tpu_custom_call" | custom-call | tf_op jit(solution)/shard_map/pallas_call | solution.py:114
  216.9 5.4 %collective-permute-done.41 = bf16[40,2048]{1,0:T(8,128)(2,1)S(1)} collective-permute-done((bf16[40,2048]{1,0:T(8,128)(2,1)S(1)}, bf16[40,2048]{1,0:T(8,128)(2,1)S(1)}, u32[]{:S(2)}, u32[]{:S(2)}) %collective-permute-start.41) | collective-permute-done | bytes 163872 | tf_op jit(solution)/shard_map/ppermute | solution.py:22
  226.6 12.0 %fusion.2.back_ref = f32[688,1280]{1,0:T(8,128)} fusion(bf16[1280,4096]{1,0:T(8,128)(2,1)} %shard_map.160.cot_ref, bf16[1,688,4096]{2,1,0:T(8,128)(2,1)S(1)} %bitcast.118), kind=kOutput, calls=%fused_computation.2 | convolution fusion | flops 7214202880 | bytes 19644416 | tf_op jit(solution)/shard_map/dot_general | solution.py:419
  241.8 2.7 shard_map.161.refs_4_
  246.6 4.5 %shard_map.162.refs_4_ = bf16[1280,4096]{1,0:T(8,128)(2,1)} custom-call(s32[50]{0:T(128)S(1)} %pad_add_fusion.4.at, bf16[8,80,2048]{2,1,0:T(8,128)(2,1)S(1)} %bitcast.97, bf16[8,80,2048]{2,1,0:T(8,128)(2,1)S(1)} %bitcast.98, bf16[8,80,2048]{2,1,0:T(8,128)(2,1)S(1)} %bitcast.99, bf16[8,80,2048]{2,1,0:T(8,128)(2,1)S(1)} %bitcast.100, ...), custom_call_target="tpu_custom_call", output_to_operand_aliasing={{}: (5, {})} | custom-call | tf_op jit(solution)/shard_map/pallas_call | solution.py:114
  251.2 2.7 shard_map.163.rows_ref
  253.9 22.5 %shard_map.164 = (bf16[688,1280]{1,0:T(8,128)(2,1)}, bf16[688,1280]{1,0:T(8,128)(2,1)}, bf16[688,1280]{1,0:T(8,128)(2,1)}) custom-call(bf16[1280,4096]{1,0:T(8,128)(2,1)} %shard_map.163.rows_ref, bf16[688,4096]{1,0:T(8,128)(2,1)} %bitcast.111, bf16[688,4096]{1,0:T(8,128)(2,1)} %bitcast.112, f32[688,1280]{1,0:T(8,128)} %fusion.2.back_ref), custom_call_target="tpu_custom_call" | custom-call | tf_op jit(solution)/shard_map/pallas_call | solution.py:152
  276.4 27.6 %shard_map.165 = (bf16[688,4096]{1,0:T(8,128)(2,1)}, bf16[688,4096]{1,0:T(8,128)(2,1)}, bf16[688,4096]{1,0:T(8,128)(2,1)}) custom-call(bf16[1280,4096]{1,0:T(8,128)(2,1)} %shard_map.163.rows_ref, bf16[1280,4096]{1,0:T(8,128)(2,1)} %shard_map.160.cot_ref, bf16[688,1280]{1,0:T(8,128)(2,1)} %get-tuple-element.293.hidden_ref, ...), custom_call_target="tpu_custom_call" | custom-call | tf_op jit(solution)/shard_map/pallas_call | solution.py:175
  (219 shorter events, 80.3 us)
Async XLA Ops:
  0.6 17.6 %collective-permute-start.1 = (bf16[128,2048]{1,0:T(8,128)(2,1)}, bf16[128,2048]{1,0:T(8,128)(2,1)S(1)}, u32[]{:S(2)}, u32[]{:S(2)}) collective-permute-start(bf16[128,2048]{1,0:T(8,128)(2,1)} %param.14), channel_id=1, source_target_pairs={{8,0},{16,8},{24,16},{9,1},{17,9},{25,17},{10,2},{18,10},{26,18},{... | collective-permute-start | bytes 1572872 | tf_op jit(solution)/shard_map/ppermute | solution.py:296
  1.9 15.2 %collective-permute-start = (bf16[128,2048]{1,0:T(8,128)(2,1)}, bf16[128,2048]{1,0:T(8,128)(2,1)S(1)}, u32[]{:S(2)}, u32[]{:S(2)}) collective-permute-start(bf16[128,2048]{1,0:T(8,128)(2,1)} %param.14), channel_id=1, source_target_pairs={{0,2},{1,3},{2,0},{3,1},{4,6},{5,7},{6,4},{7,5},{8,10},{9,11},{10,... | collective-permute-start | bytes 1572872 | tf_op jit(solution)/shard_map/ppermute | solution.py:27
  5.0 15.5 %collective-permute-start.2 = (bf16[128,2048]{1,0:T(8,128)(2,1)}, bf16[128,2048]{1,0:T(8,128)(2,1)S(1)}, u32[]{:S(2)}, u32[]{:S(2)}) collective-permute-start(bf16[128,2048]{1,0:T(8,128)(2,1)} %param.14), channel_id=1, source_target_pairs={{0,8},{8,16},{16,24},{1,9},{9,17},{17,25},{2,10},{10,18},{18,26},{... | collective-permute-start | bytes 1572872 | tf_op jit(solution)/shard_map/ppermute | solution.py:295
  20.4 17.5 %collective-permute-start.5 = (bf16[128,2048]{1,0:T(8,128)(2,1)S(1)}, bf16[128,2048]{1,0:T(8,128)(2,1)}, u32[]{:S(2)}, u32[]{:S(2)}) collective-permute-start(bf16[128,2048]{1,0:T(8,128)(2,1)S(1)} %collective-permute-done.1), channel_id=1, source_target_pairs={{8,0},{16,8},{9,1},{17,9},{10,2},{18,10},{11,3},{19,11},{12,4},{20... | collective-permute-start | bytes 1572872 | tf_op jit(solution)/shard_map/ppermute | solution.py:296
  21.7 16.2 %collective-permute-start.6 = (bf16[128,2048]{1,0:T(8,128)(2,1)S(1)}, bf16[128,2048]{1,0:T(8,128)(2,1)}, u32[]{:S(2)}, u32[]{:S(2)}) collective-permute-start(bf16[128,2048]{1,0:T(8,128)(2,1)S(1)} %collective-permute-done.2), channel_id=1, source_target_pairs={{8,16},{16,24},{9,17},{17,25},{10,18},{18,26},{11,19},{19,27},{12,... | collective-permute-start | bytes 1572872 | tf_op jit(solution)/shard_map/ppermute | solution.py:295
  37.9 26.4 %collective-permute-start.9 = (bf16[128,2048]{1,0:T(8,128)(2,1)}, bf16[128,2048]{1,0:T(8,128)(2,1)S(1)}, u32[]{:S(2)}, u32[]{:S(2)}) collective-permute-start(bf16[128,2048]{1,0:T(8,128)(2,1)} %collective-permute-done.5), channel_id=1, source_target_pairs={{8,0},{9,1},{10,2},{11,3},{12,4},{13,5},{14,6},{15,7}} | collective-permute-start | bytes 1572872 | tf_op jit(solution)/shard_map/ppermute | solution.py:296
  39.2 25.1 %collective-permute-start.11 = (bf16[128,2048]{1,0:T(8,128)(2,1)}, bf16[128,2048]{1,0:T(8,128)(2,1)}, u32[]{:S(2)}, u32[]{:S(2)}) collective-permute-start(bf16[128,2048]{1,0:T(8,128)(2,1)} %collective-permute-done.6), channel_id=1, source_target_pairs={{16,24},{17,25},{18,26},{19,27},{20,28},{21,29},{22,30},{23,31}} | collective-permute-start | bytes 1572872 | tf_op jit(solution)/shard_map/ppermute | solution.py:295
  41.8 21.0 %collective-permute-start.7 = (bf16[256,2048]{1,0:T(8,128)(2,1)S(1)}, bf16[256,2048]{1,0:T(8,128)(2,1)}, u32[]{:S(2)}, u32[]{:S(2)}) collective-permute-start(bf16[256,2048]{1,0:T(8,128)(2,1)S(1)} %pad_maximum_fusion.5), channel_id=1, source_target_pairs={{0,1},{1,0},{2,3},{3,2},{4,5},{5,4},{6,7},{7,6},{8,9},{9,8},{10,11... | collective-permute-start | bytes 3145736 | tf_op jit(solution)/shard_map/ppermute | solution.py:27
  46.0 18.4 %collective-permute-start.10 = (bf16[512,512]{1,0:T(8,128)(2,1)}, bf16[512,512]{1,0:T(8,128)(2,1)}, u32[]{:S(2)}, u32[]{:S(2)}) collective-permute-start(bf16[512,512]{1,0:T(8,128)(2,1)} %convolution_convert_fusion.7), channel_id=1, source_target_pairs={{0,4},{4,0},{1,5},{5,1},{2,6},{6,2},{3,7},{7,3},{8,12},{12,8},{9,1... | collective-permute-start | bytes 1572872 | tf_op jit(solution)/shard_map/ppermute | solution.py:22
  64.4 23.9 %collective-permute-start.12 = (bf16[80,2048]{1,0:T(8,128)(2,1)S(1)}, bf16[80,2048]{1,0:T(8,128)(2,1)S(1)}, u32[]{:S(2)}, u32[]{:S(2)}) collective-permute-start(bf16[80,2048]{1,0:T(8,128)(2,1)S(1)} %get-tuple-element.174), channel_id=1, source_target_pairs={{0,8},{8,0},{16,24},{24,16},{1,9},{9,1},{17,25},{25,17},{2,10},{10... | collective-permute-start | bytes 983048 | tf_op jit(solution)/shard_map/ppermute | solution.py:27
  71.5 16.7 %collective-permute-start.13 = (bf16[80,2048]{1,0:T(8,128)(2,1)S(1)}, bf16[80,2048]{1,0:T(8,128)(2,1)S(1)}, u32[]{:S(2)}, u32[]{:S(2)}) collective-permute-start(bf16[80,2048]{1,0:T(8,128)(2,1)S(1)} %get-tuple-element.175), channel_id=1, source_target_pairs={{0,16},{8,24},{16,0},{24,8},{1,17},{9,25},{17,1},{25,9},{2,18},{10... | collective-permute-start | bytes 983048 | tf_op jit(solution)/shard_map/ppermute | solution.py:27
  72.8 15.5 %collective-permute-start.16 = (bf16[512,512]{1,0:T(8,128)(2,1)S(1)}, bf16[512,512]{1,0:T(8,128)(2,1)S(1)}, u32[]{:S(2)}, u32[]{:S(2)}) collective-permute-start(bf16[512,512]{1,0:T(8,128)(2,1)S(1)} %convolution_convert_fusion.5), channel_id=1, source_target_pairs={{0,4},{4,0},{1,5},{5,1},{2,6},{6,2},{3,7},{7,3},{8,12},{12,8},{9,1... | collective-permute-start | bytes 1572872 | tf_op jit(solution)/shard_map/ppermute | solution.py:22
  94.7 16.0 %collective-permute-start.21 = (bf16[512,512]{1,0:T(8,128)(2,1)S(1)}, bf16[512,512]{1,0:T(8,128)(2,1)S(1)}, u32[]{:S(2)}, u32[]{:S(2)}) collective-permute-start(bf16[512,512]{1,0:T(8,128)(2,1)S(1)} %add_convert_fusion.2), channel_id=1, source_target_pairs={{0,8},{8,0},{16,24},{24,16},{1,9},{9,1},{17,25},{25,17},{2,10},{10... | collective-permute-start | bytes 1572872 | tf_op jit(solution)/shard_map/ppermute | solution.py:27
  94.9 17.2 %collective-permute-start.18 = (bf16[160,2048]{1,0:T(8,128)(2,1)S(1)}, bf16[160,2048]{1,0:T(8,128)(2,1)S(1)}, u32[]{:S(2)}, u32[]{:S(2)}) collective-permute-start(bf16[160,2048]{1,0:T(8,128)(2,1)S(1)} %constant_dynamic-update-slice_fusion), channel_id=1, source_target_pairs={{0,2},{1,3},{2,0},{3,1},{4,6},{5,7},{6,4},{7,5},{8,10},{9,11},{10,... | collective-permute-start | bytes 1966088 | tf_op jit(solution)/shard_map/ppermute | solution.py:27
  113.3 14.9 %collective-permute-start.24 = (bf16[512,512]{1,0:T(8,128)(2,1)S(1)}, bf16[512,512]{1,0:T(8,128)(2,1)S(1)}, u32[]{:S(2)}, u32[]{:S(2)}) collective-permute-start(bf16[512,512]{1,0:T(8,128)(2,1)S(1)} %convolution_convert_fusion.1), channel_id=1, source_target_pairs={{0,4},{4,0},{1,5},{5,1},{2,6},{6,2},{3,7},{7,3},{8,12},{12,8},{9,1... | collective-permute-start | bytes 1572872 | tf_op jit(solution)/shard_map/ppermute | solution.py:22
  114.0 27.1 %collective-permute-start.23 = (bf16[160,2048]{1,0:T(8,128)(2,1)S(1)}, bf16[160,2048]{1,0:T(8,128)(2,1)S(1)}, u32[]{:S(2)}, u32[]{:S(2)}) collective-permute-start(bf16[160,2048]{1,0:T(8,128)(2,1)S(1)} %constant_dynamic-update-slice_fusion.2), channel_id=1, source_target_pairs={{0,2},{1,3},{2,0},{3,1},{4,6},{5,7},{6,4},{7,5},{8,10},{9,11},{10,... | collective-permute-start | bytes 1966088 | tf_op jit(solution)/shard_map/ppermute | solution.py:27
  114.4 26.7 %collective-permute-start.22 = (bf16[160,2048]{1,0:T(8,128)(2,1)S(1)}, bf16[160,2048]{1,0:T(8,128)(2,1)}, u32[]{:S(2)}, u32[]{:S(2)}) collective-permute-start(bf16[160,2048]{1,0:T(8,128)(2,1)S(1)} %constant_dynamic-update-slice_fusion), channel_id=1, source_target_pairs={{0,4},{4,0},{1,5},{5,1},{2,6},{6,2},{3,7},{7,3},{8,12},{12,8},{9,1... | collective-permute-start | bytes 1966088 | tf_op jit(solution)/shard_map/ppermute | solution.py:22
  116.2 24.9 %collective-permute-start.25 = (bf16[512,512]{1,0:T(8,128)(2,1)S(1)}, bf16[512,512]{1,0:T(8,128)(2,1)S(1)}, u32[]{:S(2)}, u32[]{:S(2)}) collective-permute-start(bf16[512,512]{1,0:T(8,128)(2,1)S(1)} %add_convert_fusion.1), channel_id=1, source_target_pairs={{0,16},{8,24},{16,0},{24,8},{1,17},{9,25},{17,1},{25,9},{2,18},{10... | collective-permute-start | bytes 1572872 | tf_op jit(solution)/shard_map/ppermute | solution.py:27
  142.2 23.1 %collective-permute-start.26 = (bf16[240,2048]{1,0:T(8,128)(2,1)}, bf16[240,2048]{1,0:T(8,128)(2,1)}, u32[]{:S(2)}, u32[]{:S(2)}) collective-permute-start(bf16[240,2048]{1,0:T(8,128)(2,1)} %pad_maximum_fusion.8), channel_id=1, source_target_pairs={{0,4},{4,0},{1,5},{5,1},{2,6},{6,2},{3,7},{7,3},{8,12},{12,8},{9,1... | collective-permute-start | bytes 2949128 | tf_op jit(solution)/shard_map/ppermute | solution.py:22
  142.8 17.1 %collective-permute-start.27 = (bf16[160,2048]{1,0:T(8,128)(2,1)}, bf16[160,2048]{1,0:T(8,128)(2,1)}, u32[]{:S(2)}, u32[]{:S(2)}) collective-permute-start(bf16[160,2048]{1,0:T(8,128)(2,1)} %collective-permute-done.22), channel_id=1, source_target_pairs={{0,2},{1,3},{2,0},{3,1},{4,6},{5,7},{6,4},{7,5},{8,10},{9,11},{10,... | collective-permute-start | bytes 1966088 | tf_op jit(solution)/shard_map/ppermute | solution.py:27
  145.2 14.6 %collective-permute-start.28 = (bf16[512,512]{1,0:T(8,128)(2,1)}, bf16[512,512]{1,0:T(8,128)(2,1)}, u32[]{:S(2)}, u32[]{:S(2)}) collective-permute-start(bf16[512,512]{1,0:T(8,128)(2,1)} %add_convert_fusion), channel_id=1, source_target_pairs={{0,24},{8,16},{16,8},{24,0},{1,25},{9,17},{17,9},{25,1},{2,26},{10... | collective-permute-start | bytes 1572872 | tf_op jit(solution)/shard_map/ppermute | solution.py:27
  180.4 20.6 %collective-permute-start.35 = (bf16[1200,2048]{1,0:T(8,128)(2,1)S(1)}, bf16[1200,2048]{1,0:T(8,128)(2,1)S(1)}, u32[]{:S(2)}, u32[]{:S(2)}) collective-permute-start(bf16[1200,2048]{1,0:T(8,128)(2,1)S(1)} %slice_dynamic-update-slice_fusion.1), channel_id=1, source_target_pairs={{0,1},{1,0},{2,3},{3,2},{4,5},{5,4},{6,7},{7,6},{8,9},{9,8},{10,11... | collective-permute-start | bytes 14745608 | tf_op jit(solution)/shard_map/ppermute | solution.py:27
  181.1 19.8 %collective-permute-start.37 = (bf16[80,2048]{1,0:T(8,128)(2,1)S(1)}, bf16[80,2048]{1,0:T(8,128)(2,1)S(1)}, u32[]{:S(2)}, u32[]{:S(2)}) collective-permute-start(bf16[80,2048]{1,0:T(8,128)(2,1)S(1)} %get-tuple-element.303), channel_id=1, source_target_pairs={{0,16},{8,24},{16,0},{24,8},{1,17},{9,25},{17,1},{25,9},{2,18},{10... | collective-permute-start | bytes 983048 | tf_op jit(solution)/shard_map/ppermute | solution.py:27
  185.5 15.4 %collective-permute-start.36 = (bf16[80,2048]{1,0:T(8,128)(2,1)S(1)}, bf16[80,2048]{1,0:T(8,128)(2,1)S(1)}, u32[]{:S(2)}, u32[]{:S(2)}) collective-permute-start(bf16[80,2048]{1,0:T(8,128)(2,1)S(1)} %get-tuple-element.304), channel_id=1, source_target_pairs={{0,8},{8,0},{16,24},{24,16},{1,9},{9,1},{17,25},{25,17},{2,10},{10... | collective-permute-start | bytes 983048 | tf_op jit(solution)/shard_map/ppermute | solution.py:27
  185.8 15.2 %collective-permute-start.39 = (bf16[80,2048]{1,0:T(8,128)(2,1)S(1)}, bf16[80,2048]{1,0:T(8,128)(2,1)S(1)}, u32[]{:S(2)}, u32[]{:S(2)}) collective-permute-start(bf16[80,2048]{1,0:T(8,128)(2,1)S(1)} %get-tuple-element.263), channel_id=1, source_target_pairs={{0,2},{1,3},{2,0},{3,1},{4,6},{5,7},{6,4},{7,5},{8,10},{9,11},{10,... | collective-permute-start | bytes 983048 | tf_op jit(solution)/shard_map/ppermute | solution.py:27
  201.0 21.3 %collective-permute-start.44 = (bf16[160,2048]{1,0:T(8,128)(2,1)S(1)}, bf16[160,2048]{1,0:T(8,128)(2,1)S(1)}, u32[]{:S(2)}, u32[]{:S(2)}) collective-permute-start(bf16[160,2048]{1,0:T(8,128)(2,1)S(1)} %constant_dynamic-update-slice_fusion.15), channel_id=1, source_target_pairs={{0,2},{1,3},{2,0},{3,1},{4,6},{5,7},{6,4},{7,5},{8,10},{9,11},{10,... | collective-permute-start | bytes 1966088 | tf_op jit(solution)/shard_map/ppermute | solution.py:27
  202.5 19.8 %collective-permute-start.43 = (bf16[160,2048]{1,0:T(8,128)(2,1)S(1)}, bf16[160,2048]{1,0:T(8,128)(2,1)S(1)}, u32[]{:S(2)}, u32[]{:S(2)}) collective-permute-start(bf16[160,2048]{1,0:T(8,128)(2,1)S(1)} %constant_dynamic-update-slice_fusion.15), channel_id=1, source_target_pairs={{0,4},{4,0},{1,5},{5,1},{2,6},{6,2},{3,7},{7,3},{8,12},{12,8},{9,1... | collective-permute-start | bytes 1966088 | tf_op jit(solution)/shard_map/ppermute | solution.py:22
  204.3 17.9 %collective-permute-start.42 = (bf16[40,2048]{1,0:T(8,128)(2,1)S(1)}, bf16[40,2048]{1,0:T(8,128)(2,1)S(1)}, u32[]{:S(2)}, u32[]{:S(2)}) collective-permute-start(bf16[40,2048]{1,0:T(8,128)(2,1)S(1)} %slice.131), channel_id=1, source_target_pairs={{0,2},{1,3},{2,0},{3,1},{4,6},{5,7},{6,4},{7,5},{8,10},{9,11},{10,... | collective-permute-start | bytes 491528 | tf_op jit(solution)/shard_map/ppermute | solution.py:27
  204.8 17.5 %collective-permute-start.41 = (bf16[40,2048]{1,0:T(8,128)(2,1)S(1)}, bf16[40,2048]{1,0:T(8,128)(2,1)S(1)}, u32[]{:S(2)}, u32[]{:S(2)}) collective-permute-start(bf16[40,2048]{1,0:T(8,128)(2,1)S(1)} %slice.130), channel_id=1, source_target_pairs={{0,4},{4,0},{1,5},{5,1},{2,6},{6,2},{3,7},{7,3},{8,12},{12,8},{9,1... | collective-permute-start | bytes 491528 | tf_op jit(solution)/shard_map/ppermute | solution.py:22
  205.2 17.1 %collective-permute-start.40 = (bf16[80,2048]{1,0:T(8,128)(2,1)S(1)}, bf16[80,2048]{1,0:T(8,128)(2,1)S(1)}, u32[]{:S(2)}, u32[]{:S(2)}) collective-permute-start(bf16[80,2048]{1,0:T(8,128)(2,1)S(1)} %get-tuple-element.262), channel_id=1, source_target_pairs={{0,24},{8,16},{16,8},{24,0},{1,25},{9,17},{17,9},{25,1},{2,26},{10... | collective-permute-start | bytes 983048 | tf_op jit(solution)/shard_map/ppermute | solution.py:27
  222.3 16.5 %collective-permute-start.49 = (bf16[80,2048]{1,0:T(8,128)(2,1)S(1)}, bf16[80,2048]{1,0:T(8,128)(2,1)S(1)}, u32[]{:S(2)}, u32[]{:S(2)}) collective-permute-start(bf16[80,2048]{1,0:T(8,128)(2,1)S(1)} %collective-permute-done.40), channel_id=1, source_target_pairs={{0,2},{1,3},{2,0},{3,1},{4,6},{5,7},{6,4},{7,5},{8,10},{9,11},{10,... | collective-permute-start | bytes 983048 | tf_op jit(solution)/shard_map/ppermute | solution.py:27
  223.0 15.8 %collective-permute-start.48 = (bf16[80,2048]{1,0:T(8,128)(2,1)S(1)}, bf16[80,2048]{1,0:T(8,128)(2,1)S(1)}, u32[]{:S(2)}, u32[]{:S(2)}) collective-permute-start(bf16[80,2048]{1,0:T(8,128)(2,1)S(1)} %collective-permute-done.40), channel_id=1, source_target_pairs={{0,4},{4,0},{1,5},{5,1},{2,6},{6,2},{3,7},{7,3},{8,12},{12,8},{9,1... | collective-permute-start | bytes 983048 | tf_op jit(solution)/shard_map/ppermute | solution.py:22
  (38 other events, 334.7 us)

commit v5 on v4

--- a/solution.py
+++ b/solution.py
@@ -125,7 +125,8 @@
     )(table, *[value for _, value, _ in sources], *more)
 
 
-def forward_kernel(rows_ref, gate_ref, up_ref, back_ref, hidden_ref, d_gate_ref, d_up_ref):
+def forward_kernel(rows_ref, gate_ref, up_ref, back_ref, *refs):
+    hidden_ref, d_gate_ref, d_up_ref = refs[-3:]
     contract = (((1,), (1,)), ((), ()))
     rows = rows_ref[...]
     pre_gate = lax.dot_general(gate_ref[...], rows, contract, preferred_element_type=jnp.float32)
@@ -143,20 +144,22 @@
     return next((t for t in range(most, 127, -128) if size % t == 0), size)
 
 
-def forward(rows, gate_t, up_t, back):
+def forward(rows, gate_t, up_t, back, first, last, before=()):
     count, width = rows.shape
     units = gate_t.shape[0]
     tile = fitting(count, 256)
     weights = pl.BlockSpec((units, width), lambda i: (0, 0))
-    part = pl.BlockSpec((units, tile), lambda i: (0, i))
+    part = pl.BlockSpec((units, tile), lambda i: (0, first + i))
     return pl.pallas_call(
         forward_kernel,
-        grid=(count // tile,),
-        in_specs=[pl.BlockSpec((tile, width), lambda i: (i, 0)), weights, weights, part],
+        grid=(last - first,),
+        in_specs=[pl.BlockSpec((tile, width), lambda i: (first + i, 0)), weights, weights, part]
+        + [pl.BlockSpec(memory_space=pltpu.HBM)] * len(before),
         out_specs=[part] * 3,
-        out_shape=[jax.ShapeDtypeStruct((units, count), jnp.bfloat16)] * 3,
+        out_shape=[pltpu.HBM((units, count), jnp.bfloat16)] * 3,
+        input_output_aliases={4 + i: i for i in range(len(before))},
         compiler_params=pltpu.CompilerParams(vmem_limit_bytes=56 << 20),
-    )(rows, gate_t, up_t, back)
+    )(rows, gate_t, up_t, back, *before)
 
 
 def gradient_kernel(rows_ref, cot_ref, hidden_ref, d_gate_ref, d_up_ref, gate_ref, up_ref, down_ref):
@@ -395,9 +398,15 @@
                 sources.append((t, value, at))
         live["in"] = order_rows(sources, [slots_of], n_dp, piece, first, n_dp * n_br, live.get("in"))
 
+    tile = fitting(n_dp * n_br * capacity, 256)
+    early = n_dp * capacity // tile
     for r in range(len(groups) + 2):
         if 0 <= r - 3 < len(groups):
             order_group(r - 3)
+        if r == 3 and early:
+            live["made0"], live["made1"], live["made2"] = forward(
+                live["in"], gate_weight[0].T, up_weight[0].T, live["back"], 0, early
+            )
         cascade("in", r)
         if r == 0:
             for c, block in enumerate(core_flips(live.pop("cota"))):
@@ -423,7 +432,10 @@
     cotan_rows, back_grad = live.pop("cotan"), live.pop("back")
     order_group(len(groups) - 1)
     tokens_in = live.pop("in")
-    hidden, d_gate, d_up = forward(tokens_in, gate_weight[0].T, up_weight[0].T, back_grad)
+    hidden, d_gate, d_up = forward(
+        tokens_in, gate_weight[0].T, up_weight[0].T, back_grad, early, tokens_in.shape[0] // tile,
+        [live.pop(f"made{i}") for i in range(3)] if early else [],
+    )
     grad_gate, grad_up, grad_down = gradients(tokens_in, cotan_rows, hidden, d_gate, d_up)
     return (grad_gate.T[None], grad_up.T[None], grad_down[None])
 

time: 305 us -> 320 us (1.049)
  waiting for transfers between devices: 109 us -> 119 us
  Pallas kernels: 77.8 us -> 83.5 us
  starting transfers between devices: 64.7 us -> 60.5 us
    ppermute x34, waiting for transfers between devices: 76.7 us -> 89.3 us  [flip(): return lax.ppermute(value, axis, [(i, i ^ mask) for i in range(size)])]
    pallas_call x1 -> x2, Pallas kernels: 22.5 us -> 28.4 us  [forward(): pl.pallas_call(forward_kernel, grid=(last - first,), in_specs=[pl.BlockSp...]
    ppermute x14, waiting for transfers between devices: 30.3 us -> 26 us  [shift(): lax.ppermute(value, axis, [(i, (i + step) % size) for i in range(size)])]
  transfers between devices with their start and end apart: 54 -> 54, of which waited for: 19 -> 20; matrix products, arithmetic and copies ran while one was open for 16% -> 15% of each run, Pallas kernels for 8% -> 11%
where the time goes in v5:
time: 320 us; the launch traced here: 319 us
  waiting for transfers between devices  119 us (37%)
  Pallas kernels  83.5 us (26%)
  starting transfers between devices  60.5 us (19%)
  matrix products  27.5 us (9%)
  other arithmetic  17.2 us (5%)
  local copies, waits for them, and re-layouts  10 us (3%)
    ppermute x34, waiting for transfers between devices, flip(): return lax.ppermute(value, axis, [(i, i ^ mask) for i in range(size)])  89.3 us
    ppermute x34, starting transfers between devices, flip(): return lax.ppermute(value, axis, [(i, i ^ mask) for i in range(size)])  35.7 us
    pallas_call x2, Pallas kernels, forward(): pl.pallas_call(forward_kernel, grid=(last - first,), in_specs=[pl.BlockSp...  28.4 us
    pallas_call x1, Pallas kernels, gradients(): pl.pallas_call(gradient_kernel, grid=(width // tile,), in_specs=[columns,...  27.6 us
    ppermute x14, waiting for transfers between devices, shift(): lax.ppermute(value, axis, [(i, (i + step) % size) for i in range(size)])  26 us
    pallas_call x4, Pallas kernels, order_rows(): pl.pallas_call(functools.partial(order_kernel, n_mp, n_dp, piece, steps),...  18.7 us
    dot_general x1, matrix products, per_device(): lax.dot_general(down_weight[0], live['cotan'], (((1,), (1,)), ((), ())),...  13.8 us
    ppermute x14, starting transfers between devices, shift(): lax.ppermute(value, axis, [(i, (i + step) % size) for i in range(size)])  13.5 us
  transfers between devices with their start and end apart: 54, of which 20 were waited for; matrix products, arithmetic and copies ran while one was open for 15% of the time, Pallas kernels for 11%

profile of v5, /device:TPU:0, one launch (start us, length us, event | category | flops | bytes accessed | tf_op | source)
XLA Modules:
  0.0 319.1 jit_solution(13854807990178120196)
XLA Ops:
  0.6 3.0 collective-permute-start
  4.9 4.6 %collective-permute-start.2 = (bf16[128,2048]{1,0:T(8,128)(2,1)}, bf16[128,2048]{1,0:T(8,128)(2,1)S(1)}, u32[]{:S(2)}, u32[]{:S(2)}) collective-permute-start(bf16[128,2048]{1,0:T(8,128)(2,1)} %param.14), channel_id=1, source_target_pairs={{0,8},{8,16},{16,24},{1,9},{9,17},{17,25},{2,10},{10,18},{18,26},{... | collective-permute-start | bytes 1572872 | tf_op jit(solution)/shard_map/ppermute | solution.py:298
  26.2 11.5 %collective-permute-done.4 = bf16[128,2048]{1,0:T(8,128)(2,1)S(1)} collective-permute-done((bf16[128,2048]{1,0:T(8,128)(2,1)S(1)}, bf16[128,2048]{1,0:T(8,128)(2,1)S(1)}, u32[]{:S(2)}, u32[]{:S(2)}) %collective-permute-start.4) | collective-permute-done | bytes 524320 | tf_op jit(solution)/shard_map/ppermute | solution.py:27
  48.0 3.2 shard_map.157
  52.8 9.1 %collective-permute-done.8 = bf16[128,2048]{1,0:T(8,128)(2,1)} collective-permute-done((bf16[128,2048]{1,0:T(8,128)(2,1)S(1)}, bf16[128,2048]{1,0:T(8,128)(2,1)}, u32[]{:S(2)}, u32[]{:S(2)}) %collective-permute-start.8) | collective-permute-done | bytes 524320 | tf_op jit(solution)/shard_map/ppermute | solution.py:27
  68.6 6.0 %collective-permute-start.12 = (bf16[80,2048]{1,0:T(8,128)(2,1)S(1)}, bf16[80,2048]{1,0:T(8,128)(2,1)S(1)}, u32[]{:S(2)}, u32[]{:S(2)}) collective-permute-start(bf16[80,2048]{1,0:T(8,128)(2,1)S(1)} %get-tuple-element.183), channel_id=1, source_target_pairs={{0,8},{8,0},{16,24},{24,16},{1,9},{9,1},{17,25},{25,17},{2,10},{10... | collective-permute-start | bytes 983048 | tf_op jit(solution)/shard_map/ppermute | solution.py:27
  76.0 6.3 %collective-permute-done.15 = bf16[128,2048]{1,0:T(8,128)(2,1)S(1)} collective-permute-done((bf16[128,2048]{1,0:T(8,128)(2,1)S(1)}, bf16[128,2048]{1,0:T(8,128)(2,1)S(1)}, u32[]{:S(2)}, u32[]{:S(2)}) %collective-permute-start.15) | collective-permute-done | bytes 524320 | tf_op jit(solution)/shard_map/ppermute | solution.py:27
  82.7 5.5 %collective-permute-done.12 = bf16[80,2048]{1,0:T(8,128)(2,1)S(1)} collective-permute-done((bf16[80,2048]{1,0:T(8,128)(2,1)S(1)}, bf16[80,2048]{1,0:T(8,128)(2,1)S(1)}, u32[]{:S(2)}, u32[]{:S(2)}) %collective-permute-start.12) | collective-permute-done | bytes 327712 | tf_op jit(solution)/shard_map/ppermute | solution.py:27
  88.1 4.0 %collective-permute-done.13 = bf16[80,2048]{1,0:T(8,128)(2,1)S(1)} collective-permute-done((bf16[80,2048]{1,0:T(8,128)(2,1)S(1)}, bf16[80,2048]{1,0:T(8,128)(2,1)S(1)}, u32[]{:S(2)}, u32[]{:S(2)}) %collective-permute-start.13) | collective-permute-done | bytes 327712 | tf_op jit(solution)/shard_map/ppermute | solution.py:27
  100.1 12.2 %collective-permute-done.17 = bf16[80,2048]{1,0:T(8,128)(2,1)S(1)} collective-permute-done((bf16[80,2048]{1,0:T(8,128)(2,1)S(1)}, bf16[80,2048]{1,0:T(8,128)(2,1)S(1)}, u32[]{:S(2)}, u32[]{:S(2)}) %collective-permute-start.17) | collective-permute-done | bytes 327712 | tf_op jit(solution)/shard_map/ppermute | solution.py:27
  113.3 2.9 collective-permute-start.25
  121.4 17.5 %collective-permute-done.25 = bf16[512,512]{1,0:T(8,128)(2,1)S(1)} collective-permute-done((bf16[512,512]{1,0:T(8,128)(2,1)S(1)}, bf16[512,512]{1,0:T(8,128)(2,1)S(1)}, u32[]{:S(2)}, u32[]{:S(2)}) %collective-permute-start.25) | collective-permute-done | bytes 524320 | tf_op jit(solution)/shard_map/ppermute | solution.py:27
  138.9 4.5 %collective-permute-done.24 = bf16[512,512]{1,0:T(8,128)(2,1)S(1)} collective-permute-done((bf16[512,512]{1,0:T(8,128)(2,1)S(1)}, bf16[512,512]{1,0:T(8,128)(2,1)S(1)}, u32[]{:S(2)}, u32[]{:S(2)}) %collective-permute-start.24) | collective-permute-done | bytes 524320 | tf_op jit(solution)/shard_map/ppermute | solution.py:22
  147.3 2.6 collective-permute-start.28
  149.9 3.1 shard_map.159
  153.0 2.5 shard_map.158
  155.5 5.2 %collective-permute-done.28 = bf16[512,512]{1,0:T(8,128)(2,1)} collective-permute-done((bf16[512,512]{1,0:T(8,128)(2,1)}, bf16[512,512]{1,0:T(8,128)(2,1)}, u32[]{:S(2)}, u32[]{:S(2)}) %collective-permute-start.28) | collective-permute-done | bytes 524320 | tf_op jit(solution)/shard_map/ppermute | solution.py:27
  160.7 5.4 %collective-permute-done.26 = bf16[240,2048]{1,0:T(8,128)(2,1)} collective-permute-done((bf16[240,2048]{1,0:T(8,128)(2,1)}, bf16[240,2048]{1,0:T(8,128)(2,1)}, u32[]{:S(2)}, u32[]{:S(2)}) %collective-permute-start.26) | collective-permute-done | bytes 983072 | tf_op jit(solution)/shard_map/ppermute | solution.py:22
  176.8 8.1 %collective-permute-done.32 = bf16[80,2048]{1,0:T(8,128)(2,1)S(1)} collective-permute-done((bf16[80,2048]{1,0:T(8,128)(2,1)S(1)}, bf16[80,2048]{1,0:T(8,128)(2,1)S(1)}, u32[]{:S(2)}, u32[]{:S(2)}) %collective-permute-start.32) | collective-permute-done | bytes 327712 | tf_op jit(solution)/shard_map/ppermute | solution.py:22
  185.5 3.3 %collective-permute-done.34 = f32[1,128]{1,0:T(1,128)S(1)} collective-permute-done((f32[1,128]{1,0:T(1,128)S(1)}, f32[1,128]{1,0:T(1,128)S(1)}, u32[]{:S(2)}, u32[]{:S(2)}) %collective-permute-start.34) | collective-permute-done | bytes 544 | tf_op jit(solution)/shard_map/ppermute | solution.py:22
  189.5 3.6 %collective-permute-start.36 = (bf16[80,2048]{1,0:T(8,128)(2,1)S(1)}, bf16[80,2048]{1,0:T(8,128)(2,1)S(1)}, u32[]{:S(2)}, u32[]{:S(2)}) collective-permute-start(bf16[80,2048]{1,0:T(8,128)(2,1)S(1)} %get-tuple-element.322), channel_id=1, source_target_pairs={{0,8},{8,0},{16,24},{24,16},{1,9},{9,1},{17,25},{25,17},{2,10},{10... | collective-permute-start | bytes 983048 | tf_op jit(solution)/shard_map/ppermute | solution.py:27
  196.1 11.6 %collective-permute-done.36 = bf16[80,2048]{1,0:T(8,128)(2,1)S(1)} collective-permute-done((bf16[80,2048]{1,0:T(8,128)(2,1)S(1)}, bf16[80,2048]{1,0:T(8,128)(2,1)S(1)}, u32[]{:S(2)}, u32[]{:S(2)}) %collective-permute-start.36) | collective-permute-done | bytes 327712 | tf_op jit(solution)/shard_map/ppermute | solution.py:27
  207.7 3.2 %collective-permute-done.37 = bf16[80,2048]{1,0:T(8,128)(2,1)S(1)} collective-permute-done((bf16[80,2048]{1,0:T(8,128)(2,1)S(1)}, bf16[80,2048]{1,0:T(8,128)(2,1)S(1)}, u32[]{:S(2)}, u32[]{:S(2)}) %collective-permute-start.37) | collective-permute-done | bytes 327712 | tf_op jit(solution)/shard_map/ppermute | solution.py:27
  217.2 8.7 %shard_map.160.cot_ref = bf16[1280,4096]{1,0:T(8,128)(2,1)} custom-call(s32[130]{0:T(256)S(1)} %pad_add_fusion.at, bf16[15,80,2048]{2,1,0:T(8,128)(2,1)S(1)} %bitcast.93, bf16[15,80,2048]{2,1,0:T(8,128)(2,1)S(1)} %bitcast.94, bf16[15,80,2048]{2,1,0:T(8,128)(2,1)S(1)} %bitcast.95, bf16[15,80,2048]{2,1,0:T(8,128)(2,1)S(1)} %bitcast.96, ...), custom_call_target="tpu_custom_call" | custom-call | tf_op jit(solution)/shard_map/pallas_call | solution.py:114
  225.9 4.7 %collective-permute-done.41 = bf16[40,2048]{1,0:T(8,128)(2,1)S(1)} collective-permute-done((bf16[40,2048]{1,0:T(8,128)(2,1)S(1)}, bf16[40,2048]{1,0:T(8,128)(2,1)S(1)}, u32[]{:S(2)}, u32[]{:S(2)}) %collective-permute-start.41) | collective-permute-done | bytes 163872 | tf_op jit(solution)/shard_map/ppermute | solution.py:22
  236.4 13.8 %fusion.2.back_ref = f32[688,1280]{1,0:T(8,128)} fusion(bf16[1280,4096]{1,0:T(8,128)(2,1)} %shard_map.160.cot_ref, bf16[1,688,4096]{2,1,0:T(8,128)(2,1)} %param.20), kind=kOutput, calls=%fused_computation.2 | convolution fusion | flops 7214202880 | bytes 19644416 | tf_op jit(solution)/shard_map/dot_general | solution.py:428
  252.4 2.7 shard_map.161.rows_ref.refs_4_
  255.1 9.2 %shard_map.162 = (bf16[688,1280]{1,0:T(8,128)(2,1)}, bf16[688,1280]{1,0:T(8,128)(2,1)}, bf16[688,1280]{1,0:T(8,128)(2,1)}) custom-call(bf16[1280,4096]{1,0:T(8,128)(2,1)} %shard_map.161.rows_ref.refs_4_, bf16[688,4096]{1,0:T(8,128)(2,1)} %bitcast.111, bf16[688,4096]{1,0:T(8,128)(2,1)} %bitcast.113, f32[688,1280]{1,0:T(8,128)} %fusion.2.back_ref), custom_call_target="tpu_custom_call" | custom-call | tf_op jit(solution)/shard_map/pallas_call | solution.py:153
  265.1 4.6 %shard_map.163.refs_4_ = bf16[1280,4096]{1,0:T(8,128)(2,1)} custom-call(s32[50]{0:T(128)S(1)} %pad_add_fusion.4.at, bf16[8,80,2048]{2,1,0:T(8,128)(2,1)S(1)} %bitcast.97, bf16[8,80,2048]{2,1,0:T(8,128)(2,1)S(1)} %bitcast.98, bf16[8,80,2048]{2,1,0:T(8,128)(2,1)S(1)} %bitcast.99, bf16[8,80,2048]{2,1,0:T(8,128)(2,1)S(1)} %bitcast.100, ...), custom_call_target="tpu_custom_call", output_to_operand_aliasing={{}: (5, {})} | custom-call | tf_op jit(solution)/shard_map/pallas_call | solution.py:114
  269.6 2.7 shard_map.164.rows_ref
  272.3 19.2 %shard_map.165 = (bf16[688,1280]{1,0:T(8,128)(2,1)}, bf16[688,1280]{1,0:T(8,128)(2,1)}, bf16[688,1280]{1,0:T(8,128)(2,1)}) custom-call(bf16[1280,4096]{1,0:T(8,128)(2,1)} %shard_map.164.rows_ref, bf16[688,4096]{1,0:T(8,128)(2,1)} %bitcast.112, bf16[688,4096]{1,0:T(8,128)(2,1)} %bitcast.114, ...), custom_call_target="tpu_custom_call", output_to_operand_aliasing={{0}: (4, {}), {1}: (5, {}), {2}: (6, {})} | custom-call | tf_op jit(solution)/shard_map/pallas_call | solution.py:153
  291.5 27.6 %shard_map.166 = (bf16[688,4096]{1,0:T(8,128)(2,1)}, bf16[688,4096]{1,0:T(8,128)(2,1)}, bf16[688,4096]{1,0:T(8,128)(2,1)}) custom-call(bf16[1280,4096]{1,0:T(8,128)(2,1)} %shard_map.164.rows_ref, bf16[1280,4096]{1,0:T(8,128)(2,1)} %shard_map.160.cot_ref, bf16[688,1280]{1,0:T(8,128)(2,1)} %get-tuple-element.311.hidden_ref, ...), custom_call_target="tpu_custom_call" | custom-call | tf_op jit(solution)/shard_map/pallas_call | solution.py:178
  (217 shorter events, 85.7 us)
Async XLA Ops:
  20.4 17.3 %collective-permute-start.3 = (bf16[256,2048]{1,0:T(8,128)(2,1)S(1)}, bf16[256,2048]{1,0:T(8,128)(2,1)S(1)}, u32[]{:S(2)}, u32[]{:S(2)}) collective-permute-start(bf16[256,2048]{1,0:T(8,128)(2,1)S(1)} %pad_maximum_fusion.4), channel_id=1, source_target_pairs={{0,1},{1,0},{2,3},{3,2},{4,5},{5,4},{6,7},{7,6},{8,9},{9,8},{10,11... | collective-permute-start | bytes 3145736 | tf_op jit(solution)/shard_map/ppermute | solution.py:27
  20.4 17.4 %collective-permute-start.5 = (bf16[128,2048]{1,0:T(8,128)(2,1)S(1)}, bf16[128,2048]{1,0:T(8,128)(2,1)}, u32[]{:S(2)}, u32[]{:S(2)}) collective-permute-start(bf16[128,2048]{1,0:T(8,128)(2,1)S(1)} %collective-permute-done.1), channel_id=1, source_target_pairs={{8,0},{16,8},{9,1},{17,9},{10,2},{18,10},{11,3},{19,11},{12,4},{20... | collective-permute-start | bytes 1572872 | tf_op jit(solution)/shard_map/ppermute | solution.py:299
  21.7 16.2 %collective-permute-start.6 = (bf16[128,2048]{1,0:T(8,128)(2,1)S(1)}, bf16[128,2048]{1,0:T(8,128)(2,1)}, u32[]{:S(2)}, u32[]{:S(2)}) collective-permute-start(bf16[128,2048]{1,0:T(8,128)(2,1)S(1)} %collective-permute-done.2), channel_id=1, source_target_pairs={{8,16},{16,24},{9,17},{17,25},{10,18},{18,26},{11,19},{19,27},{12,... | collective-permute-start | bytes 1572872 | tf_op jit(solution)/shard_map/ppermute | solution.py:298
  40.0 24.6 %collective-permute-start.10 = (bf16[512,512]{1,0:T(8,128)(2,1)}, bf16[512,512]{1,0:T(8,128)(2,1)S(1)}, u32[]{:S(2)}, u32[]{:S(2)}) collective-permute-start(bf16[512,512]{1,0:T(8,128)(2,1)} %convolution_convert_fusion.7), channel_id=1, source_target_pairs={{0,4},{4,0},{1,5},{5,1},{2,6},{6,2},{3,7},{7,3},{8,12},{12,8},{9,1... | collective-permute-start | bytes 1572872 | tf_op jit(solution)/shard_map/ppermute | solution.py:22
  41.4 23.1 %collective-permute-start.11 = (bf16[128,2048]{1,0:T(8,128)(2,1)}, bf16[128,2048]{1,0:T(8,128)(2,1)}, u32[]{:S(2)}, u32[]{:S(2)}) collective-permute-start(bf16[128,2048]{1,0:T(8,128)(2,1)} %collective-permute-done.6), channel_id=1, source_target_pairs={{16,24},{17,25},{18,26},{19,27},{20,28},{21,29},{22,30},{23,31}} | collective-permute-start | bytes 1572872 | tf_op jit(solution)/shard_map/ppermute | solution.py:298
  42.9 21.7 %collective-permute-start.9 = (bf16[128,2048]{1,0:T(8,128)(2,1)}, bf16[128,2048]{1,0:T(8,128)(2,1)}, u32[]{:S(2)}, u32[]{:S(2)}) collective-permute-start(bf16[128,2048]{1,0:T(8,128)(2,1)} %collective-permute-done.5), channel_id=1, source_target_pairs={{8,0},{9,1},{10,2},{11,3},{12,4},{13,5},{14,6},{15,7}} | collective-permute-start | bytes 1572872 | tf_op jit(solution)/shard_map/ppermute | solution.py:299
  45.3 17.7 %collective-permute-start.7 = (bf16[256,2048]{1,0:T(8,128)(2,1)S(1)}, bf16[256,2048]{1,0:T(8,128)(2,1)}, u32[]{:S(2)}, u32[]{:S(2)}) collective-permute-start(bf16[256,2048]{1,0:T(8,128)(2,1)S(1)} %pad_maximum_fusion.5), channel_id=1, source_target_pairs={{0,1},{1,0},{2,3},{3,2},{4,5},{5,4},{6,7},{7,6},{8,9},{9,8},{10,11... | collective-permute-start | bytes 3145736 | tf_op jit(solution)/shard_map/ppermute | solution.py:27
  66.2 25.9 %collective-permute-start.16 = (bf16[512,512]{1,0:T(8,128)(2,1)S(1)}, bf16[512,512]{1,0:T(8,128)(2,1)S(1)}, u32[]{:S(2)}, u32[]{:S(2)}) collective-permute-start(bf16[512,512]{1,0:T(8,128)(2,1)S(1)} %convolution_convert_fusion.5), channel_id=1, source_target_pairs={{0,4},{4,0},{1,5},{5,1},{2,6},{6,2},{3,7},{7,3},{8,12},{12,8},{9,1... | collective-permute-start | bytes 1572872 | tf_op jit(solution)/shard_map/ppermute | solution.py:22
  66.8 15.7 %collective-permute-start.14 = (bf16[256,2048]{1,0:T(8,128)(2,1)S(1)}, bf16[256,2048]{1,0:T(8,128)(2,1)S(1)}, u32[]{:S(2)}, u32[]{:S(2)}) collective-permute-start(bf16[256,2048]{1,0:T(8,128)(2,1)S(1)} %pad_maximum_fusion.6), channel_id=1, source_target_pairs={{0,1},{1,0},{2,3},{3,2},{4,5},{5,4},{6,7},{7,6},{8,9},{9,8},{10,11... | collective-permute-start | bytes 3145736 | tf_op jit(solution)/shard_map/ppermute | solution.py:27
  68.6 19.6 %collective-permute-start.12 = (bf16[80,2048]{1,0:T(8,128)(2,1)S(1)}, bf16[80,2048]{1,0:T(8,128)(2,1)S(1)}, u32[]{:S(2)}, u32[]{:S(2)}) collective-permute-start(bf16[80,2048]{1,0:T(8,128)(2,1)S(1)} %get-tuple-element.183), channel_id=1, source_target_pairs={{0,8},{8,0},{16,24},{24,16},{1,9},{9,1},{17,25},{25,17},{2,10},{10... | collective-permute-start | bytes 983048 | tf_op jit(solution)/shard_map/ppermute | solution.py:27
  74.6 17.5 %collective-permute-start.13 = (bf16[80,2048]{1,0:T(8,128)(2,1)S(1)}, bf16[80,2048]{1,0:T(8,128)(2,1)S(1)}, u32[]{:S(2)}, u32[]{:S(2)}) collective-permute-start(bf16[80,2048]{1,0:T(8,128)(2,1)S(1)} %get-tuple-element.184), channel_id=1, source_target_pairs={{0,16},{8,24},{16,0},{24,8},{1,17},{9,25},{17,1},{25,9},{2,18},{10... | collective-permute-start | bytes 983048 | tf_op jit(solution)/shard_map/ppermute | solution.py:27
  92.3 20.1 %collective-permute-start.21 = (bf16[512,512]{1,0:T(8,128)(2,1)S(1)}, bf16[512,512]{1,0:T(8,128)(2,1)S(1)}, u32[]{:S(2)}, u32[]{:S(2)}) collective-permute-start(bf16[512,512]{1,0:T(8,128)(2,1)S(1)} %add_convert_fusion.2), channel_id=1, source_target_pairs={{0,8},{8,0},{16,24},{24,16},{1,9},{9,1},{17,25},{25,17},{2,10},{10... | collective-permute-start | bytes 1572872 | tf_op jit(solution)/shard_map/ppermute | solution.py:27
  93.7 18.7 %collective-permute-start.20 = (bf16[512,512]{1,0:T(8,128)(2,1)S(1)}, bf16[512,512]{1,0:T(8,128)(2,1)S(1)}, u32[]{:S(2)}, u32[]{:S(2)}) collective-permute-start(bf16[512,512]{1,0:T(8,128)(2,1)S(1)} %convolution_convert_fusion.3), channel_id=1, source_target_pairs={{0,4},{4,0},{1,5},{5,1},{2,6},{6,2},{3,7},{7,3},{8,12},{12,8},{9,1... | collective-permute-start | bytes 1572872 | tf_op jit(solution)/shard_map/ppermute | solution.py:22
  95.4 17.0 %collective-permute-start.18 = (bf16[160,2048]{1,0:T(8,128)(2,1)S(1)}, bf16[160,2048]{1,0:T(8,128)(2,1)S(1)}, u32[]{:S(2)}, u32[]{:S(2)}) collective-permute-start(bf16[160,2048]{1,0:T(8,128)(2,1)S(1)} %constant_dynamic-update-slice_fusion), channel_id=1, source_target_pairs={{0,2},{1,3},{2,0},{3,1},{4,6},{5,7},{6,4},{7,5},{8,10},{9,11},{10,... | collective-permute-start | bytes 1966088 | tf_op jit(solution)/shard_map/ppermute | solution.py:27
  113.3 25.6 %collective-permute-start.25 = (bf16[512,512]{1,0:T(8,128)(2,1)S(1)}, bf16[512,512]{1,0:T(8,128)(2,1)S(1)}, u32[]{:S(2)}, u32[]{:S(2)}) collective-permute-start(bf16[512,512]{1,0:T(8,128)(2,1)S(1)} %add_convert_fusion.1), channel_id=1, source_target_pairs={{0,16},{8,24},{16,0},{24,8},{1,17},{9,25},{17,1},{25,9},{2,18},{10... | collective-permute-start | bytes 1572872 | tf_op jit(solution)/shard_map/ppermute | solution.py:27
  116.2 27.2 %collective-permute-start.23 = (bf16[160,2048]{1,0:T(8,128)(2,1)S(1)}, bf16[160,2048]{1,0:T(8,128)(2,1)S(1)}, u32[]{:S(2)}, u32[]{:S(2)}) collective-permute-start(bf16[160,2048]{1,0:T(8,128)(2,1)S(1)} %constant_dynamic-update-slice_fusion.2), channel_id=1, source_target_pairs={{0,2},{1,3},{2,0},{3,1},{4,6},{5,7},{6,4},{7,5},{8,10},{9,11},{10,... | collective-permute-start | bytes 1966088 | tf_op jit(solution)/shard_map/ppermute | solution.py:27
  116.8 26.6 %collective-permute-start.22 = (bf16[160,2048]{1,0:T(8,128)(2,1)S(1)}, bf16[160,2048]{1,0:T(8,128)(2,1)}, u32[]{:S(2)}, u32[]{:S(2)}) collective-permute-start(bf16[160,2048]{1,0:T(8,128)(2,1)S(1)} %constant_dynamic-update-slice_fusion), channel_id=1, source_target_pairs={{0,4},{4,0},{1,5},{5,1},{2,6},{6,2},{3,7},{7,3},{8,12},{12,8},{9,1... | collective-permute-start | bytes 1966088 | tf_op jit(solution)/shard_map/ppermute | solution.py:22
  118.2 25.2 %collective-permute-start.24 = (bf16[512,512]{1,0:T(8,128)(2,1)S(1)}, bf16[512,512]{1,0:T(8,128)(2,1)S(1)}, u32[]{:S(2)}, u32[]{:S(2)}) collective-permute-start(bf16[512,512]{1,0:T(8,128)(2,1)S(1)} %convolution_convert_fusion.1), channel_id=1, source_target_pairs={{0,4},{4,0},{1,5},{5,1},{2,6},{6,2},{3,7},{7,3},{8,12},{12,8},{9,1... | collective-permute-start | bytes 1572872 | tf_op jit(solution)/shard_map/ppermute | solution.py:22
  144.4 21.8 %collective-permute-start.26 = (bf16[240,2048]{1,0:T(8,128)(2,1)}, bf16[240,2048]{1,0:T(8,128)(2,1)}, u32[]{:S(2)}, u32[]{:S(2)}) collective-permute-start(bf16[240,2048]{1,0:T(8,128)(2,1)} %pad_maximum_fusion.8), channel_id=1, source_target_pairs={{0,4},{4,0},{1,5},{5,1},{2,6},{6,2},{3,7},{7,3},{8,12},{12,8},{9,1... | collective-permute-start | bytes 2949128 | tf_op jit(solution)/shard_map/ppermute | solution.py:22
  144.7 16.0 %collective-permute-start.27 = (bf16[160,2048]{1,0:T(8,128)(2,1)}, bf16[160,2048]{1,0:T(8,128)(2,1)}, u32[]{:S(2)}, u32[]{:S(2)}) collective-permute-start(bf16[160,2048]{1,0:T(8,128)(2,1)} %collective-permute-done.22), channel_id=1, source_target_pairs={{0,2},{1,3},{2,0},{3,1},{4,6},{5,7},{6,4},{7,5},{8,10},{9,11},{10,... | collective-permute-start | bytes 1966088 | tf_op jit(solution)/shard_map/ppermute | solution.py:27
  188.8 22.2 %collective-permute-start.35 = (bf16[1200,2048]{1,0:T(8,128)(2,1)S(1)}, bf16[1200,2048]{1,0:T(8,128)(2,1)S(1)}, u32[]{:S(2)}, u32[]{:S(2)}) collective-permute-start(bf16[1200,2048]{1,0:T(8,128)(2,1)S(1)} %slice_dynamic-update-slice_fusion.1), channel_id=1, source_target_pairs={{0,1},{1,0},{2,3},{3,2},{4,5},{5,4},{6,7},{7,6},{8,9},{9,8},{10,11... | collective-permute-start | bytes 14745608 | tf_op jit(solution)/shard_map/ppermute | solution.py:27
  189.5 18.2 %collective-permute-start.36 = (bf16[80,2048]{1,0:T(8,128)(2,1)S(1)}, bf16[80,2048]{1,0:T(8,128)(2,1)S(1)}, u32[]{:S(2)}, u32[]{:S(2)}) collective-permute-start(bf16[80,2048]{1,0:T(8,128)(2,1)S(1)} %get-tuple-element.322), channel_id=1, source_target_pairs={{0,8},{8,0},{16,24},{24,16},{1,9},{9,1},{17,25},{25,17},{2,10},{10... | collective-permute-start | bytes 983048 | tf_op jit(solution)/shard_map/ppermute | solution.py:27
  193.1 17.8 %collective-permute-start.37 = (bf16[80,2048]{1,0:T(8,128)(2,1)S(1)}, bf16[80,2048]{1,0:T(8,128)(2,1)S(1)}, u32[]{:S(2)}, u32[]{:S(2)}) collective-permute-start(bf16[80,2048]{1,0:T(8,128)(2,1)S(1)} %get-tuple-element.321), channel_id=1, source_target_pairs={{0,16},{8,24},{16,0},{24,8},{1,17},{9,25},{17,1},{25,9},{2,18},{10... | collective-permute-start | bytes 983048 | tf_op jit(solution)/shard_map/ppermute | solution.py:27
  193.6 17.4 %collective-permute-start.38 = (bf16[80,2048]{1,0:T(8,128)(2,1)S(1)}, bf16[80,2048]{1,0:T(8,128)(2,1)S(1)}, u32[]{:S(2)}, u32[]{:S(2)}) collective-permute-start(bf16[80,2048]{1,0:T(8,128)(2,1)S(1)} %get-tuple-element.272), channel_id=1, source_target_pairs={{0,4},{4,0},{1,5},{5,1},{2,6},{6,2},{3,7},{7,3},{8,12},{12,8},{9,1... | collective-permute-start | bytes 983048 | tf_op jit(solution)/shard_map/ppermute | solution.py:22
  211.0 21.1 %collective-permute-start.43 = (bf16[160,2048]{1,0:T(8,128)(2,1)S(1)}, bf16[160,2048]{1,0:T(8,128)(2,1)S(1)}, u32[]{:S(2)}, u32[]{:S(2)}) collective-permute-start(bf16[160,2048]{1,0:T(8,128)(2,1)S(1)} %constant_dynamic-update-slice_fusion.15), channel_id=1, source_target_pairs={{0,4},{4,0},{1,5},{5,1},{2,6},{6,2},{3,7},{7,3},{8,12},{12,8},{9,1... | collective-permute-start | bytes 1966088 | tf_op jit(solution)/shard_map/ppermute | solution.py:22
  212.8 19.3 %collective-permute-start.44 = (bf16[160,2048]{1,0:T(8,128)(2,1)S(1)}, bf16[160,2048]{1,0:T(8,128)(2,1)S(1)}, u32[]{:S(2)}, u32[]{:S(2)}) collective-permute-start(bf16[160,2048]{1,0:T(8,128)(2,1)S(1)} %constant_dynamic-update-slice_fusion.15), channel_id=1, source_target_pairs={{0,2},{1,3},{2,0},{3,1},{4,6},{5,7},{6,4},{7,5},{8,10},{9,11},{10,... | collective-permute-start | bytes 1966088 | tf_op jit(solution)/shard_map/ppermute | solution.py:27
  213.6 17.0 %collective-permute-start.41 = (bf16[40,2048]{1,0:T(8,128)(2,1)S(1)}, bf16[40,2048]{1,0:T(8,128)(2,1)S(1)}, u32[]{:S(2)}, u32[]{:S(2)}) collective-permute-start(bf16[40,2048]{1,0:T(8,128)(2,1)S(1)} %slice.130), channel_id=1, source_target_pairs={{0,4},{4,0},{1,5},{5,1},{2,6},{6,2},{3,7},{7,3},{8,12},{12,8},{9,1... | collective-permute-start | bytes 491528 | tf_op jit(solution)/shard_map/ppermute | solution.py:22
  214.0 18.1 %collective-permute-start.42 = (bf16[40,2048]{1,0:T(8,128)(2,1)S(1)}, bf16[40,2048]{1,0:T(8,128)(2,1)S(1)}, u32[]{:S(2)}, u32[]{:S(2)}) collective-permute-start(bf16[40,2048]{1,0:T(8,128)(2,1)S(1)} %slice.131), channel_id=1, source_target_pairs={{0,2},{1,3},{2,0},{3,1},{4,6},{5,7},{6,4},{7,5},{8,10},{9,11},{10,... | collective-permute-start | bytes 491528 | tf_op jit(solution)/shard_map/ppermute | solution.py:27
  215.4 16.7 %collective-permute-start.40 = (bf16[80,2048]{1,0:T(8,128)(2,1)S(1)}, bf16[80,2048]{1,0:T(8,128)(2,1)S(1)}, u32[]{:S(2)}, u32[]{:S(2)}) collective-permute-start(bf16[80,2048]{1,0:T(8,128)(2,1)S(1)} %get-tuple-element.271), channel_id=1, source_target_pairs={{0,24},{8,16},{16,8},{24,0},{1,25},{9,17},{17,9},{25,1},{2,26},{10... | collective-permute-start | bytes 983048 | tf_op jit(solution)/shard_map/ppermute | solution.py:27
  232.1 18.4 %collective-permute-start.48 = (bf16[80,2048]{1,0:T(8,128)(2,1)S(1)}, bf16[80,2048]{1,0:T(8,128)(2,1)S(1)}, u32[]{:S(2)}, u32[]{:S(2)}) collective-permute-start(bf16[80,2048]{1,0:T(8,128)(2,1)S(1)} %collective-permute-done.40), channel_id=1, source_target_pairs={{0,4},{4,0},{1,5},{5,1},{2,6},{6,2},{3,7},{7,3},{8,12},{12,8},{9,1... | collective-permute-start | bytes 983048 | tf_op jit(solution)/shard_map/ppermute | solution.py:22
  232.6 18.0 %collective-permute-start.49 = (bf16[80,2048]{1,0:T(8,128)(2,1)S(1)}, bf16[80,2048]{1,0:T(8,128)(2,1)S(1)}, u32[]{:S(2)}, u32[]{:S(2)}) collective-permute-start(bf16[80,2048]{1,0:T(8,128)(2,1)S(1)} %collective-permute-done.40), channel_id=1, source_target_pairs={{0,2},{1,3},{2,0},{3,1},{4,6},{5,7},{6,4},{7,5},{8,10},{9,11},{10,... | collective-permute-start | bytes 983048 | tf_op jit(solution)/shard_map/ppermute | solution.py:27
  233.3 17.1 %collective-permute-start.46 = (bf16[80,2048]{1,0:T(8,128)(2,1)S(1)}, bf16[80,2048]{1,0:T(8,128)(2,1)S(1)}, u32[]{:S(2)}, u32[]{:S(2)}) collective-permute-start(bf16[80,2048]{1,0:T(8,128)(2,1)S(1)} %slice.132), channel_id=1, source_target_pairs={{0,4},{4,0},{1,5},{5,1},{2,6},{6,2},{3,7},{7,3},{8,12},{12,8},{9,1... | collective-permute-start | bytes 983048 | tf_op jit(solution)/shard_map/ppermute | solution.py:22
  (37 other events, 365.8 us)
